TPU v7x, 32 devices: a whole 2x2x4 slice. The times are simulated.
32 devices in a mesh: seq: 8 (over y, x, core), mp: 4 (over z).
Axes of the slice: x: 2, y: 2, z: 4, core: 2. Of those that a mesh axis runs over, the one named last changes fastest.
Arguments:
- tokens: bfloat16 [1024, 2, 1536], P('seq'), may hold values from -6 to 6
- lengths: int32 [2], replicated, may hold values from 256 to 1024, as said below
- expert_ids: int32 [1024, 2, 6], P('seq'), may hold values from 0 to 15, all different within a row; in each aligned block of 256 rows (0 to 255, 256 to 511, ..., all dimensions but the last counted through in order) at most 192 rows name the same one
- norm_gains: float32 [2, 1536], replicated, may hold values from 0.5 to 1.5
- in_z: bfloat16 [1536, 3072], P(None, 'mp'), may hold values from -0.15625 to 0.15625
- in_x: bfloat16 [1536, 3072], P(None, 'mp'), may hold values from -0.15625 to 0.15625
- in_bc: bfloat16 [1536, 256], replicated, may hold values from -0.15625 to 0.15625
- in_dt: bfloat16 [1536, 48], P(None, 'mp'), may hold values from -0.15625 to 0.15625
- conv_x: float32 [5, 3072], P(None, 'mp'), may hold values from -3 to 3
- conv_bc: float32 [5, 256], replicated, may hold values from -3 to 3
- head_par: float32 [3, 48], P(None, 'mp'), may hold values from -7 to 1.5, as said below
- gn_gain: float32 [3072], P('mp'), may hold values from 0.5 to 1.5
- out_w: bfloat16 [3072, 1536], P('mp'), may hold values from -0.109375 to 0.109375
- router: bfloat16 [1536, 16], replicated, may hold values from -0.078125 to 0.078125
- shared_in: bfloat16 [2, 1536, 1024], P(None, None, 'mp'), may hold values from -0.15625 to 0.15625
- shared_down: bfloat16 [1024, 1536], P('mp'), may hold values from -0.1875 to 0.1875
- expert_in: bfloat16 [32, 2, 1536, 256], P(('seq', 'mp')), may hold values from -0.15625 to 0.15625
- expert_down: bfloat16 [32, 256, 1536], P(('seq', 'mp')), may hold values from -0.5 to 0.5
- d_out: bfloat16 [1024, 2, 1536], P('seq'), may hold values from -6 to 6
Outputs:
- output: float32 [1024, 2, 1536], P('seq')
- d_tokens: float32 [1024, 2, 1536], P('seq')
- g_norm_gains: float32 [2, 1536], replicated
- g_in_z: float32 [1536, 3072], P(None, 'mp')
- g_in_x: float32 [1536, 3072], P(None, 'mp')
- g_in_bc: float32 [1536, 256], replicated
- g_in_dt: float32 [1536, 48], P(None, 'mp')
- g_conv_x: float32 [5, 3072], P(None, 'mp')
- g_conv_bc: float32 [5, 256], replicated
- g_head_par: float32 [3, 48], P(None, 'mp')
- g_gn_gain: float32 [3072], P('mp')
- g_out_w: float32 [3072, 1536], P('mp')
- g_router: float32 [1536, 16], replicated
- g_shared_in: float32 [2, 1536, 1024], P(None, None, 'mp')
- g_shared_down: float32 [1024, 1536], P('mp')
- g_expert_in: float32 [32, 2, 1536, 256], P(('seq', 'mp'))
- g_expert_down: float32 [32, 256, 1536], P(('seq', 'mp'))
Inputs may be any that keep to these rules, and one draw needn't show every extreme that they name: `lengths`: one sequence, drawn from the seed, uses all 1024 positions; used positions come first. `expert_ids`: among the tokens of one index of seq (aligned blocks of 256 tokens), no expert is named more than 192 times, a bound that some block reaches. `head_par`: rows are step bias, log decay rate, skip weight.
All inputs are finite; a program needn't handle non-finite values.
Results may differ from a plain program's by a relative error of at most 0.035.
Values may be sent and summed in bfloat16 or wider, within the bound.
No kernel may reach another device: no remote copies, remote signals or barrier semaphores. Data moves between devices by JAX's collectives and lax.ppermute only.
A program may use at most 256 MiB of HBM per device.

v0:
```python
import jax
import jax.numpy as jnp
from jax import lax
from jax.sharding import PartitionSpec as P

HEAD_DIM = 64
STATE = 128
KCONV = 4
INNER = 3072


HIGHEST_PRECISION = lax.Precision.HIGHEST
EPSILON = 1e-05


def passed_along(block, axis, distance):
    devices = range(lax.axis_size(axis))
    route = [(i - distance, i) for i in devices if i - distance in devices]
    return lax.ppermute(block, axis, route)


def carried_in(array, axis, join, neutral):
    place = lax.axis_index(axis)
    gathered = jax.tree.map(
        lambda a, kind: lax.all_gather(a.astype(kind), axis), array, (jnp.bfloat16, jnp.bfloat16)
    )
    state = jax.tree.map(lambda a, e: jnp.zeros_like(a) + jnp.asarray(e, a.dtype), array, neutral)

    def one(turn, state):
        return join(
            state,
            jax.tree.map(
                lambda a, own: lax.dynamic_index_in_dim(a, turn, 0, False).astype(own.dtype),
                gathered,
                array,
            ),
        )

    return lax.fori_loop(0, place, one, state)


def entering_2(array, axis, combine, identity):
    size, index = (lax.axis_size(axis), lax.axis_index(axis))
    everything = jax.tree.map(
        lambda part, kind: lax.all_gather(part.astype(kind), axis),
        array,
        jax.tree.map(lambda a: jnp.bfloat16 if a.dtype == jnp.float32 else a.dtype, array),
    )
    start = jax.tree.map(
        lambda part, zero: jnp.broadcast_to(jnp.asarray(zero, part.dtype), part.shape),
        array,
        identity,
    )

    def turn(k, before):
        at = size - 1 - k
        reached = at > index
        new = combine(
            before, jax.tree.map(lambda part, own: part[at].astype(own.dtype), everything, array)
        )
        return jax.tree.map(lambda a, b: jnp.where(reached, a, b), new, before)

    return lax.fori_loop(0, size, turn, start)


def prepare(xbc_rows, edge_rows, dt_raw, conv_all, rates, live_mask, width_x):
    span_rows = xbc_rows.shape[0]
    padded = jnp.concatenate([edge_rows, xbc_rows], axis=0)
    summed = conv_all[KCONV]
    for tap_index in range(KCONV):
        summed = summed + conv_all[tap_index] * padded[tap_index : tap_index + span_rows]
    active = jax.nn.silu(summed)
    x_ssm = active[..., :width_x] * live_mask[..., None]
    b_mat = active[..., width_x : width_x + STATE]
    c_mat = active[..., width_x + STATE :]
    stepped = jax.nn.softplus(dt_raw + rates[0]) * live_mask[..., None]
    log_decay = -jnp.exp(rates[1]) * stepped
    return (
        x_ssm.reshape(span_rows, x_ssm.shape[1], -1, HEAD_DIM),
        b_mat,
        c_mat,
        log_decay,
        stepped,
    )


def ssd_core(x_ssm, b_mat, c_mat, log_decay, stepped, skip_gain):
    span_rows = x_ssm.shape[0]
    cumulative = jnp.cumsum(log_decay, axis=0)
    order_mask = (jnp.arange(span_rows)[:, None] >= jnp.arange(span_rows)[None, :])[
        :, :, None, None
    ]
    log_gaps = cumulative[:, None] - cumulative[None, :]
    decays = jnp.where(order_mask, jnp.exp(jnp.where(order_mask, log_gaps, 0.0)), 0.0)
    scores = jnp.einsum("tsn,usn->tus", c_mat, b_mat, precision=HIGHEST_PRECISION)
    weighted = x_ssm * stepped[..., None]
    outputs = jnp.einsum(
        "tush,ushp->tshp", decays * scores[..., None], weighted, precision=HIGHEST_PRECISION
    )
    outputs = outputs + skip_gain[:, None] * x_ssm
    remaining = jnp.exp(cumulative[-1][None] - cumulative)
    local_state = jnp.einsum(
        "ushp,usn->shpn", weighted * remaining[..., None], b_mat, precision=HIGHEST_PRECISION
    )
    return (outputs, local_state, jnp.exp(cumulative[-1]))


def state_term(c_mat, log_decay, entering):
    cumulative = jnp.cumsum(log_decay, axis=0)
    return (
        jnp.einsum("tsn,shpn->tshp", c_mat, entering, precision=HIGHEST_PRECISION)
        * jnp.exp(cumulative)[..., None]
    )


def route_table(flat_ids, experts, capacity):
    total_routes = flat_ids.shape[0]
    onehot = (flat_ids[:, None] == jnp.arange(experts, dtype=jnp.int32)[None, :]).astype(jnp.int32)
    slot_ranks = jnp.sum((jnp.cumsum(onehot, axis=0) - onehot) * onehot, axis=1)
    slot_table = jnp.full((experts * capacity,), total_routes, jnp.int32)
    slot_table = slot_table.at[flat_ids * capacity + slot_ranks].set(
        jnp.arange(total_routes, dtype=jnp.int32)
    )
    return (slot_table.reshape(experts, capacity), slot_ranks)


def silu_slope(value_in):
    sigmoid_v = jax.nn.sigmoid(value_in)
    return sigmoid_v * (1.0 + value_in * (1.0 - sigmoid_v))


def link_forward(earlier, later):
    return (earlier[0] * later[0], later[0][..., None, None] * earlier[1] + later[1])


def link_backward(earlier, later):
    return (later[0] * earlier[0], later[1] + later[0][..., None, None] * earlier[1])


def dispatch_layout(expert_ids, experts):
    block_rows = expert_ids.shape[0] * expert_ids.shape[1]
    topk_count = expert_ids.shape[2]
    capacity = (2 * block_rows * topk_count + experts - 1) // experts
    flat_ids = expert_ids.reshape(-1)
    slot_table, slot_ranks = route_table(flat_ids, experts, capacity)
    groups = lax.axis_size("mp") // 2
    own_group = lax.axis_index("mp") // 2
    mine_table = lax.dynamic_index_in_dim(
        slot_table.reshape(experts // groups, groups, capacity), own_group, axis=1, keepdims=False
    )
    total_routes = block_rows * topk_count
    live_slot = mine_table < total_routes
    safe_route = jnp.minimum(mine_table, total_routes - 1)
    own_route = (flat_ids % groups == own_group).astype(jnp.float32)
    positions = flat_ids // groups * capacity + slot_ranks
    return (live_slot, safe_route, own_route, positions)


def mixer_forward(
    tokens_f, norm_gains, in_z, in_x, in_bc, in_dt, conv_all, head_par, gn_gain, out_w, live_mask
):
    scale_one = lax.rsqrt(jnp.mean(tokens_f * tokens_f, axis=-1, keepdims=True) + EPSILON)
    normed = (tokens_f * scale_one * norm_gains[0]).astype(jnp.bfloat16)
    gate_z = jnp.dot(normed, in_z, preferred_element_type=jnp.float32)
    xbc_rows = jnp.concatenate(
        [
            jnp.dot(normed, in_x, preferred_element_type=jnp.float32),
            jnp.dot(normed, in_bc, preferred_element_type=jnp.float32),
        ],
        axis=-1,
    ).astype(jnp.bfloat16)
    dt_raw = jnp.dot(normed, in_dt, preferred_element_type=jnp.float32)
    edge_rows = passed_along(xbc_rows[xbc_rows.shape[0] - (KCONV - 1) :], "seq", 1)
    prepared = prepare(
        xbc_rows.astype(jnp.float32),
        edge_rows.astype(jnp.float32),
        dt_raw,
        conv_all,
        head_par[:2],
        live_mask,
        in_x.shape[1],
    )
    x_ssm, b_mat, c_mat, log_decay, stepped = prepared
    base_out, local_state, total_decay = ssd_core(
        x_ssm, b_mat, c_mat, log_decay, stepped, head_par[2]
    )
    identity = (jnp.ones_like(total_decay), jnp.zeros_like(local_state))
    _, entering = carried_in((total_decay, local_state), "seq", link_forward, identity)
    mixed_y = (base_out + state_term(c_mat, log_decay, entering)).reshape(gate_z.shape)
    gated_y = mixed_y * jax.nn.silu(gate_z)
    square_sum = lax.psum(jnp.sum(gated_y * gated_y, axis=-1), "mp")
    inner_scale = lax.rsqrt(square_sum / INNER + EPSILON)[..., None]
    normed_y = (gated_y * inner_scale * gn_gain).astype(jnp.bfloat16)
    mixer_out = lax.psum(
        jnp.dot(normed_y, out_w, preferred_element_type=jnp.float32).astype(jnp.bfloat16), "mp"
    ).astype(jnp.float32)
    return (
        scale_one,
        normed,
        gate_z,
        xbc_rows,
        dt_raw,
        edge_rows,
        entering,
        mixed_y,
        gated_y,
        inner_scale,
        normed_y,
        mixer_out,
        tokens_f + mixer_out,
    )


def expert_forward(
    residual, norm_gains, router, shared_in, shared_down, expert_in, expert_down, expert_ids
):
    model_width = residual.shape[-1]
    topk_count = expert_ids.shape[2]
    scale_two = lax.rsqrt(jnp.mean(residual * residual, axis=-1, keepdims=True) + EPSILON)
    normed_two = (residual * scale_two * norm_gains[1]).astype(jnp.bfloat16)
    experts = router.shape[1]
    logits = jnp.dot(normed_two, router, preferred_element_type=jnp.float32)
    pick_mask = (expert_ids[..., None] == jnp.arange(experts, dtype=jnp.int32)).astype(jnp.float32)
    gate_probs = jax.nn.softmax(jnp.sum(pick_mask * logits[..., None, :], axis=-1), axis=-1)
    shared_gate = jnp.dot(normed_two, shared_in[0], preferred_element_type=jnp.float32)
    shared_up = jnp.dot(normed_two, shared_in[1], preferred_element_type=jnp.float32)
    shared_hidden = (jax.nn.silu(shared_gate) * shared_up).astype(jnp.bfloat16)
    moe_part = jnp.dot(shared_hidden, shared_down, preferred_element_type=jnp.float32)
    layout = dispatch_layout(expert_ids, experts)
    live_slot, safe_route, own_route, positions = layout
    flat_rows = normed_two.reshape(-1, model_width)
    send_rows = jnp.where(live_slot[..., None], flat_rows[safe_route // topk_count], 0)
    received = lax.all_to_all(send_rows, "seq", split_axis=0, concat_axis=0, tiled=True)
    flat_in = received.reshape(-1, model_width)
    gate_e = jnp.dot(flat_in, expert_in[0, 0], preferred_element_type=jnp.float32)
    up_e = jnp.dot(flat_in, expert_in[0, 1], preferred_element_type=jnp.float32)
    hidden_e = (jax.nn.silu(gate_e) * up_e).astype(jnp.bfloat16)
    part_e = (
        jnp.dot(hidden_e, expert_down[0], preferred_element_type=jnp.float32)
        .astype(jnp.bfloat16)
        .reshape(received.shape)
    )
    returned = lax.all_to_all(part_e, "seq", split_axis=0, concat_axis=0, tiled=True)
    route_vals = returned.reshape(-1, model_width)[positions]
    gate_weight = (gate_probs.reshape(-1) * own_route).reshape(-1, topk_count)
    routed = jnp.sum(
        route_vals.astype(jnp.float32).reshape(-1, topk_count, model_width)
        * gate_weight[..., None],
        axis=1,
    )
    moe_part = moe_part + routed.reshape(residual.shape)
    return (
        scale_two,
        normed_two,
        pick_mask,
        gate_probs,
        shared_gate,
        shared_up,
        shared_hidden,
        layout,
        received,
        route_vals,
        moe_part,
    )


def body(
    tokens,
    lengths,
    expert_ids,
    norm_gains,
    in_z,
    in_x,
    in_bc,
    in_dt,
    conv_x,
    conv_bc,
    head_par,
    gn_gain,
    out_w,
    router,
    shared_in,
    shared_down,
    expert_in,
    expert_down,
    d_out,
):
    piece_rows = tokens.shape[0]
    model_width = tokens.shape[2]
    topk_count = expert_ids.shape[2]
    positions_here = lax.axis_index("seq") * piece_rows + jnp.arange(piece_rows, dtype=jnp.int32)
    live_mask = (positions_here[:, None] < lengths[None, :]).astype(jnp.float32)
    tokens_f = tokens.astype(jnp.float32)
    conv_all = jnp.concatenate([conv_x, conv_bc], axis=-1)
    mixer_saved = mixer_forward(
        tokens_f,
        norm_gains,
        in_z,
        in_x,
        in_bc,
        in_dt,
        conv_all,
        head_par,
        gn_gain,
        out_w,
        live_mask,
    )
    expert_saved = expert_forward(
        mixer_saved[12],
        norm_gains,
        router,
        shared_in,
        shared_down,
        expert_in,
        expert_down,
        expert_ids,
    )
    output = mixer_saved[12] + lax.psum(expert_saved[10].astype(jnp.bfloat16), "mp").astype(
        jnp.float32
    )
    mixer_saved = mixer_forward(
        tokens_f,
        norm_gains,
        in_z,
        in_x,
        in_bc,
        in_dt,
        conv_all,
        head_par,
        gn_gain,
        out_w,
        live_mask,
    )
    expert_saved = expert_forward(
        mixer_saved[12],
        norm_gains,
        router,
        shared_in,
        shared_down,
        expert_in,
        expert_down,
        expert_ids,
    )
    (
        scale_one,
        normed,
        gate_z,
        xbc_rows,
        dt_raw,
        edge_rows,
        entering,
        mixed_y,
        gated_y,
        inner_scale,
        normed_y,
        mixer_out,
        residual,
    ) = mixer_saved
    (
        scale_two,
        normed_two,
        pick_mask,
        gate_probs,
        shared_gate,
        shared_up,
        shared_hidden,
        layout,
        received,
        route_vals,
        _,
    ) = expert_saved
    live_slot, safe_route, own_route, positions = layout
    grad_out = d_out.astype(jnp.float32)
    flat_grad = grad_out.reshape(-1, model_width)
    grad_shared = jnp.einsum("psd,fd->psf", d_out, shared_down, preferred_element_type=jnp.float32)
    grad_sgate = (grad_shared * shared_up * silu_slope(shared_gate)).astype(jnp.bfloat16)
    grad_sup = (grad_shared * jax.nn.silu(shared_gate)).astype(jnp.bfloat16)
    g_shared_down = jnp.einsum(
        "psf,psd->fd", shared_hidden, d_out, preferred_element_type=jnp.float32
    )
    g_shared_in = jnp.stack(
        [
            jnp.einsum("psd,psf->df", normed_two, grad_sgate, preferred_element_type=jnp.float32),
            jnp.einsum("psd,psf->df", normed_two, grad_sup, preferred_element_type=jnp.float32),
        ]
    )
    grad_normed_two = jnp.einsum(
        "psf,df->psd", grad_sgate, shared_in[0], preferred_element_type=jnp.float32
    ) + jnp.einsum("psf,df->psd", grad_sup, shared_in[1], preferred_element_type=jnp.float32)
    grad_gate = jnp.einsum(
        "rkd,rd->rk",
        route_vals.reshape(-1, topk_count, model_width),
        d_out.reshape(-1, model_width),
        preferred_element_type=jnp.float32,
    ) * own_route.reshape(-1, topk_count)
    flat_gates = gate_probs.reshape(-1)
    grad_send = jnp.where(
        live_slot[..., None],
        flat_grad[safe_route // topk_count] * flat_gates[safe_route][..., None],
        0.0,
    ).astype(jnp.bfloat16)
    grad_received = lax.all_to_all(grad_send, "seq", split_axis=0, concat_axis=0, tiled=True)
    flat_in = received.reshape(-1, model_width)
    gate_e = jnp.dot(flat_in, expert_in[0, 0], preferred_element_type=jnp.float32)
    up_e = jnp.dot(flat_in, expert_in[0, 1], preferred_element_type=jnp.float32)
    hidden_e = (jax.nn.silu(gate_e) * up_e).astype(jnp.bfloat16)
    flat_dy = grad_received.reshape(-1, model_width)
    g_expert_down = jnp.einsum("rf,rd->fd", hidden_e, flat_dy, preferred_element_type=jnp.float32)[
        None
    ]
    grad_hidden_e = jnp.einsum(
        "rd,fd->rf", flat_dy, expert_down[0], preferred_element_type=jnp.float32
    )
    grad_gate_e = (grad_hidden_e * up_e * silu_slope(gate_e)).astype(jnp.bfloat16)
    grad_up_e = (grad_hidden_e * jax.nn.silu(gate_e)).astype(jnp.bfloat16)
    g_expert_in = jnp.stack(
        [
            jnp.einsum("rd,rf->df", flat_in, grad_gate_e, preferred_element_type=jnp.float32),
            jnp.einsum("rd,rf->df", flat_in, grad_up_e, preferred_element_type=jnp.float32),
        ]
    )[None]
    grad_rows = (
        jnp.einsum("rf,df->rd", grad_gate_e, expert_in[0, 0], preferred_element_type=jnp.float32)
        + jnp.einsum("rf,df->rd", grad_up_e, expert_in[0, 1], preferred_element_type=jnp.float32)
    ).astype(jnp.bfloat16)
    grad_returned = lax.all_to_all(
        grad_rows.reshape(received.shape), "seq", split_axis=0, concat_axis=0, tiled=True
    )
    grad_routes = (
        grad_returned.reshape(-1, model_width)[positions].astype(jnp.float32) * own_route[:, None]
    )
    grad_normed_two = grad_normed_two + jnp.sum(
        grad_routes.reshape(-1, topk_count, model_width), axis=1
    ).reshape(normed_two.shape)
    summed_two, summed_gate = (
        lax.psum(grad_normed_two.astype(jnp.bfloat16), "mp").astype(jnp.float32),
        lax.psum(grad_gate.reshape(gate_probs.shape).astype(jnp.bfloat16), "mp").astype(
            jnp.float32
        ),
    )
    grad_chosen = gate_probs * (
        summed_gate - jnp.sum(gate_probs * summed_gate, axis=-1, keepdims=True)
    )
    grad_logits = jnp.sum(pick_mask * grad_chosen[..., None], axis=-2).astype(jnp.bfloat16)
    grad_normed_two = summed_two + jnp.einsum(
        "pse,de->psd", grad_logits, router, preferred_element_type=jnp.float32
    )
    g_router = jnp.einsum(
        "psd,pse->de", normed_two, grad_logits, preferred_element_type=jnp.float32
    )
    scaled_two = residual * scale_two
    gain_grad_two = grad_normed_two * norm_gains[1]
    grad_residual = grad_out + scale_two * (
        gain_grad_two - scaled_two * jnp.mean(gain_grad_two * scaled_two, axis=-1, keepdims=True)
    )
    g_gain_two = jnp.sum(grad_normed_two * scaled_two, axis=(0, 1))
    grad_mix = grad_residual.astype(jnp.bfloat16)
    g_out_w = jnp.einsum("psi,psd->id", normed_y, grad_mix, preferred_element_type=jnp.float32)
    grad_norm_y = jnp.einsum("psd,id->psi", grad_mix, out_w, preferred_element_type=jnp.float32)
    statistic = jnp.sum(grad_mix.astype(jnp.float32) * mixer_out, axis=-1, keepdims=True)
    g_gn_gain = jnp.sum(grad_norm_y * gated_y * inner_scale, axis=(0, 1))
    grad_gated = (
        inner_scale * gn_gain * grad_norm_y
        - gated_y * inner_scale * inner_scale * statistic / INNER
    )
    grad_y = grad_gated * jax.nn.silu(gate_z)
    grad_z = (grad_gated * mixed_y * silu_slope(gate_z)).astype(jnp.bfloat16)

    def prep_fn(xbc_f, edge_f, dt_in, conv_in, rates_in):
        return prepare(xbc_f, edge_f, dt_in, conv_in, rates_in, live_mask, in_x.shape[1])

    prepared, prep_pull = jax.vjp(
        prep_fn,
        xbc_rows.astype(jnp.float32),
        edge_rows.astype(jnp.float32),
        dt_raw,
        conv_all,
        head_par[:2],
    )
    x_ssm, b_mat, c_mat, log_decay, stepped = prepared
    core_out, core_pull = jax.vjp(ssd_core, x_ssm, b_mat, c_mat, log_decay, stepped, head_par[2])
    total_decay = core_out[2]
    grad_y4 = grad_y.reshape(x_ssm.shape)
    _, state_pull = jax.vjp(state_term, c_mat, log_decay, entering)
    grad_c_one, grad_decay_one, grad_entering = state_pull(grad_y4)
    identity = (jnp.ones_like(total_decay), jnp.zeros_like(grad_entering))
    _, grad_leaving = entering_2((total_decay, grad_entering), "seq", link_backward, identity)
    grad_total = jnp.sum(grad_leaving * entering, axis=(-2, -1))
    grad_x, grad_b, grad_c_two, grad_decay_two, grad_step, grad_skip = core_pull(
        (grad_y4, grad_leaving, grad_total)
    )
    grad_xbc, grad_edge, grad_dt, grad_conv, grad_rates = prep_pull(
        (grad_x, grad_b, grad_c_one + grad_c_two, grad_decay_one + grad_decay_two, grad_step)
    )
    from_next = passed_along(grad_edge, "seq", -1)
    border = piece_rows - (KCONV - 1)
    grad_xbc = jnp.concatenate([grad_xbc[:border], grad_xbc[border:] + from_next], axis=0)
    width_x = in_x.shape[1]
    grad_xpart = grad_xbc[..., :width_x].astype(jnp.bfloat16)
    grad_dt_low = grad_dt.astype(jnp.bfloat16)
    partial_normed = (
        jnp.einsum("psi,di->psd", grad_z, in_z, preferred_element_type=jnp.float32)
        + jnp.einsum("psi,di->psd", grad_xpart, in_x, preferred_element_type=jnp.float32)
        + jnp.einsum("psh,dh->psd", grad_dt_low, in_dt, preferred_element_type=jnp.float32)
    )
    summed_one, summed_bc, summed_conv_bc = (
        lax.psum(partial_normed.astype(jnp.bfloat16), "mp").astype(jnp.float32),
        lax.psum(grad_xbc[..., width_x:].astype(jnp.bfloat16), "mp").astype(jnp.float32),
        lax.psum(grad_conv[:, width_x:].astype(jnp.bfloat16), "mp").astype(jnp.float32),
    )
    grad_bc_low = summed_bc.astype(jnp.bfloat16)
    grad_normed = summed_one + jnp.einsum(
        "psc,dc->psd", grad_bc_low, in_bc, preferred_element_type=jnp.float32
    )
    g_in_z = jnp.einsum("psd,psi->di", normed, grad_z, preferred_element_type=jnp.float32)
    g_in_x = jnp.einsum("psd,psi->di", normed, grad_xpart, preferred_element_type=jnp.float32)
    g_in_bc = jnp.einsum("psd,psc->dc", normed, grad_bc_low, preferred_element_type=jnp.float32)
    g_in_dt = jnp.einsum("psd,psh->dh", normed, grad_dt_low, preferred_element_type=jnp.float32)
    scaled_one = tokens_f * scale_one
    gain_grad_one = grad_normed * norm_gains[0]
    d_tokens = grad_residual + scale_one * (
        gain_grad_one - scaled_one * jnp.mean(gain_grad_one * scaled_one, axis=-1, keepdims=True)
    )
    g_gain_one = jnp.sum(grad_normed * scaled_one, axis=(0, 1))
    g_head_par = jnp.concatenate([grad_rates, grad_skip[None]], axis=0)
    seq_sums = (
        lax.psum(jnp.stack([g_gain_one, g_gain_two]).astype(jnp.bfloat16), "seq").astype(
            jnp.float32
        ),
        lax.psum(g_in_z.astype(jnp.bfloat16), "seq").astype(jnp.float32),
        lax.psum(g_in_x.astype(jnp.bfloat16), "seq").astype(jnp.float32),
        lax.psum(g_in_bc.astype(jnp.bfloat16), "seq").astype(jnp.float32),
        lax.psum(g_in_dt.astype(jnp.bfloat16), "seq").astype(jnp.float32),
        lax.psum(grad_conv[:, :width_x].astype(jnp.bfloat16), "seq").astype(jnp.float32),
        lax.psum(summed_conv_bc.astype(jnp.bfloat16), "seq").astype(jnp.float32),
        lax.psum(g_head_par.astype(jnp.bfloat16), "seq").astype(jnp.float32),
        lax.psum(g_gn_gain.astype(jnp.bfloat16), "seq").astype(jnp.float32),
        lax.psum(g_out_w.astype(jnp.bfloat16), "seq").astype(jnp.float32),
        lax.psum(g_router.astype(jnp.bfloat16), "seq").astype(jnp.float32),
        lax.psum(g_shared_in.astype(jnp.bfloat16), "seq").astype(jnp.float32),
        lax.psum(g_shared_down.astype(jnp.bfloat16), "seq").astype(jnp.float32),
    )
    return (
        output,
        d_tokens,
        seq_sums[0],
        seq_sums[1],
        seq_sums[2],
        seq_sums[3],
        seq_sums[4],
        seq_sums[5],
        seq_sums[6],
        seq_sums[7],
        seq_sums[8],
        seq_sums[9],
        seq_sums[10],
        seq_sums[11],
        seq_sums[12],
        g_expert_in,
        g_expert_down,
    )


def solution(mesh):
    in_specs = (
        P("seq", None, None),
        P(),
        P("seq", None, None),
        P(),
        P(None, "mp"),
        P(None, "mp"),
        P(),
        P(None, "mp"),
        P(None, "mp"),
        P(),
        P(None, "mp"),
        P("mp"),
        P("mp", None),
        P(),
        P(None, None, "mp"),
        P("mp", None),
        P(("seq", "mp"), None, None, None),
        P(("seq", "mp"), None, None),
        P("seq", None, None),
    )
    out_specs = (
        P("seq", None, None),
        P("seq", None, None),
        P(),
        P(None, "mp"),
        P(None, "mp"),
        P(),
        P(None, "mp"),
        P(None, "mp"),
        P(),
        P(None, "mp"),
        P("mp"),
        P("mp", None),
        P(),
        P(None, None, "mp"),
        P("mp", None),
        P(("seq", "mp"), None, None, None),
        P(("seq", "mp"), None, None),
    )
    return jax.shard_map(body, mesh=mesh, in_specs=in_specs, out_specs=out_specs, check_vma=False)
```

profile of v0, /device:TPU:0, one launch (start us, length us, event | category | flops | bytes accessed | tf_op | source)
XLA Modules:
  0.0 907.6 jit_solution(12110160160960930135)
XLA Ops:
  41.8 9.4 %all_gather.10 = bf16[8,2,12]{2,1,0:T(2,128)(2,1)S(1)} all-gather(bf16[1,2,12]{2,1,0:T(2,128)(2,1)} %get-tuple-element.439), channel_id=1, replica_groups=mesh['seq'=8,'mp'=4] {'seq'}, dimensions={0}, use_global_device_ids=true | all-gather | bytes 432 | tf_op jit(solution)/shard_map/all_gather | solution.py:25
  53.9 14.0 %all-gather.5.cloned.1.call-done = bf16[16,12,64,128]{3,2,1,0:T(8,128)(2,1)} async-done(((bf16[2,12,64,128]{3,2,1,0:T(8,128)(2,1)}), bf16[16,12,64,128]{3,2,1,0:T(8,128)(2,1)}) %all-gather.5.cloned.1.call-update) | async-done | bytes 3145744 | tf_op jit(solution)/shard_map/all_gather | solution.py:25
  80.6 11.9 %psum.153 = f32[128,2]{0,1:T(2,128)S(1)} all-reduce(f32[128,2]{0,1:T(2,128)S(1)} %get-tuple-element.414), channel_id=1, replica_groups=mesh['seq'=8,'mp'=4] {'mp'}, use_global_device_ids=true, to_apply=%region_5.6 | all-reduce | flops 256 | bytes 2048 | tf_op jit(solution)/shard_map/psum | solution.py:191
  103.4 41.1 %all-reduce.25.cloned.1.call-done = bf16[128,2,1536]{2,0,1:T(8,128)(2,1)} async-done(((bf16[128,2,1536]{2,0,1:T(8,128)(2,1)}), bf16[128,2,1536]{2,0,1:T(8,128)(2,1)}) %all-reduce.25.cloned.1.call-update) | async-done | bytes 786448 | tf_op jit(solution)/shard_map/psum | solution.py:194
  172.9 11.9 %gather_fusion.2 = f32[1536,1536]{1,0:T(8,128)} fusion(f32[256,1536]{1,0:T(8,128)} %reshape.600, s32[2048]{0:T(1024)S(1)} %pad_clamp_fusion.2), kind=kCustom, calls=%fused_computation.2 | custom fusion | bytes 18880512 | tf_op jit(solution)/shard_map/gather | solution.py:399
  186.2 8.4 gather_fusion.3
  200.3 21.5 %all-to-all-done = bf16[8,192,1536]{2,1,0:T(8,128)(2,1)} async-done(((bf16[8,192,1536]{2,1,0:T(8,128)(2,1)}), bf16[8,192,1536]{2,1,0:T(8,128)(2,1)}, u32[]{:S(2)}, u32[]{:S(2)}) %all-to-all-start) | async-done | bytes 4718624 | tf_op jit(solution)/shard_map/all_to_all | solution.py:233
  236.7 44.7 %all-to-all-done.2 = bf16[8,192,1536]{2,1,0:T(8,128)(2,1)} async-done(((bf16[8,192,1536]{2,1,0:T(8,128)(2,1)}), bf16[8,192,1536]{2,1,0:T(8,128)(2,1)}, u32[]{:S(2)}, u32[]{:S(2)}) %all-to-all-start.2) | async-done | bytes 4718624 | tf_op jit(solution)/shard_map/all_to_all | solution.py:402
  302.7 48.1 %all-to-all-done.1 = bf16[8,192,1536]{2,1,0:T(8,128)(2,1)} async-done(((bf16[8,192,1536]{2,1,0:T(8,128)(2,1)}), bf16[8,192,1536]{2,1,0:T(8,128)(2,1)}, u32[]{:S(2)}, u32[]{:S(2)}) %all-to-all-start.1) | async-done | bytes 4718624 | tf_op jit(solution)/shard_map/all_to_all | solution.py:243
  366.6 13.3 %gather_fusion.1 = bf16[1536,1536]{1,0:T(8,128)(2,1)} fusion(bf16[1536,1536]{1,0:T(8,128)(2,1)} %bitcast.39, s32[2048]{0:T(1024)S(1)} %pad_clamp_fusion.1), kind=kCustom, calls=%fused_computation.1 | custom fusion | bytes 9443328 | tf_op jit(solution)/shard_map/gather | solution.py:244
  380.0 8.3 gather.21
  388.3 6.6 fusion.229
  396.2 14.0 %all-to-all-done.3 = bf16[8,192,1536]{2,1,0:T(8,128)(2,1)} async-done(((bf16[8,192,1536]{2,1,0:T(8,128)(2,1)}), bf16[8,192,1536]{2,1,0:T(8,128)(2,1)}, u32[]{:S(2)}, u32[]{:S(2)}) %all-to-all-start.3) | async-done | bytes 4718624 | tf_op jit(solution)/shard_map/all_to_all | solution.py:426
  410.2 13.3 %gather_fusion.4 = bf16[1536,1536]{1,0:T(8,128)(2,1)} fusion(bf16[1536,1536]{1,0:T(8,128)(2,1)} %bitcast.46, s32[2048]{0:T(1024)S(1)} %pad_clamp_fusion.1), kind=kCustom, calls=%fused_computation.4 | custom fusion | bytes 9443328 | tf_op jit(solution)/shard_map/gather | solution.py:430
  423.5 9.1 %reshape.613 = f32[256,6,1536]{2,1,0:T(8,128)} reshape(bf16[1536,1536]{1,0:T(8,128)(2,1)} %gather_fusion.4) | data formatting | bytes 14155776 | tf_op jit(solution)/shard_map/convert_element_type | solution.py:430
  432.6 10.6 %multiply_reduce_fusion = f32[256,1536]{1,0:T(8,128)} fusion(f32[256,6,1536]{2,1,0:T(8,128)} %reshape.613, f32[256,6]{1,0:T(8,128)S(1)} %convert_element_type.316), kind=kLoop, calls=%fused_computation.11 | loop fusion | flops 4325376 | bytes 11016192 | tf_op jit(solution)/shard_map/reduce_sum | solution.py:432
  450.9 10.3 %psum.157 = bf16[128,2,6]{0,2,1:T(8,128)(2,1)S(1)} all-reduce(bf16[128,2,6]{0,2,1:T(8,128)(2,1)S(1)} %copy.296), channel_id=1, replica_groups=mesh['seq'=8,'mp'=4] {'mp'}, use_global_device_ids=true, to_apply=%region_19.20 | all-reduce | flops 1536 | bytes 6144 | tf_op jit(solution)/shard_map/psum | solution.py:437
  462.7 28.6 %all-reduce.27.cloned.1.call-done = bf16[128,2,1536]{2,0,1:T(8,128)(2,1)} async-done(((bf16[128,2,1536]{2,0,1:T(8,128)(2,1)}), bf16[128,2,1536]{2,0,1:T(8,128)(2,1)}) %all-reduce.27.cloned.1.call-update) | async-done | bytes 786448 | tf_op jit(solution)/shard_map/psum | solution.py:436
  513.6 8.9 multiply_reduce_fusion.1
  543.1 23.2 %while.34 = (s32[]{:T(128)}, f32[2,12,64,128]{3,2,1,0:T(8,128)}, s32[]{:T(128)}, bf16[8,2,12,64,128]{4,3,2,1,0:T(8,128)(2,1)}, bf16[8,2,12]{2,1,0:T(2,128)(2,1)}...) while((s32[]{:T(128)}, f32[2,12,64,128]{3,2,1,0:T(8,128)}, s32[]{:T(128)}, ...), condition=%wide.region_26.27_spmd.clone, body=%wide.region_25.26_spmd.clone.sunk | while | flops 983072 | bytes 1966495 | solution.py:63
  605.0 11.3 %psum.166 = bf16[5,256]{1,0:T(8,128)(2,1)} all-reduce(bf16[5,256]{1,0:T(8,128)(2,1)S(1)} %add_convert_fusion.1), channel_id=1, replica_groups=mesh['seq'=8,'mp'=4] {'mp'}, use_global_device_ids=true, to_apply=%region_52.53 | all-reduce | flops 1280 | bytes 5120 | tf_op jit(solution)/shard_map/psum | solution.py:509
  621.0 51.0 %all-reduce.33.cloned.1.call-done = (bf16[128,2,1536]{2,0,1:T(8,128)(2,1)}, bf16[128,2,256]{2,0,1:T(8,128)(2,1)}, bf16[128,2,1536]{2,0,1:T(8,128)(2,1)}) async-done(((bf16[128,2,1536]{2,0,1:T(8,128)(2,1)}, bf16[128,2,256]{2,0,1:T(8,128)(2,1)}, bf16[128,2,1536]{2,0,1:T(8,128)(2,1)}), (bf16[128,2,1536]{2,0,1:T(8,128)(2,1)}, bf16[128,2,256]{2,0,1:T(8,128)(2,1)}, ...) | async-done | bytes 1703952 | tf_op jit(solution)/shard_map/psum | solution.py:318
  698.1 32.5 %all-reduce.29.cloned.1.call-done = (bf16[2,1536]{1,0:T(2,128)(2,1)}, bf16[1536,12]{0,1:T(8,128)(2,1)}, bf16[5,768]{1,0:T(8,128)(2,1)}, bf16[5,256]{1,0:T(8,128)...) async-done(((bf16[2,1536]{1,0:T(2,128)(2,1)}, bf16[1536,12]{0,1:T(8,128)(2,1)}, bf16[5,768]{1,0:T(8,128)(2,1)}, ...) | async-done | bytes 104024 | tf_op jit(solution)/shard_map/psum | solution.py:527
  740.0 145.2 %all-reduce.31.cloned.1.call-done = (bf16[1536,768]{1,0:T(8,128)(2,1)}, bf16[1536,768]{1,0:T(8,128)(2,1)}, bf16[1536,256]{1,0:T(8,128)(2,1)}, bf16[768,1536]{1,0...) async-done(((bf16[1536,768]{1,0:T(8,128)(2,1)}, bf16[1536,768]{1,0:T(8,128)(2,1)}, bf16[1536,256]{1,0:T(8,128)(2,1)}, bf16[768,1536]{1,0:T(8,128)(2,1)}, ...) | async-done | bytes 10223632 | tf_op jit(solution)/shard_map/psum | solution.py:530
  (542 shorter events, 317.1 us)
Async XLA Ops:
  7.2 85.9 %copy-start = (bf16[768,1536]{1,0:T(8,128)(2,1)S(1)}, bf16[768,1536]{1,0:T(8,128)(2,1)}, u32[]{:S(2)}) copy-start(bf16[768,1536]{1,0:T(8,128)(2,1)} %param.35) | copy-start | bytes 7077892
  7.2 60.7 %all-gather.5.cloned.1.call-start = ((), (), s32[]{:S(2)}) async-start(), calls=%async_computation.6 | async-start | bytes 3538944 | tf_op jit(solution)/shard_map/all_gather | solution.py:25
  14.4 9.9 %collective-permute-start = (bf16[3,2,1024]{2,0,1:T(4,128)(2,1)}, bf16[3,2,1024]{2,0,1:T(4,128)(2,1)}, u32[]{:S(2)}, u32[]{:S(2)}) collective-permute-start(bf16[3,2,1024]{2,0,1:T(4,128)(2,1)} %fusion.181), channel_id=1, source_target_pairs={{0,4},{4,8},{8,12},{12,16},{16,20},{20,24},{24,28},{1,5},{5,9},{9,... | collective-permute-start | bytes 36872 | tf_op jit(solution)/shard_map/ppermute | solution.py:19
  30.7 22.4 %copy-start.21 = (f32[128,2,768]{0,2,1:T(8,128)}, f32[128,2,768]{0,2,1:T(8,128)S(1)}, u32[]{:S(2)}) copy-start(f32[128,2,768]{0,2,1:T(8,128)S(1)} %copy.273) | copy-start | bytes 2359300
  33.4 111.1 %all-reduce.25.cloned.1.call-start = ((), (), s32[]{:S(2)}) async-start(), calls=%async_computation.4 | async-start | bytes 1572864 | tf_op jit(solution)/shard_map/psum | solution.py:194
  76.8 16.4 %copy-start.93 = (f32[768]{0:T(1024)S(1)}, f32[768]{0:T(1024)}, u32[]{:S(2)}) copy-start(f32[768]{0:T(1024)} %param.34) | copy-start | bytes 9220
  96.0 50.1 %copy-start.81 = (f32[1536]{0:T(1024)S(1)}, f32[1536]{0:T(1024)}, u32[]{:S(2)}) copy-start(f32[1536]{0:T(1024)} %get-tuple-element.367) | copy-start | bytes 18436
  162.3 59.5 %all-to-all-start = ((bf16[8,192,1536]{2,1,0:T(8,128)(2,1)}), bf16[8,192,1536]{2,1,0:T(8,128)(2,1)}, u32[]{:S(2)}, u32[]{:S(2)}) async-start(bf16[8,192,1536]{2,1,0:T(8,128)(2,1)} %broadcast_select_fusion), calls=%async_computation | async-start | bytes 9437184 | tf_op jit(solution)/shard_map/all_to_all | solution.py:233
  167.1 18.0 %copy-start.84 = (s32[128,2,6]{0,2,1:T(8,128)}, s32[128,2,6]{0,2,1:T(8,128)S(1)}, u32[]{:S(2)}) copy-start(s32[128,2,6]{0,2,1:T(8,128)S(1)} %copy.286) | copy-start | bytes 18436
  221.8 59.6 %all-to-all-start.2 = ((bf16[8,192,1536]{2,1,0:T(8,128)(2,1)}), bf16[8,192,1536]{2,1,0:T(8,128)(2,1)}, u32[]{:S(2)}, u32[]{:S(2)}) async-start(bf16[8,192,1536]{2,1,0:T(8,128)(2,1)} %select_convert_fusion), calls=%async_computation.2 | async-start | bytes 9437184 | tf_op jit(solution)/shard_map/all_to_all | solution.py:402
  291.5 59.4 %all-to-all-start.1 = ((bf16[8,192,1536]{2,1,0:T(8,128)(2,1)}), bf16[8,192,1536]{2,1,0:T(8,128)(2,1)}, u32[]{:S(2)}, u32[]{:S(2)}) async-start(bf16[8,192,1536]{2,1,0:T(8,128)(2,1)} %bitcast.342), calls=%async_computation.1 | async-start | bytes 9437184 | tf_op jit(solution)/shard_map/all_to_all | solution.py:243
  350.9 59.4 %all-to-all-start.3 = ((bf16[8,192,1536]{2,1,0:T(8,128)(2,1)}), bf16[8,192,1536]{2,1,0:T(8,128)(2,1)}, u32[]{:S(2)}, u32[]{:S(2)}) async-start(bf16[8,192,1536]{2,1,0:T(8,128)(2,1)} %bitcast.344), calls=%async_computation.3 | async-start | bytes 9437184 | tf_op jit(solution)/shard_map/all_to_all | solution.py:426
  355.5 135.9 %all-reduce.27.cloned.1.call-start = ((), (), s32[]{:S(2)}) async-start(), calls=%async_computation.5 | async-start | bytes 1572864 | tf_op jit(solution)/shard_map/psum | solution.py:436
  446.4 45.0 %copy-start.82 = (f32[1536]{0:T(1024)S(1)}, f32[1536]{0:T(1024)}, u32[]{:S(2)}) copy-start(f32[1536]{0:T(1024)} %get-tuple-element.367) | copy-start | bytes 18436
  449.9 93.2 %all-gather.7.cloned.1.call-start = ((), (), s32[]{:S(2)}) async-start(), calls=%async_computation.7 | async-start | bytes 3538944 | tf_op jit(solution)/shard_map/all_gather | solution.py:45
  462.7 31.8 %copy-start.107 = (bf16[128,2,16]{0,2,1:T(8,128)(2,1)}, bf16[128,2,16]{0,2,1:T(8,128)(2,1)S(1)}, u32[]{:S(2)}) copy-start(bf16[128,2,16]{0,2,1:T(8,128)(2,1)S(1)} %select_reduce_fusion) | copy-start | bytes 24580
  462.7 31.8 %copy-start.124 = (f32[128,2]{0,1:T(2,128)S(1)}, f32[128,2]{0,1:T(2,128)}, u32[]{:S(2)}) copy-start(f32[128,2]{0,1:T(2,128)} %copy-done.123) | copy-start | bytes 3076
  505.1 166.9 %all-reduce.33.cloned.1.call-start = ((), (), s32[]{:S(2)}) async-start(), calls=%async_computation.10 | async-start | bytes 3407872 | tf_op jit(solution)/shard_map/psum | solution.py:318
  588.9 3.1 collective-permute-start.1
  596.4 134.3 %all-reduce.29.cloned.1.call-start = ((), (), s32[]{:S(2)}) async-start(), calls=%async_computation.8 | async-start | bytes 247808 | tf_op jit(solution)/shard_map/psum | solution.py:527
  600.6 16.4 %copy-start.150 = (f32[12]{0:T(128)S(1)}, f32[12]{0:T(128)}, u32[]{:S(2)}) copy-start(f32[12]{0:T(128)} %get-tuple-element.405) | copy-start | bytes 148
  600.7 17.0 %copy-start.106 = (bf16[128,2,12]{0,2,1:T(8,128)(2,1)S(1)}, bf16[128,2,12]{0,2,1:T(8,128)(2,1)}, u32[]{:S(2)}) copy-start(bf16[128,2,12]{0,2,1:T(8,128)(2,1)} %copy-done.105) | copy-start | bytes 18436
  600.7 17.0 %copy-start.146 = (f32[128,2]{0,1:T(2,128)S(1)}, f32[128,2]{0,1:T(2,128)}, u32[]{:S(2)}) copy-start(f32[128,2]{0,1:T(2,128)} %copy-done.144) | copy-start | bytes 3076
  675.9 209.3 %all-reduce.31.cloned.1.call-start = ((), (), s32[]{:S(2)}) async-start(), calls=%async_computation.9 | async-start | bytes 20447232 | tf_op jit(solution)/shard_map/psum | solution.py:530
  (146 other events, 513.2 us)
Sparse Core Ops, SparseCore 0:
  33.6 34.3 all-gather.4
  96.1 48.3 all-reduce.24
  450.0 41.2 all-reduce.26
  505.2 31.6 all-gather.6
  596.5 75.4 all-reduce.32
  676.9 53.7 all-reduce.28
  737.2 147.8 all-reduce.30
where the time goes:
time: 918 us; the launch traced here: 908 us
  waiting for transfers between devices  441 us (48%)
  local copies, waits for them, and re-layouts  140 us (15%)
  matrix products  129 us (14%)
  other arithmetic  113 us (12%)
  blocking collectives  42.9 us (5%)
  starting transfers between devices  24.2 us (3%)
  between operations  16.3 us (2%)
    psum x1, waiting for transfers between devices, body(): lax.psum(g_in_z.astype(jnp.bfloat16), 'seq').astype(jnp.float32)  145 us
    psum x1, waiting for transfers between devices, body(): lax.psum(expert_saved[10].astype(jnp.bfloat16), 'mp').astype(jnp.float32)  51 us
    all_to_all x1, waiting for transfers between devices, expert_forward(): lax.all_to_all(part_e, 'seq', split_axis=0, concat_axis=0, tiled=True)  48.1 us
    all_to_all x1, waiting for transfers between devices, body(): lax.all_to_all(grad_send, 'seq', split_axis=0, concat_axis=0, tiled=True)  44.7 us
    psum x1, waiting for transfers between devices, mixer_forward(): lax.psum(jnp.dot(normed_y, out_w, preferred_element_type=jnp.float32).ast...  41.1 us
    psum x1, waiting for transfers between devices, body(): lax.psum(jnp.stack([g_gain_one, g_gain_two]).astype(jnp.bfloat16), 'seq')  32.5 us
    psum x1, waiting for transfers between devices, body(): lax.psum(grad_normed_two.astype(jnp.bfloat16), 'mp').astype(jnp.float32)  28.6 us
    gather x2, local copies, waits for them, and re-layouts, expert_forward(): route_vals = returned.reshape(-1, model_width)[positions]  21.6 us
  transfers between devices with their start and end apart: 13, of which 11 were waited for; matrix products, arithmetic and copies ran while one was open for 22% of the time, Pallas kernels for 0%

commit v1 on v0

v1 whole, which is shorter than its diff:
```python
import functools

import jax
import jax.numpy as jnp
from jax import lax
from jax.experimental import pallas as pl
from jax.experimental.pallas import tpu as pltpu
from jax.sharding import PartitionSpec as P

HEAD_DIM = 64
STATE = 128
KCONV = 4
INNER = 3072
LANES = 128
FRONT = 16
EPSILON = 1e-05
F32 = jnp.float32
BF16 = jnp.bfloat16
HIGHEST = lax.Precision.HIGHEST
NN = (((1,), (0,)), ((), ()))
NT = (((1,), (1,)), ((), ()))
TN = (((0,), (0,)), ((), ()))


class Each:
    def __init__(self, array):
        self.array = array


class Scalars:
    def __init__(self, array):
        self.array = array


class Block:
    def __init__(self, array, rows, at):
        self.array, self.rows, self.at = array, rows, at


def struct(shape, dtype):
    return jax.ShapeDtypeStruct(tuple(shape), dtype)


def call(kernel, outs, args, flops, name, grid=1, index=None):
    def spec(a):
        if isinstance(a, Scalars):
            return pl.BlockSpec(memory_space=pltpu.SMEM)
        if isinstance(a, Block):
            return pl.BlockSpec((a.rows, a.array.shape[1]), lambda s, at, k=a.at: (at[k], 0))
        if isinstance(a, Each):
            rest = a.array.shape[1:]
            return pl.BlockSpec((None, *rest), lambda s, *_: (s,) + (0,) * len(rest))
        return pl.BlockSpec(a.shape, lambda s, *_: (0,) * len(a.shape))

    def plain(a):
        return a.array if isinstance(a, (Each, Scalars, Block)) else a

    arrays = [plain(a) for a in args]
    shapes = [plain(a) for a in outs]
    moved = sum(
        a.rows * a.array.shape[1] * a.array.dtype.itemsize
        if isinstance(a, Block)
        else plain(a).size * plain(a).dtype.itemsize
        for a in (*args, *outs)
    )
    grid_spec = pltpu.PrefetchScalarGridSpec(
        num_scalar_prefetch=0 if index is None else 1,
        grid=(grid,),
        in_specs=[spec(a) for a in args],
        out_specs=[spec(a) for a in outs],
    )
    return pl.pallas_call(
        kernel,
        out_shape=shapes,
        grid_spec=grid_spec,
        compiler_params=pltpu.CompilerParams(vmem_limit_bytes=60 * 2**20),
        cost_estimate=pl.CostEstimate(flops=int(flops), bytes_accessed=int(moved), transcendentals=0),
        name=name,
    )(*([] if index is None else [index]), *arrays)


def dot(a, b, dims=NN):
    return lax.dot_general(a.astype(BF16), b.astype(BF16), dims, preferred_element_type=F32)


def exact(a, b, dims=NN):
    return lax.dot_general(a, b, dims, precision=HIGHEST, preferred_element_type=F32)


def sigmoid(v):
    return 1.0 / (1.0 + jnp.exp(-v))


def iota(shape, axis):
    return lax.broadcasted_iota(jnp.int32, shape, axis)


def two_terms(v):
    high = v.astype(BF16)
    return high, (v - high.astype(F32)).astype(BF16)


def to_lanes(v):
    return jnp.concatenate([v, jnp.zeros((v.shape[0], LANES - v.shape[1]), v.dtype)], axis=1)


def spread_matrix(width):
    return (iota((LANES, width), 1) // HEAD_DIM == iota((LANES, width), 0)).astype(F32)


def prepared(xbc, dt, conv_x, conv_bc, head_par, meta):
    rows = dt.shape[0]
    width = conv_x.shape[1]
    conv = jnp.concatenate([conv_x[...], conv_bc[...]], axis=1)
    hp = to_lanes(head_par[...])
    where = iota((rows, 1), 0) + meta[2]
    live = (where < meta[pl.program_id(0)]).astype(F32)
    xf = xbc[...].astype(F32)
    summed = conv[KCONV : KCONV + 1]
    taps = []
    for j in range(KCONV):
        shifted = xf[FRONT - (KCONV - 1) + j : FRONT - (KCONV - 1) + j + rows]
        taps.append(shifted)
        summed = summed + conv[j : j + 1] * shifted
    sig = sigmoid(summed)
    act = summed * sig
    xs = act[:, :width] * live
    b = act[:, width : width + STATE]
    c = act[:, width + STATE :]
    raw = dt[...] + hp[0:1]
    step = (jnp.maximum(raw, 0.0) + jnp.log1p(jnp.exp(-jnp.abs(raw)))) * live
    rate = -jnp.exp(hp[1:2])
    logd = rate * step
    lower = (iota((rows, rows), 0) >= iota((rows, rows), 1)).astype(F32)
    cum = exact(lower, logd)
    return dict(
        conv=conv, skip=hp[2:3], live=live, taps=taps, summed=summed, sig=sig, xs=xs, b=b, c=c, raw=raw,
        step=step, rate=rate, logd=logd, cum=cum,
    )


def pack_state(o_send, state, decay):
    size = state.shape[0]
    high, low = two_terms(decay)
    row = iota((FRONT, LANES), 0)
    more = jnp.where(row == 0, high.astype(F32), 0.0) + jnp.where(row == 1, low.astype(F32), 0.0)
    o_send[:size, :] = state.astype(BF16)
    o_send[size:, :] = more.astype(BF16)


def unpack_state(send):
    size = send.shape[0] - FRONT
    more = send[size:, :].astype(F32)
    return send[:size, :].astype(F32), more[0:1] + more[1:2]


def k_in(tok, gains, wz, wx, wbc, wdt, conv_x, conv_bc, head_par, meta, o_norm, o_z, o_xbc, o_dt, o_send, o_tot):
    width = wz.shape[1]
    x = tok[...].astype(F32)
    scale = lax.rsqrt(jnp.mean(x * x, axis=-1, keepdims=True) + EPSILON)
    normed = (x * scale * gains[0:1]).astype(BF16)
    own = normed[FRONT:]
    o_norm[...] = own
    o_xbc[:, :width] = dot(normed, wx[...]).astype(BF16)
    o_xbc[:, width:] = dot(normed, wbc[...]).astype(BF16)
    o_dt[...] = to_lanes(dot(own, wdt[...]))
    o_z[...] = dot(own, wz[...])
    p = prepared(o_xbc, o_dt, conv_x, conv_bc, head_par, meta)
    rows = own.shape[0]
    last = p["cum"][rows - 1 : rows]
    weight = exact(p["step"] * jnp.exp(last - p["cum"]), spread_matrix(width))
    decay = jnp.exp(last)
    pack_state(o_send, dot(p["xs"] * weight, p["b"], TN), decay)
    o_tot[...] = jnp.broadcast_to(decay, o_tot.shape)


def pair_masks(rows):
    low = iota((rows, LANES), 1) < HEAD_DIM
    return low, jnp.logical_not(low)


def decays(cum, cum_t, h, ahead):
    gap = cum[:, h : h + 1] - cum_t[h : h + 1, :]
    return jnp.where(ahead, jnp.exp(jnp.where(ahead, gap, 0.0)), 0.0)


def by_halves(v, low, high):
    return jnp.concatenate(
        [jnp.where(low, v, 0.0).astype(BF16), jnp.where(high, v, 0.0).astype(BF16)], axis=0
    )


def k_intra(xbc, dt, conv_x, conv_bc, head_par, meta, o_y, o_c, o_ecum):
    width = o_y.shape[1]
    p = prepared(xbc, dt, conv_x, conv_bc, head_par, meta)
    xs, cum = p["xs"], p["cum"]
    rows = cum.shape[0]
    spread = spread_matrix(width)
    ahead = iota((rows, rows), 0) >= iota((rows, rows), 1)
    cum_t = cum.T
    scores = dot(p["c"], p["b"], NT)
    spread_out = exact(
        jnp.concatenate([p["step"], jnp.exp(cum), jnp.broadcast_to(p["skip"], (8, LANES))], axis=0), spread
    )
    xw = xs * spread_out[:rows]
    skip = spread_out[2 * rows : 2 * rows + 1]
    low, high = pair_masks(rows)
    o_c[...] = p["c"].astype(BF16)
    o_ecum[...] = spread_out[rows : 2 * rows]
    for pair in range(width // LANES):
        cols = slice(pair * LANES, (pair + 1) * LANES)
        mats = [(decays(cum, cum_t, h, ahead) * scores).astype(BF16) for h in (2 * pair, 2 * pair + 1)]
        within = dot(jnp.concatenate(mats, axis=1), by_halves(xw[:, cols], low, high))
        o_y[:, cols] = within + skip[:, cols] * xs[:, cols]


def k_scan(first, last, after, recv, send_in, total, whole, before, reach, *outs):
    own, own_decay = unpack_state(send_in)
    if first:
        whole_now, total_now = own, own_decay
        before_now, reach_now = None, None
    else:
        whole_now, total_now = whole[...], total[0:1]
        before_now, reach_now = before[...], reach[0:1]
    state, decay = unpack_state(recv)
    size = state.shape[0]
    mine = iota((size, LANES), 1) == iota((size, LANES), 0) // HEAD_DIM

    def rows_of(d):
        return jnp.sum(jnp.where(mine, d, 0.0), axis=1, keepdims=True)

    is_after = after[0] == 1
    if first:
        new_before = jnp.where(is_after, state, 0.0)
        new_reach = jnp.where(is_after, decay, 1.0)
    else:
        new_before = jnp.where(is_after, before_now + rows_of(reach_now) * state, before_now)
        new_reach = jnp.where(is_after, reach_now * decay, reach_now)
    outs[0][...] = new_before
    if last:
        return
    o_before, o_reach, o_whole, o_total, o_send = outs
    o_reach[...] = jnp.broadcast_to(new_reach, o_reach.shape)
    new_whole = jnp.where(
        is_after, whole_now + rows_of(total_now) * state, state + rows_of(decay) * whole_now
    )
    new_total = total_now * decay
    o_whole[...] = new_whole
    o_total[...] = jnp.broadcast_to(new_total, o_total.shape)
    pack_state(o_send, new_whole, new_total)


def k_out(y0, c, ecum, entering, z, gain, w, o_y, o_part):
    model = w.shape[1]
    y = y0[...] + ecum[...] * dot(c[...], entering[...], NT)
    o_y[...] = y
    zv = z[...]
    gated = y * zv * sigmoid(zv)
    high, low = two_terms(jnp.sum(gated * gated, axis=-1, keepdims=True))
    o_part[:, :model] = dot(gated * gain[...], w[...]).astype(BF16)
    o_part[:, model:] = to_lanes(jnp.concatenate([high, low], axis=1))


def k_back_gate(dm, y, z, gain, w, c, ecum, total, o_dz, o_dy, o_send, o_gain, o_norm):
    model = w.shape[1]
    more = dm[:, model:].astype(F32)
    stat = more[:, 0:1] + more[:, 1:2]
    scale = more[:, 2:3] + more[:, 3:4]
    dn = dot(dm[:, :model], w[...], NT)
    zv = z[...]
    sig = sigmoid(zv)
    silu = zv * sig
    yv = y[...]
    gated = yv * silu
    dgated = scale * gain[...] * dn - gated * (scale * scale * stat / INNER)
    o_dz[...] = (dgated * yv * sig * (1.0 + zv * (1.0 - sig))).astype(BF16)
    dy = dgated * silu
    o_dy[...] = dy
    o_gain[...] = jnp.broadcast_to(jnp.sum(dn * gated * scale, axis=0, keepdims=True), o_gain.shape)
    o_norm[...] = (gated * scale * gain[...]).astype(BF16)
    pack_state(o_send, dot(ecum[...] * dy, c[...], TN), total[0:1])


def k_back_intra(xbc, dt, conv_x, conv_bc, head_par, meta, dy, dz, wz, o_dxw, o_db, o_dc, o_dcum, o_dn):
    width = dy.shape[1]
    p = prepared(xbc, dt, conv_x, conv_bc, head_par, meta)
    cum = p["cum"]
    rows = cum.shape[0]
    o_dn[...] = dot(dz[...], wz[...], NT)
    ahead = iota((rows, rows), 0) >= iota((rows, rows), 1)
    cum_t = cum.T
    scores = dot(p["c"], p["b"], NT)
    xw = p["xs"] * exact(p["step"], spread_matrix(width))
    low, high = pair_masks(rows)
    lane = iota((rows, LANES), 1)
    sub = iota((LANES, rows), 0)
    dscores = jnp.zeros((rows, rows), F32)
    plus = jnp.zeros((rows, LANES), F32)
    minus = jnp.zeros((LANES, rows), F32)
    for pair in range(width // LANES):
        cols = slice(pair * LANES, (pair + 1) * LANES)
        dstack = by_halves(dy[:, cols], low, high)
        dmats = dot(dstack, xw[:, cols], NT)
        mats = []
        for i, h in enumerate((2 * pair, 2 * pair + 1)):
            decay = decays(cum, cum_t, h, ahead)
            mat = decay * scores
            dmat = dmats[i * rows : (i + 1) * rows]
            dscores = dscores + dmat * decay
            flow = dmat * mat
            plus = jnp.where(lane == h, jnp.sum(flow, axis=1, keepdims=True), plus)
            minus = jnp.where(sub == h, jnp.sum(flow, axis=0, keepdims=True), minus)
            mats.append(mat.astype(BF16))
        o_dxw[:, cols] = dot(jnp.concatenate(mats, axis=0), dstack, TN)
    o_dcum[...] = plus - minus.T
    o_dc[...] = dot(dscores, p["b"])
    o_db[...] = dot(dscores, p["c"], TN)


def k_back_state(
    xbc, dt, conv_x, conv_bc, head_par, meta, dy, dxw0, db0, dc0, dcum0, entering, leaving,
    o_dxbc, o_ddt, o_conv, o_hp,
):
    width = dy.shape[1]
    p = prepared(xbc, dt, conv_x, conv_bc, head_par, meta)
    xs, b, c, cum, step, rate, live = (p[k] for k in ("xs", "b", "c", "cum", "step", "rate", "live"))
    summed, sig, conv = p["summed"], p["sig"], p["conv"]
    rows = cum.shape[0]
    spread = spread_matrix(width)
    last = cum[rows - 1 : rows]
    spread_out = exact(
        jnp.concatenate(
            [step, jnp.exp(cum), jnp.exp(last - cum), jnp.broadcast_to(p["skip"], (8, LANES))], axis=0
        ),
        spread,
    )
    step_x, ecum_x, rem_x = (spread_out[i * rows : (i + 1) * rows] for i in range(3))
    skip_x = spread_out[3 * rows : 3 * rows + 1]
    dyv = dy[...]
    h0 = entering[...]
    h1 = leaving[...]
    xw = xs * step_x
    scaled_dy = ecum_x * dyv
    dc = dc0[...] + dot(scaled_dy, h0)
    from_state = scaled_dy * dot(c, h0, NT)
    to_state = rem_x * dot(b, h1, NT)
    dxw = dxw0[...] + to_state
    db = db0[...] + dot(xw * rem_x, h1)
    dtotal = jnp.sum(exact(spread, h1 * h0), axis=1, keepdims=True)
    sums = exact(jnp.concatenate([from_state, xw * to_state, dxw * xs, dyv * xs], axis=0), spread, NT)
    flow = sums[rows : 2 * rows]
    dlast = jnp.broadcast_to(dtotal, (LANES, LANES)).T[0:1] * jnp.exp(last) + jnp.sum(
        flow, axis=0, keepdims=True
    )
    dcum = dcum0[...] + sums[:rows] - flow
    dcum = dcum + jnp.where(iota((rows, LANES), 0) == rows - 1, dlast, 0.0)
    upper = (iota((rows, rows), 0) <= iota((rows, rows), 1)).astype(F32)
    dlogd = exact(upper, dcum)
    draw = (sums[2 * rows : 3 * rows] + dlogd * rate) * live * sigmoid(p["raw"])
    o_ddt[...] = draw.astype(BF16)
    row = iota((8, LANES), 0)
    o_hp[...] = (
        jnp.where(row == 0, jnp.sum(draw, axis=0, keepdims=True), 0.0)
        + jnp.where(row == 1, jnp.sum(dlogd * p["logd"], axis=0, keepdims=True), 0.0)
        + jnp.where(row == 2, jnp.sum(sums[3 * rows : 4 * rows], axis=0, keepdims=True), 0.0)
    )
    dx = (dxw * step_x + skip_x * dyv) * live
    dsummed = jnp.concatenate([dx, db, dc], axis=1) * sig * (1.0 + summed * (1.0 - sig))
    zeros = jnp.zeros((FRONT, dsummed.shape[1]), F32)
    padded = jnp.concatenate([zeros, dsummed, zeros], axis=0)
    total = rows + FRONT
    out = jnp.zeros((total, dsummed.shape[1]), F32)
    for j in range(KCONV):
        shift = KCONV - 1 - j
        out = out + conv[j : j + 1] * padded[shift : shift + total]
        o_conv[j : j + 1] = jnp.sum(dsummed * p["taps"][j], axis=0, keepdims=True)
    o_conv[KCONV : KCONV + 1] = jnp.sum(dsummed, axis=0, keepdims=True)
    o_conv[KCONV + 1 :] = jnp.zeros((o_conv.shape[0] - KCONV - 1, dsummed.shape[1]), F32)
    o_dxbc[...] = out


def k_back_in(dn0, dxbc, edge, ddt, tok, wx, wbc, wdt, o_part, o_dx, o_bc, o_gain):
    width = wx.shape[1]
    rows = dn0.shape[0]
    tail = jnp.concatenate([jnp.zeros((rows - FRONT, edge.shape[1]), F32), edge[...]], axis=0)
    own = (dxbc[FRONT:, :] + tail).astype(BF16)
    dx, dbc = own[:, :width], own[:, width:]
    o_dx[:, :width] = dx
    o_dx[:, width:] = ddt[...]
    o_bc[...] = dbc
    dn = dn0[...] + dot(dx, wx[...], NT) + dot(dbc, wbc[...], NT) + dot(ddt[...], to_lanes(wdt[...]), NT)
    o_part[...] = dn.astype(BF16)
    x = tok[FRONT:, :].astype(F32)
    scale = lax.rsqrt(jnp.mean(x * x, axis=-1, keepdims=True) + EPSILON)
    o_gain[...] = jnp.broadcast_to(jnp.sum(dn * x * scale, axis=0, keepdims=True), o_gain.shape)


def k_rows_one(arrived, tok, gains, o_residual, o_mixer, o_two, o_scales):
    model = tok.shape[1]
    total = sum(arrived[k].astype(F32) for k in range(arrived.shape[0]))
    scale = lax.rsqrt((total[:, model : model + 1] + total[:, model + 1 : model + 2]) / INNER + EPSILON)
    mixer = total[:, :model] * scale
    residual = tok[...].astype(F32) + mixer
    scale_two = lax.rsqrt(jnp.mean(residual * residual, axis=-1, keepdims=True) + EPSILON)
    o_residual[...] = residual
    o_mixer[...] = mixer
    o_two[...] = (residual * scale_two * gains[1:2]).astype(BF16)
    o_scales[...] = to_lanes(jnp.concatenate([scale, scale_two], axis=1))


def k_rows_two(arrived, dout, two, residual, mixer, scales, gains, router, o_dm, o_dr, o_gain, o_router):
    model = two.shape[1]
    experts = router.shape[1]
    both = sum(arrived[k].astype(F32) for k in range(arrived.shape[0]))
    dn2, dgate = both[:, :model], both[:, model:]
    w = to_lanes(router[...])
    probs = masked_softmax(dot(two[...], w), dout[:, model:].astype(F32))
    dlog = (probs * (dgate - jnp.sum(probs * dgate, axis=-1, keepdims=True))).astype(BF16)
    dn2 = dn2 + dot(dlog, w, NT)
    o_router[...] = dot(dlog, two[...], TN)[:experts]
    scale, scale_two = scales[:, 0:1], scales[:, 1:2]
    scaled = residual[...] * scale_two
    o_gain[...] = jnp.broadcast_to(jnp.sum(dn2 * scaled, axis=0, keepdims=True), o_gain.shape)
    gg = dn2 * gains[1:2]
    dr = dout[:, :model].astype(F32) + scale_two * (
        gg - scaled * jnp.mean(gg * scaled, axis=-1, keepdims=True)
    )
    o_dr[...] = dr
    dm = dr.astype(BF16)
    o_dm[:, :model] = dm
    stat = jnp.sum(dm.astype(F32) * mixer[...], axis=-1, keepdims=True)
    o_dm[:, model:] = to_lanes(jnp.concatenate([*two_terms(stat), *two_terms(scale)], axis=1))


def k_rows_three(arrived, tok, dr, gains, o_dtok):
    dn1 = sum(arrived[k].astype(F32) for k in range(arrived.shape[0]))
    x = tok[...].astype(F32)
    scale = lax.rsqrt(jnp.mean(x * x, axis=-1, keepdims=True) + EPSILON)
    scaled = x * scale
    gg = dn1 * gains[0:1]
    o_dtok[...] = (
        dr[...] + scale * (gg - scaled * jnp.mean(gg * scaled, axis=-1, keepdims=True))
    ).astype(BF16)


def k_rows_out(arrived, residual, o_out):
    total = sum(arrived[k].astype(F32) for k in range(arrived.shape[0]))
    o_out[...] = (residual[...] + total).astype(BF16)


def masked_softmax(logits, mask):
    on = mask > 0.0
    top = jnp.max(jnp.where(on, logits, -3.0e38), axis=-1, keepdims=True)
    e = jnp.where(on, jnp.exp(jnp.where(on, logits - top, 0.0)), 0.0)
    return e / jnp.sum(e, axis=-1, keepdims=True)


def mlp(x, do, wg, wu, wd, gate):
    g = dot(x, wg)
    u = dot(x, wu)
    sig = sigmoid(g)
    silu = g * sig
    hid = (silu * u).astype(BF16)
    dh = dot(do, wd, NT)
    if gate is None:
        hg, dgate = hid, None
    else:
        hf = hid.astype(F32)
        dgate = jnp.sum(hf * dh, axis=-1, keepdims=True)
        hg = (hf * gate).astype(BF16)
        dh = dh * gate
    dg = (dh * u * sig * (1.0 + g * (1.0 - sig))).astype(BF16)
    du = (dh * silu).astype(BF16)
    return hg, dg, du, dgate


def k_expert(slots, index, *refs):
    router, w_in, w_down = refs[:3]
    count = sum(slots)
    xs, ds = refs[3 : 3 + count], refs[3 + count : 3 + 2 * count]
    outs = refs[3 + 2 * count :]
    width = w_in.shape[2]
    wg, wu, wd = w_in[0, 0], w_in[0, 1], w_down[0]
    w = to_lanes(router[...])
    at = 0
    for i, pieces in enumerate(slots):
        o_out, o_dx, o_keep = outs[3 * i : 3 * i + 3]
        x = jnp.concatenate([xs[at + j][...] for j in range(pieces)], axis=0)
        dall = jnp.concatenate([ds[at + j][...] for j in range(pieces)], axis=0)
        at += pieces
        do = dall[:, :width]
        mask = dall[:, width:].astype(F32)
        lane = iota(mask.shape, 1)
        probs = masked_softmax(dot(x, w), mask)
        gate = jnp.sum(jnp.where(lane == index[0], probs, 0.0), axis=-1, keepdims=True)
        hg, dg, du, dgate = mlp(x, do, wg, wu, wd, gate)
        half = hg.shape[1]
        o_keep[:, :half] = hg
        o_keep[:, half : 2 * half] = dg
        o_keep[:, 2 * half :] = du
        o_out[...] = dot(hg, wd).astype(BF16)
        o_dx[:, :width] = (dot(dg, wg, NT) + dot(du, wu, NT)).astype(BF16)
        chosen = jnp.sum(jnp.where(lane == index[0], mask, 0.0), axis=-1, keepdims=True) > 0.0
        o_dx[:, width:] = jnp.where(jnp.logical_and(lane == index[0], chosen), dgate, 0.0).astype(BF16)


def k_shared(x, do, w_in, w_down, o_out, o_dx):
    width = w_in.shape[1]
    wg, wu, wd = w_in[0], w_in[1], w_down[...]
    hg, dg, du, _ = mlp(x[...], do[:, :width], wg, wu, wd, None)
    o_out[...] = dot(hg, wd).astype(BF16)
    o_dx[...] = (dot(dg, wg, NT) + dot(du, wu, NT)).astype(BF16)


def taken(xs, i, slots):
    at = sum(slots[:i])
    return jnp.concatenate([xs[at + j][...] for j in range(slots[i])], axis=0)


def k_weights(slots, index, *refs):
    s_in, s_down = refs[:2]
    pieces, count = sum(slots), len(slots)
    xs = refs[2 : 2 + pieces]
    ds = refs[2 + pieces : 2 + pieces + count]
    ks = refs[2 + pieces + count : 2 + pieces + 2 * count]
    o_in, o_down, o_s_in, o_s_down = refs[2 + pieces + 2 * count :]
    width, half = o_in.shape[1], o_in.shape[2]
    for i in range(count):
        x = taken(xs, i, slots)
        do = ds[i][:, :width]
        kept = ks[i][...]
        hg, dg, du, _ = mlp(x, do, s_in[0], s_in[1], s_down[...], None)
        parts = (
            dot(x, kept[:, half : 2 * half], TN),
            dot(x, kept[:, 2 * half :], TN),
            dot(kept[:, :half], do, TN),
            dot(x, dg, TN),
            dot(x, du, TN),
            dot(hg, do, TN),
        )
        into = (o_in.at[0], o_in.at[1], o_down, o_s_in.at[0], o_s_in.at[1], o_s_down)
        for ref, part in zip(into, parts):
            if i == 0:
                ref[...] = part
            else:
                ref[...] += part


def k_outer(slots_a, slots_b, count_b, *refs):
    refs = refs[1:]
    na = sum(slots_a)
    a_refs = refs[:na]
    b_refs = [refs[na + j * sum(slots_b) : na + (j + 1) * sum(slots_b)] for j in range(count_b)]
    outs = refs[na + count_b * sum(slots_b) :]
    totals = [None] * count_b
    for i in range(len(slots_a)):
        a = taken(a_refs, i, slots_a)
        for j in range(count_b):
            part = dot(a, taken(b_refs[j], i, slots_b), TN)
            totals[j] = part if totals[j] is None else totals[j] + part
    for j in range(count_b):
        outs[j][...] = totals[j]


def outer(a, bs, name):
    step = 256
    columns = a.pieces[0].shape[1]
    args, specs = [], []
    for g in (a, *bs):
        for piece in g.pieces:
            args.append(piece)
            if g is a:
                specs.append(pl.BlockSpec((piece.shape[0], step), lambda i, *_: (0, i)))
            else:
                specs.append(pl.BlockSpec(piece.shape, lambda i, *_: (0, 0)))
    widths = [b.pieces[0].shape[1] for b in bs]
    rows = sum(p.shape[0] for p in a.pieces)
    grid_spec = pltpu.PrefetchScalarGridSpec(
        num_scalar_prefetch=1,
        grid=(columns // step,),
        in_specs=specs,
        out_specs=[pl.BlockSpec((step, w), lambda i, *_: (i, 0)) for w in widths],
    )
    moved = sum(x.size * x.dtype.itemsize for x in args) + sum(4 * columns * w for w in widths)
    return pl.pallas_call(
        functools.partial(k_outer, a.slots, bs[0].slots, len(bs)),
        out_shape=[struct((columns, w), F32) for w in widths],
        grid_spec=grid_spec,
        compiler_params=pltpu.CompilerParams(vmem_limit_bytes=60 * 2**20),
        cost_estimate=pl.CostEstimate(
            flops=2 * rows * columns * sum(widths), bytes_accessed=int(moved), transcendentals=0
        ),
        name=name,
    )(a.index, *args)


def flip(array, axis, bit):
    return lax.ppermute(array, axis, [(i, i ^ bit) for i in range(lax.axis_size(axis))])


def bits_of(axis):
    return [1 << b for b in range(lax.axis_size(axis).bit_length() - 1)]


class Gathered:
    def __init__(self, pieces, slots, index):
        self.pieces, self.slots, self.index = pieces, slots, index

    def part(self, first, last):
        at, to = sum(self.slots[:first]), sum(self.slots[:last])
        return Gathered(self.pieces[at:to], self.slots[first:last], self.index[first:last])


XOR_ORDER = (0, 1, 2, 3, 4, 5, 6, 7)


def gather(own):
    size = lax.axis_size("seq")
    place = lax.axis_index("seq")
    if size != 8:
        every = lax.all_gather(own, "seq")
        return Gathered([every[k] for k in range(size)], [1] * size, jnp.arange(size, dtype=jnp.int32))
    core, x, y = bits_of("seq")
    half = own.shape[0] // 2
    by_x = flip(own, "seq", x)
    by_y = flip(own, "seq", y)
    top = flip(by_x[:half], "seq", y)
    bottom = flip(by_y[half:], "seq", x)
    near = [own, by_x, by_y, top, bottom]
    far = [flip(a, "seq", core) for a in near]
    pieces = [near[0], far[0], near[1], far[1], near[2], far[2], near[3], near[4], far[3], far[4]]
    index = jnp.stack([place ^ k for k in XOR_ORDER]).astype(jnp.int32)
    return Gathered(pieces, [1, 1, 1, 1, 1, 1, 2, 2], index)


def low_sum(*terms):
    return sum(t.astype(F32) for t in terms).astype(BF16)


def k_split(x0, x1, y0, y1, d0, d1, o_x, o_y, o_x_late, o_y_late):
    half = o_x_late.shape[0]
    x = low_sum(x0[...], x1[...])
    y = low_sum(y0[...], y1[...])
    d = low_sum(d0[...], d1[...])
    o_x[:half, :] = d[:half]
    o_x[half:, :] = x[:half]
    o_y[:half, :] = d[half:]
    o_y[half:, :] = y[half:]
    o_x_late[...] = x[half:]
    o_y_late[...] = y[:half]


def k_late(x, y, ax, ay, o_x, o_y):
    half = x.shape[0]
    o_x[...] = low_sum(x[...], ay[:half, :])
    o_y[...] = low_sum(y[...], ax[:half, :])


def k_join(a, b, more, ax, ay, bx, by, o):
    half = bx.shape[0]
    w = more.shape[1]
    total = a[...].astype(F32) + b[...].astype(F32)
    o[:half, :] = low_sum(total[:half], ax[half:, :], by[...])
    o[half:, :] = low_sum(total[half:], ay[half:, :], bx[...])
    o[:, :w] = low_sum(o[:, :w], more[...])


def scatter(parts, more, name):
    size = lax.axis_size("seq")
    if size != 8:
        every = jnp.concatenate(parts, axis=0)
        total = lax.psum_scatter(every, "seq", scatter_dimension=0, tiled=True)
        return jnp.concatenate(
            [low_sum(total[:, : more.shape[1]], more), total[:, more.shape[1] :]], axis=1
        )
    core, x, y = bits_of("seq")
    rows, width = parts[0].shape
    r1, r3, r5, r7 = (flip(parts[k], "seq", core) for k in (1, 3, 5, 7))
    full, part = struct((rows, width), BF16), struct((rows // 2, width), BF16)
    to_x, to_y, late_x, late_y = call(
        k_split, [full, full, part, part], [parts[2], r3, parts[4], r5, parts[6], r7], 0, name + "_split"
    )
    ax, ay = flip(to_x, "seq", x), flip(to_y, "seq", y)
    late_x, late_y = call(k_late, [part, part], [late_x, late_y, ax, ay], 0, name + "_late")
    bx, by = flip(late_x, "seq", x), flip(late_y, "seq", y)
    [out] = call(k_join, [full], [parts[0], r1, more, ax, ay, bx, by], 0, name + "_join")
    return out


def scan(send, backward, name):
    place = lax.axis_index("seq")
    seqs, size = send.shape[0], send.shape[1] - FRONT
    bits = bits_of("seq")
    state = struct((seqs, size, LANES), F32)
    row = struct((seqs, 8, LANES), F32)
    total = whole = before = reach = None
    own = send
    for bit in bits:
        recv = flip(send, "seq", bit)
        is_set = (place & bit) != 0
        after = (jnp.logical_not(is_set) if backward else is_set).astype(jnp.int32)[None]
        first, last = bit == bits[0], bit == bits[-1]
        outs = [state] if last else [state, row, state, row, struct(own.shape, BF16)]
        if first:
            held = []
            kernel = lambda after, recv, own, *o, last=last: k_scan(
                True, last, after, recv, own, None, None, None, None, *o
            )
        else:
            held = [Each(a) for a in (total, whole, before, reach)]
            kernel = functools.partial(k_scan, False, last)
        made = call(
            kernel,
            [Each(o) for o in outs],
            [Scalars(after), Each(recv), Each(own), *held],
            0,
            name,
            grid=seqs,
        )
        if last:
            return made[0]
        before, reach, whole, total, send = made
    return before


def rows_of_mp(array):
    share = array.shape[0] // lax.axis_size("mp")
    return lax.dynamic_slice_in_dim(array, lax.axis_index("mp") * share, share, 0)


def shares_of_mp(array):
    size = lax.axis_size("mp")
    cut = array.reshape(size, array.shape[0] // size, array.shape[1])
    return lax.all_to_all(cut, "mp", 0, 0, tiled=True)


def gather_mp(array):
    return lax.all_gather(array, "mp", tiled=True)


def all_sum(array, axes):
    for axis in axes:
        for bit in bits_of(axis):
            array = array + flip(array, axis, bit)
    return array


def passed_along(block, axis, distance):
    devices = range(lax.axis_size(axis))
    route = [(i - distance, i) for i in devices if i - distance in devices]
    return lax.ppermute(block, axis, route)


def body(
    tokens, lengths, expert_ids, norm_gains, in_z, in_x, in_bc, in_dt, conv_x, conv_bc,
    head_par, gn_gain, out_w, router, shared_in, shared_down, expert_in, expert_down, d_out,
):
    piece, seqs, model = tokens.shape
    width = in_z.shape[1]
    heads = head_par.shape[1]
    experts = router.shape[1]
    half = expert_in.shape[-1]
    n_seq, n_mp = lax.axis_size("seq"), lax.axis_size("mp")
    seq_at, mp_at = lax.axis_index("seq"), lax.axis_index("mp")
    rows = seqs * piece
    share = rows // n_mp
    bc = 2 * STATE

    meta = jnp.concatenate([lengths, (seq_at * piece).astype(jnp.int32)[None]])
    tok = jnp.transpose(tokens, (1, 0, 2))
    edge_in = passed_along(tokens[piece - (KCONV - 1) :], "seq", 1)
    front = jnp.pad(jnp.transpose(edge_in, (1, 0, 2)), ((0, 0), (FRONT - (KCONV - 1), 0), (0, 0)))
    tok_front = jnp.concatenate([front, tok], axis=1)
    gn = gn_gain[None]
    picked = jnp.sum(
        (expert_ids[..., None] == jnp.arange(LANES, dtype=jnp.int32)).astype(F32), axis=2
    ).astype(BF16)
    small = [conv_x, conv_bc, head_par, Scalars(meta)]

    def both(*shape, dtype=F32):
        return Each(struct((seqs, *shape), dtype))

    normed, gate_z, xbc, dt_raw, send, totals = call(
        k_in,
        [
            both(piece, model, dtype=BF16),
            both(piece, width),
            both(piece + FRONT, width + bc, dtype=BF16),
            both(piece, LANES),
            both(width + FRONT, LANES, dtype=BF16),
            both(8, LANES),
        ],
        [Each(tok_front), norm_gains, in_z, in_x, in_bc, in_dt, *small],
        2 * rows * model * (2 * width + bc + LANES),
        "mixer_in",
        grid=seqs,
    )
    d_ext, send = lax.optimization_barrier((jnp.transpose(jnp.concatenate([d_out, picked], axis=-1), (1, 0, 2)), send))
    d_ext = d_ext.reshape(rows, model + LANES)
    d_all = lax.all_gather(d_ext, "seq", tiled=True)
    entering = scan(send, False, "scan")
    intra, c_mat, ecum = call(
        k_intra,
        [both(piece, width), both(piece, STATE, dtype=BF16), both(piece, width)],
        [Each(xbc), Each(dt_raw), *small],
        2 * rows * piece * width * 4,
        "mixer_intra",
        grid=seqs,
    )
    mixed, part = call(
        k_out,
        [both(piece, width), both(piece, model + LANES, dtype=BF16)],
        [Each(intra), Each(c_mat), Each(ecum), Each(entering), Each(gate_z), gn, out_w],
        2 * rows * width * (STATE + model),
        "mixer_out",
        grid=seqs,
    )
    tok_own = rows_of_mp(tok.reshape(rows, model))
    d_own = rows_of_mp(d_ext)
    arrived = shares_of_mp(part.reshape(rows, model + LANES))
    normed, part = lax.optimization_barrier((normed, part))
    if n_seq == 8:
        n_got = gather(normed.reshape(rows, model))
    of_share = struct((share, model), F32)
    residual, mixer_own, two_own, scales = call(
        k_rows_one,
        [of_share, of_share, struct((share, model), BF16), struct((share, LANES), F32)],
        [arrived, tok_own, norm_gains],
        0,
        "rows_one",
    )
    two = gather_mp(two_own)

    out_shared, dx_shared = call(
        k_shared,
        [struct((rows, model), BF16), struct((rows, model), BF16)],
        [two, d_ext, shared_in, shared_down],
        2 * rows * model * half * 6,
        "shared",
    )
    x_got = gather(two)
    mine = ((seq_at * n_mp + mp_at) // 2).astype(jnp.int32)[None]
    groups = [(0, 2), (2, 6), (6, 8)] if n_seq == 8 else [(i, i + 4) for i in range(0, n_seq, 4)]
    e_out, e_dx, e_keep = [], [], []
    for first, last in groups:
        part_x = x_got.part(first, last)
        blocks, at = [mine], 1
        d_blocks = []
        for i, pieces in enumerate(part_x.slots):
            for j in range(pieces):
                blocks.append(part_x.index[i : i + 1] * pieces + j)
                d_blocks.append(Block(d_all, rows // pieces, at))
                at += 1
        outs = [
            struct((rows, model), BF16),
            struct((rows, model + LANES), BF16),
            struct((rows, 3 * half), BF16),
        ] * (last - first)
        made = call(
            functools.partial(k_expert, part_x.slots),
            outs,
            [router, expert_in, expert_down, *part_x.pieces, *d_blocks],
            2 * rows * (last - first) * model * half * 6.5,
            "experts",
            index=jnp.concatenate(blocks),
        )
        e_out += made[0::3]
        e_dx += made[1::3]
        e_keep += made[2::3]

    arrived = shares_of_mp(scatter(e_dx, dx_shared, "dx"))
    g_expert_in = g_expert_down = g_shared_in = g_shared_down = 0.0
    for at in range(0, n_seq, 8):
        now = x_got.part(at, at + 8)
        flops = 2 * 8 * rows * model * half
        made = call(
            functools.partial(k_weights, now.slots),
            [struct((2, model, half), F32), struct((half, model), F32)] * 2,
            [shared_in, shared_down, *now.pieces]
            + [Block(d_all, rows, i) for i in range(8)]
            + e_keep[at : at + 8],
            9 * flops,
            "expert_weights",
            index=now.index,
        )
        g_expert_in, g_expert_down = g_expert_in + made[0], g_expert_down + made[1]
        g_shared_in, g_shared_down = g_shared_in + made[2], g_shared_down + made[3]

    dm_own, d_residual, g_gain_two, g_router = call(
        k_rows_two,
        [
            struct((share, model + LANES), BF16),
            of_share,
            struct((8, model), F32),
            struct((experts, model), F32),
        ],
        [arrived, d_own, two_own, residual, mixer_own, scales, norm_gains, router],
        0,
        "rows_two",
    )
    dm = gather_mp(dm_own).reshape(seqs, piece, model + LANES)

    dz, dy, send, g_gn, normed_y = call(
        k_back_gate,
        [
            both(piece, width, dtype=BF16),
            both(piece, width),
            both(width + FRONT, LANES, dtype=BF16),
            both(8, width),
            both(piece, width, dtype=BF16),
        ],
        [Each(dm), Each(mixed), Each(gate_z), gn, out_w, Each(c_mat), Each(ecum), Each(totals)],
        2 * rows * width * (model + STATE),
        "back_gate",
        grid=seqs,
    )
    leaving = scan(send, True, "scan_back")
    if n_seq != 8:
        normed, leaving = lax.optimization_barrier((normed, leaving))
        n_got = gather(normed.reshape(rows, model))
    g_out_w = lax.dot_general(
        normed_y.reshape(rows, width), dm.reshape(rows, model + LANES)[:, :model], TN, preferred_element_type=F32
    )
    g_out_w = lax.psum(g_out_w.astype(BF16), "seq").astype(F32)

    out_arrived = shares_of_mp(scatter(e_out, out_shared, "out"))
    [out_own] = call(
        k_rows_out, [struct((share, model), BF16)], [out_arrived, residual], 0, "rows_out"
    )
    output = jnp.transpose(gather_mp(out_own).reshape(seqs, piece, model), (1, 0, 2)).astype(F32)

    dz_got = gather(dz.reshape(rows, width))
    dxw0, db0, dc0, dcum0, dn0 = call(
        k_back_intra,
        [both(piece, width), both(piece, STATE), both(piece, STATE), both(piece, LANES), both(piece, model)],
        [Each(xbc), Each(dt_raw), *small, Each(dy), Each(dz), in_z],
        2 * rows * width * (model + 4 * piece),
        "back_intra",
        grid=seqs,
    )
    d_xbc, d_dt, g_conv, g_hp = call(
        k_back_state,
        [
            both(piece + FRONT, width + bc),
            both(piece, LANES, dtype=BF16),
            both(8, width + bc),
            both(8, LANES),
        ],
        [
            Each(xbc), Each(dt_raw), *small, Each(dy), Each(dxw0), Each(db0), Each(dc0), Each(dcum0),
            Each(entering), Each(leaving),
        ],
        2 * rows * width * STATE * 20,
        "back_state",
        grid=seqs,
    )
    edge = passed_along(d_xbc[:, :FRONT], "seq", -1)
    part, dx, d_bc, g_gain_one = call(
        k_back_in,
        [
            both(piece, model, dtype=BF16),
            both(piece, width + LANES, dtype=BF16),
            both(piece, bc, dtype=BF16),
            both(8, model),
        ],
        [Each(dn0), Each(d_xbc), Each(edge), Each(d_dt), Each(tok_front), in_x, in_bc, in_dt],
        2 * rows * (width + bc + LANES) * model,
        "back_in",
        grid=seqs,
    )
    arrived = shares_of_mp(part.reshape(rows, model))
    d_bc = all_sum(d_bc.reshape(rows, bc), ("mp",))
    dx_got = gather(dx.reshape(rows, width + LANES))
    bc_got = gather(d_bc)
    [dtok_own] = call(
        k_rows_three, [struct((share, model), BF16)], [arrived, tok_own, d_residual, norm_gains], 0, "rows_three"
    )
    d_tokens = jnp.transpose(gather_mp(dtok_own).reshape(seqs, piece, model), (1, 0, 2)).astype(F32)

    g_in_z = g_in_x = g_in_bc = 0.0
    for at in range(0, n_seq, 8):
        now = n_got.part(at, at + 8)
        [a] = outer(now, [dz_got.part(at, at + 8)], "weights_z")
        b, c = outer(now, [dx_got.part(at, at + 8), bc_got.part(at, at + 8)], "weights_x")
        g_in_z, g_in_x, g_in_bc = g_in_z + a, g_in_x + b, g_in_bc + c

    g_conv = jnp.sum(g_conv, axis=0)
    g_gn, g_hp = jnp.sum(g_gn, axis=0)[:1], jnp.sum(g_hp, axis=0)[:3]
    rest = model - width - LANES
    along = jnp.concatenate(
        [
            jnp.concatenate([g_conv[: KCONV + 1, :width], g_gn, jnp.zeros((2, width), F32)], axis=0),
            jnp.pad(g_hp, ((0, 5), (0, rest))),
        ],
        axis=1,
    )
    every = jnp.concatenate(
        [
            jnp.pad(g_conv[: KCONV + 1, width:], ((0, 0), (0, model - bc))),
            jnp.sum(g_gain_one, axis=0)[:1],
            g_gain_two[:2],
            g_router,
        ],
        axis=0,
    )
    summed = all_sum(jnp.concatenate([along, every], axis=0), ("seq",))
    every = all_sum(summed[8:], ("mp",))
    return (
        output,
        d_tokens,
        every[5:7],
        g_in_z,
        g_in_x[:, :width],
        g_in_bc,
        g_in_x[:, width : width + heads],
        summed[: KCONV + 1, :width],
        every[: KCONV + 1, :bc],
        summed[:3, width : width + heads],
        summed[KCONV + 1, :width],
        g_out_w,
        every[8:].T,
        g_shared_in,
        g_shared_down,
        g_expert_in[None],
        g_expert_down[None],
    )


def solution(mesh):
    in_specs = (
        P("seq", None, None),
        P(),
        P("seq", None, None),
        P(),
        P(None, "mp"),
        P(None, "mp"),
        P(),
        P(None, "mp"),
        P(None, "mp"),
        P(),
        P(None, "mp"),
        P("mp"),
        P("mp", None),
        P(),
        P(None, None, "mp"),
        P("mp", None),
        P(("seq", "mp"), None, None, None),
        P(("seq", "mp"), None, None),
        P("seq", None, None),
    )
    out_specs = (
        P("seq", None, None),
        P("seq", None, None),
        P(),
        P(None, "mp"),
        P(None, "mp"),
        P(),
        P(None, "mp"),
        P(None, "mp"),
        P(),
        P(None, "mp"),
        P("mp"),
        P("mp", None),
        P(),
        P(None, None, "mp"),
        P("mp", None),
        P(("seq", "mp"), None, None, None),
        P(("seq", "mp"), None, None),
    )
    return jax.shard_map(body, mesh=mesh, in_specs=in_specs, out_specs=out_specs, check_vma=False)
```

time: 918 us -> 579 us (0.63)
  waiting for transfers between devices: 441 us -> 147 us
  Pallas kernels: 0 us -> 195 us
  matrix products: 129 us -> 2.21 us
  other arithmetic: 113 us -> 10.4 us
  local copies, waits for them, and re-layouts: 140 us -> 53.1 us
  starting transfers between devices: 24.2 us -> 73.4 us
  blocking collectives: 42.9 us -> 75 us
    psum x5 -> x1, waiting for transfers between devices: 298 us -> 18.4 us  [body(): g_out_w = lax.psum(g_out_w.astype(BF16), 'seq').astype(F32)]
    pallas_call x0 -> x30, Pallas kernels: none -> 195 us  [the longest x28 169 us: call(): pl.pallas_call(kernel, out_shape=shapes, grid_spec=grid_spec, compiler_pa...]
    dot_general x49 -> x1, matrix products: 129 us -> 2.21 us  [body(): lax.dot_general(normed_y.reshape(rows, width), dm.reshape(rows, model + L...]
    ppermute x0 -> x74, waiting for transfers between devices: none -> 93.9 us  [flip(): lax.ppermute(array, axis, [(i, i ^ bit) for i in range(lax.axis_size(axis...]
    all_to_all x4, waiting for transfers between devices: 128 us -> 34.9 us  [shares_of_mp(): return lax.all_to_all(cut, 'mp', 0, 0, tiled=True)]
    all_gather x1 -> x4, blocking collectives: 9.39 us -> 75 us  [gather_mp(): return lax.all_gather(array, 'mp', tiled=True)]
    gather x7 -> x0, local copies, waits for them, and re-layouts: 61.5 us -> none  [the longest x2 21.6 us: expert_forward(): route_vals = returned.reshape(-1, model_width)[positions]]
    ppermute x0 -> x74, starting transfers between devices: none -> 52.5 us  [flip(): lax.ppermute(array, axis, [(i, i ^ bit) for i in range(lax.axis_size(axis...]
  transfers between devices with their start and end apart: 13 -> 82, of which waited for: 11 -> 23; matrix products, arithmetic and copies ran while one was open for 22% -> 8% of each run, Pallas kernels for 0% -> 32%
where the time goes in v1:
time: 579 us; the launch traced here: 571 us
  Pallas kernels  195 us (34%)
  waiting for transfers between devices  147 us (25%)
  blocking collectives  75 us (13%)
  starting transfers between devices  73.4 us (13%)
  local copies, waits for them, and re-layouts  53.1 us (9%)
  between operations  15.1 us (3%)
  other arithmetic  10.4 us (2%)
    pallas_call x28, Pallas kernels, call(): pl.pallas_call(kernel, out_shape=shapes, grid_spec=grid_spec, compiler_pa...  169 us
    ppermute x74, waiting for transfers between devices, flip(): lax.ppermute(array, axis, [(i, i ^ bit) for i in range(lax.axis_size(axis...  93.9 us
    all_gather x4, blocking collectives, gather_mp(): return lax.all_gather(array, 'mp', tiled=True)  75 us
    ppermute x74, starting transfers between devices, flip(): lax.ppermute(array, axis, [(i, i ^ bit) for i in range(lax.axis_size(axis...  52.5 us
    all_to_all x4, waiting for transfers between devices, shares_of_mp(): return lax.all_to_all(cut, 'mp', 0, 0, tiled=True)  34.9 us
    pallas_call x2, Pallas kernels, outer(): pl.pallas_call(functools.partial(k_outer, a.slots, bs[0].slots, len(bs)),...  25.7 us
    unnamed x131, local copies, waits for them, and re-layouts  21.4 us
    psum x1, waiting for transfers between devices, body(): g_out_w = lax.psum(g_out_w.astype(BF16), 'seq').astype(F32)  18.4 us
  transfers between devices with their start and end apart: 82, of which 23 were waited for; matrix products, arithmetic and copies ran while one was open for 8% of the time, Pallas kernels for 32%

profile of v1, /device:TPU:0, one launch (start us, length us, event | category | flops | bytes accessed | tf_op | source)
XLA Modules:
  0.0 571.1 jit_solution(9988544194927973555)
XLA Ops:
  15.4 7.5 %mixer_in.1 = (bf16[2,128,1536]{2,1,0:T(8,128)(2,1)}, f32[2,128,768]{2,1,0:T(8,128)}, bf16[2,144,1024]{2,1,0:T(8,128)(2,1)}, f32[2,128,128]{2,1,0:T(8,128)}, bf1...) custom-call(bf16[2,144,1536]{2,1,0:T(8,128)(2,1)} %fusion.1.tok, f32[2,1536]{1,0:T(2,128)} %gains.7, ...), custom_call_target="tpu_custom_call" | custom-call | flops 1509949440 | bytes 9162908 | tf_op jit(solution)/shard_map/mixer_in/pallas_call | solution.py:72
  32.8 17.2 %collective-permute-done.2.recv = bf16[2,784,128]{2,1,0:T(8,128)(2,1)S(1)} collective-permute-done((bf16[2,784,128]{2,1,0:T(8,128)(2,1)}, bf16[2,784,128]{2,1,0:T(8,128)(2,1)S(1)}, u32[]{:S(2)}, u32[]{:S(2)}) %collective-permute-start.2) | collective-permute-done | bytes 401440 | tf_op jit(solution)/shard_map/ppermute | solution.py:598
  60.1 9.5 %collective-permute-done.3.recv = bf16[2,784,128]{2,1,0:T(8,128)(2,1)S(1)} collective-permute-done((bf16[2,784,128]{2,1,0:T(8,128)(2,1)}, bf16[2,784,128]{2,1,0:T(8,128)(2,1)S(1)}, u32[]{:S(2)}, u32[]{:S(2)}) %collective-permute-start.3) | collective-permute-done | bytes 401440 | tf_op jit(solution)/shard_map/ppermute | solution.py:598
  83.4 15.8 %all-to-all-done.arrived = bf16[4,64,1664]{2,1,0:T(8,128)(2,1)S(1)} async-done(((bf16[4,64,1664]{2,1,0:T(8,128)(2,1)}), bf16[4,64,1664]{2,1,0:T(8,128)(2,1)S(1)}, u32[]{:S(2)}, u32[]{:S(2)}) %all-to-all-start) | async-done | bytes 852000 | tf_op jit(solution)/shard_map/all_to_all | solution.py:734
  102.5 16.2 %all_gather.15.refs_3_.x.refs_2_ = bf16[256,1536]{1,0:T(8,128)(2,1)S(1)} all-gather(bf16[64,1536]{1,0:T(8,128)(2,1)} %get-tuple-element.140.two), channel_id=1, replica_groups=mesh['seq'=8,'mp'=4] {'mp'}, dimensions={0}, use_global_device_ids=true | all-gather | bytes 983040 | tf_op jit(solution)/shard_map/all_gather | solution.py:738
  122.9 8.2 %collective-permute-done.6.refs_3_.refs_4_ = bf16[256,1536]{1,0:T(8,128)(2,1)S(1)} collective-permute-done((bf16[256,1536]{1,0:T(8,128)(2,1)S(1)}, bf16[256,1536]{1,0:T(8,128)(2,1)S(1)}, u32[]{:S(2)}, u32[]{:S(2)}) %collective-permute-start.6) | collective-permute-done | bytes 786464 | tf_op jit(solution)/shard_map/ppermute | solution.py:598
  140.5 5.5 collective-permute-done.12.refs_3_.refs_8_
  149.2 12.4 %experts.4 = (bf16[256,1536]{1,0:T(8,128)(2,1)}, bf16[256,1664]{1,0:T(8,128)(2,1)}, bf16[256,768]{1,0:T(8,128)(2,1)}, bf16[256,1536]{1,0:T(8,128)(2,1)}, bf16[25...) custom-call(s32[5]{0:T(128)} %concatenate.34.index, ...), custom_call_target="tpu_custom_call" | custom-call | flops 5234491392 | bytes 17088512 | tf_op jit(solution)/shard_map/experts/pallas_call | solution.py:72
  162.3 7.6 %experts.5 = (bf16[256,1536]{1,0:T(8,128)(2,1)}, bf16[256,1664]{1,0:T(8,128)(2,1)}, bf16[256,768]{1,0:T(8,128)(2,1)}, bf16[256,1536]{1,0:T(8,128)(2,1)}, bf16[25...) custom-call(s32[5]{0:T(128)} %concatenate.35.index, bf16[1536,16]{1,0:T(8,128)(2,1)} %copy.55.refs_0_.router, ...), custom_call_target="tpu_custom_call" | custom-call | flops 2617245696 | bytes 9748480 | tf_op jit(solution)/shard_map/experts/pallas_call | solution.py:72
  180.3 21.9 %experts.3 = (bf16[256,1536]{1,0:T(8,128)(2,1)}, bf16[256,1664]{1,0:T(8,128)(2,1)}, bf16[256,768]{1,0:T(8,128)(2,1)}, bf16[256,1536]{1,0:T(8,128)(2,1)}, bf16[25...) custom-call(s32[3]{0:T(128)} %pad_add_fusion.index, bf16[1536,16]{1,0:T(8,128)(2,1)} %copy.55.refs_0_.router, ...), custom_call_target="tpu_custom_call" | custom-call | flops 2617245696 | bytes 9748480 | tf_op jit(solution)/shard_map/experts/pallas_call | solution.py:72
  230.7 19.2 %all-to-all-done.2.arrived = bf16[4,64,1664]{2,1,0:T(8,128)(2,1)S(1)} async-done(((bf16[4,64,1664]{2,1,0:T(8,128)(2,1)}), bf16[4,64,1664]{2,1,0:T(8,128)(2,1)S(1)}, u32[]{:S(2)}, u32[]{:S(2)}) %all-to-all-start.2) | async-done | bytes 852000 | tf_op jit(solution)/shard_map/all_to_all | solution.py:734
  254.2 19.4 %all_gather.18 = bf16[256,1664]{1,0:T(8,128)(2,1)} all-gather(bf16[64,1664]{1,0:T(8,128)(2,1)} %get-tuple-element.175), channel_id=1, replica_groups=mesh['seq'=8,'mp'=4] {'mp'}, dimensions={0}, use_global_device_ids=true | all-gather | bytes 1064960 | tf_op jit(solution)/shard_map/all_gather | solution.py:738
  273.6 5.6 back_gate.1
  302.0 11.8 %collective-permute-done.39.refs_3_ = bf16[256,1536]{1,0:T(8,128)(2,1)} collective-permute-done((bf16[256,1536]{1,0:T(8,128)(2,1)}, bf16[256,1536]{1,0:T(8,128)(2,1)}, u32[]{:S(2)}, u32[]{:S(2)}) %collective-permute-start.39) | collective-permute-done | bytes 786464 | tf_op jit(solution)/shard_map/ppermute | solution.py:598
  315.8 7.1 %back_intra.1 = (f32[2,128,768]{2,1,0:T(8,128)}, f32[2,128,128]{2,1,0:T(8,128)}, f32[2,128,128]{2,1,0:T(8,128)}, f32[2,128,128]{2,1,0:T(8,128)}, f32[2,128,1536]{2,1,0:T(8,128)}) custom-call(bf16[2,144,1024]{2,1,0:T(8,128)(2,1)} %get-tuple-element.121.xbc, f32[2,128,128]{2,1,0:T(8,128)} %get-tuple-element.122.dt, f32[5,768]{1,0:T(8,128)} %conv_x.7, ...), custom_call_target="tpu_custom_call" | custom-call | flops 805306368 | bytes 7032988 | tf_op jit(solution)/shard_map/back_intra/pallas_call | solution.py:72
  325.5 13.1 %back_state.1 = (f32[2,144,1024]{2,1,0:T(8,128)}, bf16[2,128,128]{2,1,0:T(8,128)(2,1)}, f32[2,8,1024]{2,1,0:T(8,128)}, f32[2,8,128]{2,1,0:T(8,128)}) custom-call(bf16[2,144,1024]{2,1,0:T(8,128)(2,1)} %get-tuple-element.121.xbc, f32[2,128,128]{2,1,0:T(8,128)} %get-tuple-element.122.dt, f32[5,768]{1,0:T(8,128)} %conv_x.7, f32[5,256]{1,0:T(8,128)} %conv_bc.7, ...), custom_call_target="tpu_custom_call" | custom-call | flops 1006632960 | bytes 5599388 | tf_op jit(solution)/shard_map/back_state/pallas_call | solution.py:72
  350.3 6.1 %back_in.1 = (bf16[2,128,1536]{2,1,0:T(8,128)(2,1)}, bf16[2,128,896]{2,1,0:T(8,128)(2,1)}, bf16[2,128,256]{2,1,0:T(8,128)(2,1)}, f32[2,8,1536]{2,1,0:T(8,128)}) custom-call(f32[2,128,1536]{2,1,0:T(8,128)} %get-tuple-element.180.dn0, f32[2,144,1024]{2,1,0:T(8,128)} %get-tuple-element.196.dxbc, f32[2,16,1024]{2,1,0:T(8,128)} %copy-done.36, ...), custom_call_target="tpu_custom_call" | custom-call | flops 905969664 | bytes 8491008 | tf_op jit(solution)/shard_map/back_in/pallas_call | solution.py:72
  376.6 7.7 %collective-permute-done.48.refs_13_ = bf16[256,768]{1,0:T(8,128)(2,1)} collective-permute-done((bf16[256,768]{1,0:T(8,128)(2,1)S(1)}, bf16[256,768]{1,0:T(8,128)(2,1)}, u32[]{:S(2)}, u32[]{:S(2)}) %collective-permute-start.48) | collective-permute-done | bytes 393248 | tf_op jit(solution)/shard_map/ppermute | solution.py:598
  403.2 25.2 %expert_weights.1 = (f32[2,1536,256]{2,1,0:T(8,128)}, f32[256,1536]{1,0:T(8,128)}, f32[2,1536,256]{2,1,0:T(8,128)}, f32[256,1536]{1,0:T(8,128)}) custom-call(s32[8]{0:T(128)} %stack.44.refs_0_.index, bf16[2,1536,256]{2,1,0:T(8,128)(2,1)} %refs_0_.4, bf16[256,1536]{1,0:T(8,128)(2,1)} %refs_1_.7, bf16[256,1536]{1,0:T(8,128)(2,1)} %copy-done.1, ...), custom_call_target="tpu_custom_call" | custom-call | flops 14495514624 | bytes 28049408 | tf_op jit(solution)/shard_map/expert_weights/pallas_call | solution.py:72
  441.0 19.2 %all_gather.17 = bf16[256,1536]{1,0:T(8,128)(2,1)S(1)} all-gather(bf16[64,1536]{1,0:T(8,128)(2,1)S(1)} %copy-done.24), channel_id=1, replica_groups=mesh['seq'=8,'mp'=4] {'mp'}, dimensions={0}, use_global_device_ids=true | all-gather | bytes 983040 | tf_op jit(solution)/shard_map/all_gather | solution.py:738
  471.3 11.3 %weights_z.1 = f32[1536,768]{1,0:T(8,128)} custom-call(s32[8]{0:T(128)} %stack.44.refs_0_.index, bf16[256,1536]{1,0:T(8,128)(2,1)} %bitcast.76, bf16[256,1536]{1,0:T(8,128)(2,1)} %collective-permute-done.38.refs_2_, bf16[256,1536]{1,0:T(8,128)(2,1)} %collective-permute-done.39.refs_3_, bf16[256,1536]{1,0:T(8,128)(2,1)} %collective-permute-done.40.refs_4_, ...), custom_call_target="tpu_custom_call" | custom-call | flops 4831838208 | bytes 14155776 | tf_op jit(solution)/shard_map/weights_z/pallas_call | solution.py:585
  482.6 18.4 %all-reduce.5.cloned.1.call-done = bf16[768,1536]{1,0:T(8,128)(2,1)} async-done(((bf16[768,1536]{1,0:T(8,128)(2,1)}), bf16[768,1536]{1,0:T(8,128)(2,1)}) %all-reduce.5.cloned.1.call-update) | async-done | bytes 2359312 | tf_op jit(solution)/shard_map/psum | solution.py:924
  517.4 14.4 %weights_x.1 = (f32[1536,896]{1,0:T(8,128)}, f32[1536,256]{1,0:T(8,128)}) custom-call(s32[8]{0:T(128)} %stack.44.refs_0_.index, bf16[256,1536]{1,0:T(8,128)(2,1)} %bitcast.77, bf16[256,1536]{1,0:T(8,128)(2,1)} %collective-permute-done.38.refs_2_, bf16[256,1536]{1,0:T(8,128)(2,1)} %collective-permute-done.39.refs_3_, ...), custom_call_target="tpu_custom_call" | custom-call | flops 7247757312 | bytes 18087936 | tf_op jit(solution)/shard_map/weights_x/pallas_call | solution.py:585
  541.9 20.2 %all_gather.19 = bf16[256,1536]{1,0:T(8,128)(2,1)S(1)} all-gather(bf16[64,1536]{1,0:T(8,128)(2,1)} %rows_three.1), channel_id=1, replica_groups=mesh['seq'=8,'mp'=4] {'mp'}, dimensions={0}, use_global_device_ids=true | all-gather | bytes 983040 | tf_op jit(solution)/shard_map/all_gather | solution.py:738
  (366 shorter events, 235.6 us)
Async XLA Ops:
  7.2 141.2 %all-gather.2.cloned.1.call-start = ((), (), s32[]{:S(2)}) async-start(), calls=%async_computation.4 | async-start | bytes 7667712 | tf_op jit(solution)/shard_map/all_gather | solution.py:800
  230.2 55.0 %collective-permute-start.10 = (bf16[256,1536]{1,0:T(8,128)(2,1)}, bf16[256,1536]{1,0:T(8,128)(2,1)S(1)}, u32[]{:S(2)}, u32[]{:S(2)}) collective-permute-start(bf16[256,1536]{1,0:T(8,128)(2,1)} %get-tuple-element.146), channel_id=1, source_target_pairs={{0,4},{4,0},{8,12},{12,8},{16,20},{20,16},{24,28},{28,24},{1,5},{5... | collective-permute-start | bytes 2359304 | tf_op jit(solution)/shard_map/ppermute | solution.py:598
  230.2 56.3 %collective-permute-start.11 = (bf16[256,1536]{1,0:T(8,128)(2,1)}, bf16[256,1536]{1,0:T(8,128)(2,1)S(1)}, u32[]{:S(2)}, u32[]{:S(2)}) collective-permute-start(bf16[256,1536]{1,0:T(8,128)(2,1)} %get-tuple-element.148), channel_id=1, source_target_pairs={{0,4},{4,0},{8,12},{12,8},{16,20},{20,16},{24,28},{28,24},{1,5},{5... | collective-permute-start | bytes 2359304 | tf_op jit(solution)/shard_map/ppermute | solution.py:598
  230.7 57.6 %collective-permute-start.16 = (bf16[256,1536]{1,0:T(8,128)(2,1)}, bf16[256,1536]{1,0:T(8,128)(2,1)S(1)}, u32[]{:S(2)}, u32[]{:S(2)}) collective-permute-start(bf16[256,1536]{1,0:T(8,128)(2,1)} %get-tuple-element.150), channel_id=1, source_target_pairs={{0,4},{4,0},{8,12},{12,8},{16,20},{20,16},{24,28},{28,24},{1,5},{5... | collective-permute-start | bytes 2359304 | tf_op jit(solution)/shard_map/ppermute | solution.py:598
  286.5 53.0 %collective-permute-start.41 = (bf16[256,1536]{1,0:T(8,128)(2,1)}, bf16[256,1536]{1,0:T(8,128)(2,1)}, u32[]{:S(2)}, u32[]{:S(2)}) collective-permute-start(bf16[256,1536]{1,0:T(8,128)(2,1)} %bitcast.75), channel_id=1, source_target_pairs={{0,16},{4,20},{8,24},{12,28},{16,0},{20,4},{24,8},{28,12},{1,17},{... | collective-permute-start | bytes 2359304 | tf_op jit(solution)/shard_map/ppermute | solution.py:598
  293.0 48.9 %collective-permute-start.17 = (bf16[256,1536]{1,0:T(8,128)(2,1)}, bf16[256,1536]{1,0:T(8,128)(2,1)S(1)}, u32[]{:S(2)}, u32[]{:S(2)}) collective-permute-start(bf16[256,1536]{1,0:T(8,128)(2,1)} %get-tuple-element.151), channel_id=1, source_target_pairs={{0,8},{4,12},{8,0},{12,4},{16,24},{20,28},{24,16},{28,20},{1,9},{5... | collective-permute-start | bytes 2359304 | tf_op jit(solution)/shard_map/ppermute | solution.py:598
  301.7 58.3 %collective-permute-start.18 = (bf16[256,1536]{1,0:T(8,128)(2,1)}, bf16[256,1536]{1,0:T(8,128)(2,1)S(1)}, u32[]{:S(2)}, u32[]{:S(2)}) collective-permute-start(bf16[256,1536]{1,0:T(8,128)(2,1)} %get-tuple-element.152), channel_id=1, source_target_pairs={{0,16},{4,20},{8,24},{12,28},{16,0},{20,4},{24,8},{28,12},{1,17},{... | collective-permute-start | bytes 2359304 | tf_op jit(solution)/shard_map/ppermute | solution.py:598
  313.8 50.2 %collective-permute-start.40 = (bf16[256,1536]{1,0:T(8,128)(2,1)}, bf16[256,1536]{1,0:T(8,128)(2,1)}, u32[]{:S(2)}, u32[]{:S(2)}) collective-permute-start(bf16[256,1536]{1,0:T(8,128)(2,1)} %collective-permute-done.39.refs_3_), channel_id=1, source_target_pairs={{0,4},{4,0},{8,12},{12,8},{16,20},{20,16},{24,28},{28,24},{1,5},{5... | collective-permute-start | bytes 2359304 | tf_op jit(solution)/shard_map/ppermute | solution.py:598
  315.8 48.3 %collective-permute-start.5 = (bf16[256,1536]{1,0:T(8,128)(2,1)}, bf16[256,1536]{1,0:T(8,128)(2,1)S(1)}, u32[]{:S(2)}, u32[]{:S(2)}) collective-permute-start(bf16[256,1536]{1,0:T(8,128)(2,1)} %get-tuple-element.143), channel_id=1, source_target_pairs={{0,4},{4,0},{8,12},{12,8},{16,20},{20,16},{24,28},{28,24},{1,5},{5... | collective-permute-start | bytes 2359304 | tf_op jit(solution)/shard_map/ppermute | solution.py:598
  364.0 33.4 %collective-permute-start.42 = (bf16[256,1536]{1,0:T(8,128)(2,1)}, bf16[256,1536]{1,0:T(8,128)(2,1)}, u32[]{:S(2)}, u32[]{:S(2)}) collective-permute-start(bf16[256,1536]{1,0:T(8,128)(2,1)} %collective-permute-done.41.refs_5_), channel_id=1, source_target_pairs={{0,4},{4,0},{8,12},{12,8},{16,20},{20,16},{24,28},{28,24},{1,5},{5... | collective-permute-start | bytes 2359304 | tf_op jit(solution)/shard_map/ppermute | solution.py:598
  392.3 36.1 %all-to-all-start.1 = ((bf16[4,64,1536]{2,1,0:T(8,128)(2,1)}), bf16[4,64,1536]{2,1,0:T(8,128)(2,1)S(1)}, u32[]{:S(2)}, u32[]{:S(2)}) async-start(bf16[4,64,1536]{2,1,0:T(8,128)(2,1)} %bitcast.60), calls=%async_computation.1 | async-start | bytes 1572864 | tf_op jit(solution)/shard_map/all_to_all | solution.py:734
  395.8 105.2 %all-reduce.5.cloned.1.call-start = ((), (), s32[]{:S(2)}) async-start(), calls=%async_computation.5 | async-start | bytes 4718592 | tf_op jit(solution)/shard_map/psum | solution.py:924
  397.3 34.9 %collective-permute-start.52 = (bf16[128,768]{1,0:T(8,128)(2,1)S(1)}, bf16[128,768]{1,0:T(8,128)(2,1)}, u32[]{:S(2)}, u32[]{:S(2)}) collective-permute-start(bf16[128,768]{1,0:T(8,128)(2,1)S(1)} %slice.142), channel_id=1, source_target_pairs={{0,16},{4,20},{8,24},{12,28},{16,0},{20,4},{24,8},{28,12},{1,17},{... | collective-permute-start | bytes 589832 | tf_op jit(solution)/shard_map/ppermute | solution.py:598
  399.1 39.6 %collective-permute-start.57 = (bf16[256,896]{1,0:T(8,128)(2,1)}, bf16[256,896]{1,0:T(8,128)(2,1)S(1)}, u32[]{:S(2)}, u32[]{:S(2)}) collective-permute-start(bf16[256,896]{1,0:T(8,128)(2,1)} %bitcast.32.refs_11_), channel_id=1, source_target_pairs={{0,8},{4,12},{8,0},{12,4},{16,24},{20,28},{24,16},{28,20},{1,9},{5... | collective-permute-start | bytes 1376264 | tf_op jit(solution)/shard_map/ppermute | solution.py:598
  399.6 39.5 %collective-permute-start.59 = (bf16[256,896]{1,0:T(8,128)(2,1)}, bf16[256,896]{1,0:T(8,128)(2,1)}, u32[]{:S(2)}, u32[]{:S(2)}) collective-permute-start(bf16[256,896]{1,0:T(8,128)(2,1)} %bitcast.32.refs_11_), channel_id=1, source_target_pairs={{0,16},{4,20},{8,24},{12,28},{16,0},{20,4},{24,8},{28,12},{1,17},{... | collective-permute-start | bytes 1376264 | tf_op jit(solution)/shard_map/ppermute | solution.py:598
  399.9 32.9 %collective-permute-start.68 = (bf16[256,256]{1,0:T(8,128)(2,1)S(1)}, bf16[256,256]{1,0:T(8,128)(2,1)}, u32[]{:S(2)}, u32[]{:S(2)}) collective-permute-start(bf16[256,256]{1,0:T(8,128)(2,1)S(1)} %add.53.refs_21_), channel_id=1, source_target_pairs={{0,8},{4,12},{8,0},{12,4},{16,24},{20,28},{24,16},{28,20},{1,9},{5... | collective-permute-start | bytes 393224 | tf_op jit(solution)/shard_map/ppermute | solution.py:598
  401.5 31.3 %collective-permute-start.35 = (f32[32,1536]{1,0:T(8,128)S(1)}, f32[32,1536]{1,0:T(8,128)S(1)}, u32[]{:S(2)}, u32[]{:S(2)}) collective-permute-start(f32[32,1536]{1,0:T(8,128)S(1)} %add.48), channel_id=1, source_target_pairs={{0,16},{4,20},{8,24},{12,28},{16,0},{20,4},{24,8},{28,12},{1,17},{... | collective-permute-start | bytes 589832 | tf_op jit(solution)/shard_map/ppermute | solution.py:598
  432.8 31.0 %collective-permute-start.49 = (bf16[256,768]{1,0:T(8,128)(2,1)}, bf16[256,768]{1,0:T(8,128)(2,1)S(1)}, u32[]{:S(2)}, u32[]{:S(2)}) collective-permute-start(bf16[256,768]{1,0:T(8,128)(2,1)} %collective-permute-done.48.refs_13_), channel_id=1, source_target_pairs={{0,4},{4,0},{8,12},{12,8},{16,20},{20,16},{24,28},{28,24},{1,5},{5... | collective-permute-start | bytes 1179656 | tf_op jit(solution)/shard_map/ppermute | solution.py:598
  465.8 46.8 %collective-permute-start.69 = (bf16[256,256]{1,0:T(8,128)(2,1)}, bf16[256,256]{1,0:T(8,128)(2,1)}, u32[]{:S(2)}, u32[]{:S(2)}) collective-permute-start(bf16[256,256]{1,0:T(8,128)(2,1)} %collective-permute-done.68.refs_23_), channel_id=1, source_target_pairs={{0,4},{4,0},{8,12},{12,8},{16,20},{20,16},{24,28},{28,24},{1,5},{5... | collective-permute-start | bytes 393224 | tf_op jit(solution)/shard_map/ppermute | solution.py:598
  466.2 46.9 %collective-permute-start.61 = (bf16[128,896]{1,0:T(8,128)(2,1)S(1)}, bf16[128,896]{1,0:T(8,128)(2,1)S(1)}, u32[]{:S(2)}, u32[]{:S(2)}) collective-permute-start(bf16[128,896]{1,0:T(8,128)(2,1)S(1)} %slice.144), channel_id=1, source_target_pairs={{0,16},{4,20},{8,24},{12,28},{16,0},{20,4},{24,8},{28,12},{1,17},{... | collective-permute-start | bytes 688136 | tf_op jit(solution)/shard_map/ppermute | solution.py:598
  467.9 45.3 %collective-permute-start.62 = (bf16[128,896]{1,0:T(8,128)(2,1)S(1)}, bf16[128,896]{1,0:T(8,128)(2,1)S(1)}, u32[]{:S(2)}, u32[]{:S(2)}) collective-permute-start(bf16[128,896]{1,0:T(8,128)(2,1)S(1)} %slice.145), channel_id=1, source_target_pairs={{0,8},{4,12},{8,0},{12,4},{16,24},{20,28},{24,16},{28,20},{1,9},{5... | collective-permute-start | bytes 688136 | tf_op jit(solution)/shard_map/ppermute | solution.py:598
  469.2 40.9 %collective-permute-start.75 = (bf16[128,256]{1,0:T(8,128)(2,1)S(1)}, bf16[128,256]{1,0:T(8,128)(2,1)S(1)}, u32[]{:S(2)}, u32[]{:S(2)}) collective-permute-start(bf16[128,256]{1,0:T(8,128)(2,1)S(1)} %collective-permute-done.73.refs_28_), channel_id=1, source_target_pairs={{0,4},{4,0},{8,12},{12,8},{16,20},{20,16},{24,28},{28,24},{1,5},{5... | collective-permute-start | bytes 196616 | tf_op jit(solution)/shard_map/ppermute | solution.py:598
  469.8 40.9 %collective-permute-start.37 = (f32[24,1536]{1,0:T(8,128)S(1)}, f32[24,1536]{1,0:T(8,128)S(1)}, u32[]{:S(2)}, u32[]{:S(2)}) collective-permute-start(f32[24,1536]{1,0:T(8,128)S(1)} %slice_add_fusion), channel_id=1, source_target_pairs={{0,2},{1,3},{2,0},{3,1},{4,6},{5,7},{6,4},{7,5},{8,10},{9,11},{10,... | collective-permute-start | bytes 442376 | tf_op jit(solution)/shard_map/ppermute | solution.py:598
  505.5 33.2 %all-to-all-start.3 = ((bf16[4,64,1536]{2,1,0:T(8,128)(2,1)}), bf16[4,64,1536]{2,1,0:T(8,128)(2,1)S(1)}, u32[]{:S(2)}, u32[]{:S(2)}) async-start(bf16[4,64,1536]{2,1,0:T(8,128)(2,1)} %bitcast.27), calls=%async_computation.3 | async-start | bytes 1572864 | tf_op jit(solution)/shard_map/all_to_all | solution.py:734
  (121 other events, 1337.1 us)
Sparse Core Ops, SparseCore 0:
  24.0 59.7 all-gather.1
  435.5 65.4 all-reduce.4

commit v2 on v1

v2 whole, which is shorter than its diff:
```python
import functools

import jax
import jax.numpy as jnp
from jax import lax
from jax.experimental import pallas as pl
from jax.experimental.pallas import tpu as pltpu
from jax.sharding import PartitionSpec as P

HEAD_DIM = 64
STATE = 128
KCONV = 4
INNER = 3072
LANES = 128
SMALL = 16
FRONT = 16
EPSILON = 1e-05
F32 = jnp.float32
BF16 = jnp.bfloat16
HIGHEST = lax.Precision.HIGHEST
NN = (((1,), (0,)), ((), ()))
NT = (((1,), (1,)), ((), ()))
TN = (((0,), (0,)), ((), ()))


class Each:
    def __init__(self, array):
        self.array = array


class Scalars:
    def __init__(self, array):
        self.array = array


class Far:
    def __init__(self, array):
        self.array = array


class Rows:
    def __init__(self, array, rows):
        self.array, self.rows = array, rows


def struct(shape, dtype):
    return jax.ShapeDtypeStruct(tuple(shape), dtype)


def call(kernel, outs, args, flops, name, grid=1, index=None, scratch=(), aliases=None):
    def spec(a):
        if isinstance(a, Scalars):
            return pl.BlockSpec(memory_space=pltpu.SMEM)
        if isinstance(a, Far):
            return pl.BlockSpec(memory_space=pl.ANY)
        if isinstance(a, Rows):
            rest = a.array.shape[1:]
            return pl.BlockSpec((a.rows, *rest), lambda s, *_: (s,) + (0,) * len(rest))
        if isinstance(a, Each):
            rest = a.array.shape[1:]
            return pl.BlockSpec((None, *rest), lambda s, *_: (s,) + (0,) * len(rest))
        return pl.BlockSpec(a.shape, lambda s, *_: (0,) * len(a.shape))

    def plain(a):
        return a.array if isinstance(a, (Each, Scalars, Far, Rows)) else a

    arrays = [plain(a) for a in args]
    shapes = [plain(a) for a in outs]
    moved = sum(a.size * a.dtype.itemsize for a in (*arrays, *shapes))
    grid_spec = pltpu.PrefetchScalarGridSpec(
        num_scalar_prefetch=0 if index is None else 1,
        grid=(grid,),
        in_specs=[spec(a) for a in args],
        out_specs=[spec(a) for a in outs],
        scratch_shapes=list(scratch),
    )
    return pl.pallas_call(
        kernel,
        out_shape=shapes,
        grid_spec=grid_spec,
        input_output_aliases=aliases or {},
        compiler_params=pltpu.CompilerParams(vmem_limit_bytes=60 * 2**20),
        cost_estimate=pl.CostEstimate(flops=int(flops), bytes_accessed=int(moved), transcendentals=0),
        name=name,
    )(*([] if index is None else [index]), *arrays)


def dot(a, b, dims=NN):
    return lax.dot_general(a.astype(BF16), b.astype(BF16), dims, preferred_element_type=F32)


def exact(a, b, dims=NN):
    return lax.dot_general(a, b, dims, precision=HIGHEST, preferred_element_type=F32)


def sigmoid(v):
    return 1.0 / (1.0 + jnp.exp(-v))


def iota(shape, axis):
    return lax.broadcasted_iota(jnp.int32, shape, axis)


def two_terms(v):
    high = v.astype(BF16)
    return high, (v - high.astype(F32)).astype(BF16)


def to_lanes(v):
    return jnp.concatenate([v, jnp.zeros((v.shape[0], LANES - v.shape[1]), v.dtype)], axis=1)


def spread_matrix(width):
    return (iota((LANES, width), 1) // HEAD_DIM == iota((LANES, width), 0)).astype(F32)


def prepared(xbc, dt, conv_x, conv_bc, head_par, meta):
    rows = dt.shape[0]
    width = conv_x.shape[1]
    conv = jnp.concatenate([conv_x[...], conv_bc[...]], axis=1)
    hp = to_lanes(head_par[...])
    where = iota((rows, 1), 0) + meta[2]
    live = (where < meta[pl.program_id(0)]).astype(F32)
    xf = xbc[...].astype(F32)
    summed = conv[KCONV : KCONV + 1]
    taps = []
    for j in range(KCONV):
        shifted = xf[FRONT - (KCONV - 1) + j : FRONT - (KCONV - 1) + j + rows]
        taps.append(shifted)
        summed = summed + conv[j : j + 1] * shifted
    sig = sigmoid(summed)
    act = summed * sig
    xs = act[:, :width] * live
    b = act[:, width : width + STATE]
    c = act[:, width + STATE :]
    raw = dt[...] + hp[0:1]
    step = (jnp.maximum(raw, 0.0) + jnp.log1p(jnp.exp(-jnp.abs(raw)))) * live
    rate = -jnp.exp(hp[1:2])
    logd = rate * step
    lower = (iota((rows, rows), 0) >= iota((rows, rows), 1)).astype(F32)
    cum = exact(lower, logd)
    return dict(
        conv=conv, skip=hp[2:3], live=live, taps=taps, summed=summed, sig=sig, xs=xs, b=b, c=c, raw=raw,
        step=step, rate=rate, logd=logd, cum=cum,
    )


def pack_state(o_send, state, decay):
    size = state.shape[0]
    high, low = two_terms(decay)
    row = iota((FRONT, LANES), 0)
    more = jnp.where(row == 0, high.astype(F32), 0.0) + jnp.where(row == 1, low.astype(F32), 0.0)
    o_send[:size, :] = state.astype(BF16)
    o_send[size:, :] = more.astype(BF16)


def unpack_state(send):
    size = send.shape[0] - FRONT
    more = send[size:, :].astype(F32)
    return send[:size, :].astype(F32), more[0:1] + more[1:2]


def k_in(tok, gains, wz, wx, wbc, wdt, conv_x, conv_bc, head_par, meta, o_norm, o_z, o_xbc, o_dt, o_send, o_tot):
    width = wz.shape[1]
    x = tok[...].astype(F32)
    scale = lax.rsqrt(jnp.mean(x * x, axis=-1, keepdims=True) + EPSILON)
    normed = (x * scale * gains[0:1]).astype(BF16)
    own = normed[FRONT:]
    o_norm[...] = own
    o_xbc[:, :width] = dot(normed, wx[...]).astype(BF16)
    o_xbc[:, width:] = dot(normed, wbc[...]).astype(BF16)
    o_dt[...] = to_lanes(dot(own, wdt[...]))
    o_z[...] = dot(own, wz[...])
    p = prepared(o_xbc, o_dt, conv_x, conv_bc, head_par, meta)
    rows = own.shape[0]
    last = p["cum"][rows - 1 : rows]
    weight = exact(p["step"] * jnp.exp(last - p["cum"]), spread_matrix(width))
    decay = jnp.exp(last)
    pack_state(o_send, dot(p["xs"] * weight, p["b"], TN), decay)
    o_tot[...] = jnp.broadcast_to(decay, o_tot.shape)


def pair_masks(rows):
    low = iota((rows, LANES), 1) < HEAD_DIM
    return low, jnp.logical_not(low)


def decays(cum, cum_t, h, ahead):
    gap = cum[:, h : h + 1] - cum_t[h : h + 1, :]
    return jnp.where(ahead, jnp.exp(jnp.where(ahead, gap, 0.0)), 0.0)


def by_halves(v, low, high):
    return jnp.concatenate(
        [jnp.where(low, v, 0.0).astype(BF16), jnp.where(high, v, 0.0).astype(BF16)], axis=0
    )


def k_intra(xbc, dt, conv_x, conv_bc, head_par, meta, o_y, o_c, o_ecum):
    width = o_y.shape[1]
    p = prepared(xbc, dt, conv_x, conv_bc, head_par, meta)
    xs, cum = p["xs"], p["cum"]
    rows = cum.shape[0]
    spread = spread_matrix(width)
    ahead = iota((rows, rows), 0) >= iota((rows, rows), 1)
    cum_t = cum.T
    scores = dot(p["c"], p["b"], NT)
    spread_out = exact(
        jnp.concatenate([p["step"], jnp.exp(cum), jnp.broadcast_to(p["skip"], (8, LANES))], axis=0), spread
    )
    xw = xs * spread_out[:rows]
    skip = spread_out[2 * rows : 2 * rows + 1]
    low, high = pair_masks(rows)
    o_c[...] = p["c"].astype(BF16)
    o_ecum[...] = spread_out[rows : 2 * rows]
    for pair in range(width // LANES):
        cols = slice(pair * LANES, (pair + 1) * LANES)
        mats = [(decays(cum, cum_t, h, ahead) * scores).astype(BF16) for h in (2 * pair, 2 * pair + 1)]
        within = dot(jnp.concatenate(mats, axis=1), by_halves(xw[:, cols], low, high))
        o_y[:, cols] = within + skip[:, cols] * xs[:, cols]


def k_scan(first, last, after, recv, own, *refs):
    whole, total = unpack_state(own)
    state, decay = unpack_state(recv)
    size = state.shape[0]
    mine = iota((size, LANES), 1) == iota((size, LANES), 0) // HEAD_DIM

    def rows_of(d):
        return jnp.sum(jnp.where(mine, d, 0.0), axis=1, keepdims=True)

    is_after = after[0] == 1
    if first:
        outs = refs
        outs[0][...] = jnp.where(is_after, state, 0.0)
        new_reach = jnp.where(is_after, decay, 1.0)
    else:
        before, reach = refs[:2]
        outs = refs[2:]
        outs[0][...] = jnp.where(is_after, before[...] + rows_of(reach[0:1]) * state, before[...])
        new_reach = jnp.where(is_after, reach[0:1] * decay, reach[0:1])
    if last:
        return
    outs[1][...] = jnp.broadcast_to(new_reach, outs[1].shape)
    new_whole = jnp.where(is_after, whole + rows_of(total) * state, state + rows_of(decay) * whole)
    pack_state(outs[2], new_whole, total * decay)


def k_out(y0, c, ecum, entering, z, gain, w, o_y, o_u, o_part):
    model = w.shape[1]
    y = y0[...] + ecum[...] * dot(c[...], entering[...], NT)
    o_y[...] = y
    zv = z[...]
    gated = y * zv * sigmoid(zv)
    high, low = two_terms(jnp.sum(gated * gated, axis=-1, keepdims=True))
    o_u[...] = (gated * gain[...]).astype(BF16)
    o_part[:, :model] = dot(o_u[...], w[...]).astype(BF16)
    o_part[:, model:] = to_lanes(jnp.concatenate([high, low], axis=1))


def k_back_gate(dm, y, z, gain, w, c, ecum, total, o_dz, o_dy, o_send, o_gain):
    model = w.shape[1]
    more = dm[:, model:].astype(F32)
    stat = more[:, 0:1] + more[:, 1:2]
    scale = more[:, 2:3] + more[:, 3:4]
    dn = dot(dm[:, :model], w[...], NT)
    zv = z[...]
    sig = sigmoid(zv)
    silu = zv * sig
    yv = y[...]
    gated = yv * silu
    dgated = scale * gain[...] * dn - gated * (scale * scale * stat / INNER)
    o_dz[...] = (dgated * yv * sig * (1.0 + zv * (1.0 - sig))).astype(BF16)
    dy = dgated * silu
    o_dy[...] = dy
    o_gain[...] = jnp.broadcast_to(jnp.sum(dn * gated * scale, axis=0, keepdims=True), o_gain.shape)
    pack_state(o_send, dot(ecum[...] * dy, c[...], TN), total[0:1])


def k_back_intra(xbc, dt, conv_x, conv_bc, head_par, meta, dy, dz, wz, o_dxw, o_db, o_dc, o_dcum, o_dn):
    width = dy.shape[1]
    p = prepared(xbc, dt, conv_x, conv_bc, head_par, meta)
    cum = p["cum"]
    rows = cum.shape[0]
    o_dn[...] = dot(dz[...], wz[...], NT)
    ahead = iota((rows, rows), 0) >= iota((rows, rows), 1)
    cum_t = cum.T
    scores = dot(p["c"], p["b"], NT)
    xw = p["xs"] * exact(p["step"], spread_matrix(width))
    low, high = pair_masks(rows)
    lane = iota((rows, LANES), 1)
    sub = iota((LANES, rows), 0)
    dscores = jnp.zeros((rows, rows), F32)
    plus = jnp.zeros((rows, LANES), F32)
    minus = jnp.zeros((LANES, rows), F32)
    for pair in range(width // LANES):
        cols = slice(pair * LANES, (pair + 1) * LANES)
        dstack = by_halves(dy[:, cols], low, high)
        dmats = dot(dstack, xw[:, cols], NT)
        mats = []
        for i, h in enumerate((2 * pair, 2 * pair + 1)):
            decay = decays(cum, cum_t, h, ahead)
            mat = decay * scores
            dmat = dmats[i * rows : (i + 1) * rows]
            dscores = dscores + dmat * decay
            flow = dmat * mat
            plus = jnp.where(lane == h, jnp.sum(flow, axis=1, keepdims=True), plus)
            minus = jnp.where(sub == h, jnp.sum(flow, axis=0, keepdims=True), minus)
            mats.append(mat.astype(BF16))
        o_dxw[:, cols] = dot(jnp.concatenate(mats, axis=0), dstack, TN)
    o_dcum[...] = plus - minus.T
    o_dc[...] = dot(dscores, p["b"])
    o_db[...] = dot(dscores, p["c"], TN)


def k_back_state(
    xbc, dt, conv_x, conv_bc, head_par, meta, dy, dxw0, db0, dc0, dcum0, entering, leaving,
    o_dxbc, o_ddt, o_conv, o_hp,
):
    width = dy.shape[1]
    p = prepared(xbc, dt, conv_x, conv_bc, head_par, meta)
    xs, b, c, cum, step, rate, live = (p[k] for k in ("xs", "b", "c", "cum", "step", "rate", "live"))
    summed, sig, conv = p["summed"], p["sig"], p["conv"]
    rows = cum.shape[0]
    spread = spread_matrix(width)
    last = cum[rows - 1 : rows]
    spread_out = exact(
        jnp.concatenate(
            [step, jnp.exp(cum), jnp.exp(last - cum), jnp.broadcast_to(p["skip"], (8, LANES))], axis=0
        ),
        spread,
    )
    step_x, ecum_x, rem_x = (spread_out[i * rows : (i + 1) * rows] for i in range(3))
    skip_x = spread_out[3 * rows : 3 * rows + 1]
    dyv = dy[...]
    h0 = entering[...]
    h1 = leaving[...]
    xw = xs * step_x
    scaled_dy = ecum_x * dyv
    dc = dc0[...] + dot(scaled_dy, h0)
    from_state = scaled_dy * dot(c, h0, NT)
    to_state = rem_x * dot(b, h1, NT)
    dxw = dxw0[...] + to_state
    db = db0[...] + dot(xw * rem_x, h1)
    dtotal = jnp.sum(exact(spread, h1 * h0), axis=1, keepdims=True)
    sums = exact(jnp.concatenate([from_state, xw * to_state, dxw * xs, dyv * xs], axis=0), spread, NT)
    flow = sums[rows : 2 * rows]
    dlast = jnp.broadcast_to(dtotal, (LANES, LANES)).T[0:1] * jnp.exp(last) + jnp.sum(
        flow, axis=0, keepdims=True
    )
    dcum = dcum0[...] + sums[:rows] - flow
    dcum = dcum + jnp.where(iota((rows, LANES), 0) == rows - 1, dlast, 0.0)
    upper = (iota((rows, rows), 0) <= iota((rows, rows), 1)).astype(F32)
    dlogd = exact(upper, dcum)
    draw = (sums[2 * rows : 3 * rows] + dlogd * rate) * live * sigmoid(p["raw"])
    o_ddt[...] = draw.astype(BF16)
    row = iota((8, LANES), 0)
    o_hp[...] = (
        jnp.where(row == 0, jnp.sum(draw, axis=0, keepdims=True), 0.0)
        + jnp.where(row == 1, jnp.sum(dlogd * p["logd"], axis=0, keepdims=True), 0.0)
        + jnp.where(row == 2, jnp.sum(sums[3 * rows : 4 * rows], axis=0, keepdims=True), 0.0)
    )
    dx = (dxw * step_x + skip_x * dyv) * live
    dsummed = jnp.concatenate([dx, db, dc], axis=1) * sig * (1.0 + summed * (1.0 - sig))
    zeros = jnp.zeros((FRONT, dsummed.shape[1]), F32)
    padded = jnp.concatenate([zeros, dsummed, zeros], axis=0)
    total = rows + FRONT
    out = jnp.zeros((total, dsummed.shape[1]), F32)
    for j in range(KCONV):
        shift = KCONV - 1 - j
        out = out + conv[j : j + 1] * padded[shift : shift + total]
        o_conv[j : j + 1] = jnp.sum(dsummed * p["taps"][j], axis=0, keepdims=True)
    o_conv[KCONV : KCONV + 1] = jnp.sum(dsummed, axis=0, keepdims=True)
    o_conv[KCONV + 1 :] = jnp.zeros((o_conv.shape[0] - KCONV - 1, dsummed.shape[1]), F32)
    o_dxbc[...] = out


def beside_rows(experts, model):
    need = (experts + 2) * model // (2 * STATE) + KCONV + 1
    return -(-need // 64) * 64


def k_back_in(dn0, dxbc, edge, ddt, tok, g_conv, g_hp, g_gn, g_two, wx, wbc, wdt, o_dx, o_bc, o_part, gain):
    width = wx.shape[1]
    rows, model = dn0.shape
    experts = g_two.shape[0] - 8
    step = pl.program_id(0)
    tail = jnp.concatenate([jnp.zeros((rows - FRONT, edge.shape[1]), F32), edge[...]], axis=0)
    own = (dxbc[FRONT:, :] + tail).astype(BF16)
    dx, dbc = own[:, :width], own[:, width:]
    to = pl.ds(pl.multiple_of(step * rows, rows), rows)
    o_dx[to, :width] = dx
    o_dx[to, width:] = ddt[...]
    o_bc[to, :] = dbc
    dn = dn0[...] + dot(dx, wx[...], NT) + dot(dbc, wbc[...], NT) + dot(ddt[...], to_lanes(wdt[...]), NT)
    o_part[...] = dn.astype(BF16)
    x = tok[FRONT:, :].astype(F32)
    scale = lax.rsqrt(jnp.mean(x * x, axis=-1, keepdims=True) + EPSILON)
    now = jnp.sum(dn * x * scale, axis=0, keepdims=True)

    @pl.when(step == 0)
    def _():
        gain[0:1, :] = now

    @pl.when(step > 0)
    def _():
        gain[0:1, :] += now

    @pl.when(step == pl.num_programs(0) - 1)
    def _():
        conv = jnp.sum(g_conv[...], axis=0)
        left = jnp.concatenate(
            [
                conv[: KCONV + 1, :width],
                jnp.sum(g_gn[...], axis=0)[0:1],
                jnp.zeros((SMALL - KCONV - 2, width), F32),
            ],
            axis=0,
        )
        right = jnp.concatenate([jnp.sum(g_hp[...], axis=0), jnp.zeros((SMALL - 8, LANES), F32)], axis=0)
        below = rows * pl.num_programs(0)
        more = pl.ds(pl.multiple_of(below, rows), SMALL)
        o_dx[more, :width] = left.astype(BF16)
        o_dx[more, width:] = right.astype(BF16)
        bc = dbc.shape[1]
        cuts = [slice(j * bc, (j + 1) * bc) for j in range(model // bc)]
        kept = [g_two[:experts, c] for c in cuts]
        kept += [gain[0:1, c] for c in cuts] + [g_two[experts : experts + 1, c] for c in cuts]
        kept.append(conv[: KCONV + 1, width:])
        size = beside_rows(experts, model)
        kept.append(jnp.zeros((size - sum(k.shape[0] for k in kept), bc), F32))
        o_bc[pl.ds(pl.multiple_of(below, rows), size), :] = jnp.concatenate(kept, axis=0).astype(BF16)


def total_of(arrived):
    return sum(arrived[k].astype(F32) for k in range(arrived.shape[0]))


def k_rows_one(tok, gains, arrived, o_residual, o_mixer, o_two, o_scales):
    model = tok.shape[1]
    total = total_of(arrived)
    scale = lax.rsqrt((total[:, model : model + 1] + total[:, model + 1 : model + 2]) / INNER + EPSILON)
    mixer = total[:, :model] * scale
    residual = tok[...].astype(F32) + mixer
    scale_two = lax.rsqrt(jnp.mean(residual * residual, axis=-1, keepdims=True) + EPSILON)
    o_residual[...] = residual
    o_mixer[...] = mixer
    o_two[...] = (residual * scale_two * gains[1:2]).astype(BF16)
    o_scales[...] = to_lanes(jnp.concatenate([scale, scale_two], axis=1))


def k_rows_two(dout, two, residual, mixer, scales, gains, router, arrived, o_dm, o_dr, o_small):
    model = two.shape[1]
    experts = router.shape[1]
    both = total_of(arrived)
    dn2, dgate = both[:, :model], both[:, model:]
    w = to_lanes(router[...])
    probs = masked_softmax(dot(two[...], w), dout[:, model:].astype(F32))
    dlog = (probs * (dgate - jnp.sum(probs * dgate, axis=-1, keepdims=True))).astype(BF16)
    dn2 = dn2 + dot(dlog, w, NT)
    scale, scale_two = scales[:, 0:1], scales[:, 1:2]
    scaled = residual[...] * scale_two
    o_small[:experts, :] = dot(dlog, two[...], TN)[:experts]
    o_small[experts:, :] = jnp.broadcast_to(jnp.sum(dn2 * scaled, axis=0, keepdims=True), (8, model))
    gg = dn2 * gains[1:2]
    dr = dout[:, :model].astype(F32) + scale_two * (
        gg - scaled * jnp.mean(gg * scaled, axis=-1, keepdims=True)
    )
    o_dr[...] = dr
    dm = dr.astype(BF16)
    stat = jnp.sum(dm.astype(F32) * mixer[...], axis=-1, keepdims=True)
    o_dm[:, :model] = dm
    o_dm[:, model:] = to_lanes(jnp.concatenate([*two_terms(stat), *two_terms(scale)], axis=1))


def k_rows_out(residual, arrived, o):
    out = (residual[...] + total_of(arrived)).astype(BF16)
    for k in range(o.shape[0]):
        o[k] = out


def k_rows_three(tok, dr, gains, arrived, o):
    dn1 = total_of(arrived)
    x = tok[...].astype(F32)
    scale = lax.rsqrt(jnp.mean(x * x, axis=-1, keepdims=True) + EPSILON)
    scaled = x * scale
    gg = dn1 * gains[0:1]
    dtok = (dr[...] + scale * (gg - scaled * jnp.mean(gg * scaled, axis=-1, keepdims=True))).astype(BF16)
    for k in range(o.shape[0]):
        o[k] = dtok


def masked_softmax(logits, mask):
    on = mask > 0.0
    top = jnp.max(jnp.where(on, logits, -3.0e38), axis=-1, keepdims=True)
    e = jnp.where(on, jnp.exp(jnp.where(on, logits - top, 0.0)), 0.0)
    return e / jnp.sum(e, axis=-1, keepdims=True)


def mlp(x, do, wg, wu, wd, gate):
    g = dot(x, wg)
    u = dot(x, wu)
    sig = sigmoid(g)
    silu = g * sig
    hid = (silu * u).astype(BF16)
    dh = dot(do, wd, NT)
    if gate is None:
        hg, dgate = hid, None
    else:
        hf = hid.astype(F32)
        dgate = jnp.sum(hf * dh, axis=-1, keepdims=True)
        hg = (hf * gate).astype(BF16)
        dh = dh * gate
    dg = (dh * u * sig * (1.0 + g * (1.0 - sig))).astype(BF16)
    du = (dh * silu).astype(BF16)
    return hg, dg, du, dgate


def start_all(copies):
    made = [pltpu.make_async_copy(src, dst, sem) for src, dst, sem in copies]
    for c in made:
        c.start()
    return made


def piece_copies(xs, slots, buffer, sems):
    out, at = [], 0
    rows = buffer.shape[0] // len(slots)
    for i, pieces in enumerate(slots):
        size = rows // pieces
        out.append(
            start_all(
                (xs[at + j].at[pl.ds(0, size)], buffer.at[pl.ds(i * rows + j * size, size)], sems.at[at + j])
                for j in range(pieces)
            )
        )
        at += pieces
    return out


def finish(copies):
    for c in copies:
        c.wait()


def k_expert(slots, with_shared, index, *refs):
    mine, router, w_in, w_down = refs[:4]
    pieces, count = sum(slots), len(slots)
    xs, ds = refs[4 : 4 + pieces], refs[4 + pieces : 4 + 2 * pieces]
    shared = refs[4 + 2 * pieces : 6 + 2 * pieces] if with_shared else ()
    refs = refs[len(refs) - 9 - 2 * count :]
    o_all, outs = refs[0], refs[1 : 1 + 2 * count]
    x_buf, d_buf, out_buf, dx_buf, keep_buf, x_sem, d_sem, o_sem = refs[1 + 2 * count :]
    rows = x_buf.shape[0] // count
    x_copies = piece_copies(xs, slots, x_buf, x_sem)
    d_copies = piece_copies(ds, slots, d_buf, d_sem)
    width = w_in.shape[2]
    wg, wu, wd = w_in[0, 0], w_in[0, 1], w_down[0]
    w = to_lanes(router[...])
    half = wg.shape[1]
    stores = []
    for i in range(count):
        at = pl.ds(i * rows, rows)
        finish(x_copies[i] + d_copies[i])
        x = x_buf[at, :]
        do = d_buf[at, :width]
        mask = d_buf[at, width:].astype(F32)
        lane = iota(mask.shape, 1)
        probs = masked_softmax(dot(x, w), mask)
        gate = jnp.sum(jnp.where(lane == mine[0], probs, 0.0), axis=-1, keepdims=True)
        hg, dg, du, dgate = mlp(x, do, wg, wu, wd, gate)
        dx = dot(dg, wg, NT) + dot(du, wu, NT)
        out = dot(hg, wd)
        if with_shared and i == 0:
            out = out + shared[0][...].astype(F32)
            dx = dx + shared[1][...].astype(F32)
        dx_buf[at, :width] = dx.astype(BF16)
        chosen = jnp.sum(jnp.where(lane == mine[0], mask, 0.0), axis=-1, keepdims=True) > 0.0
        dx_buf[at, width:] = jnp.where(jnp.logical_and(lane == mine[0], chosen), dgate, 0.0).astype(BF16)
        stores += start_all([(dx_buf.at[at], outs[2 * i], o_sem.at[3 * i + 1])])
        out_buf[at, :] = out.astype(BF16)
        keep_buf[at, :half] = hg
        keep_buf[at, half : 2 * half] = dg
        keep_buf[at, 2 * half :] = du
        stores += start_all(
            [
                (
                    out_buf.at[at],
                    o_all.at[pl.ds(pl.multiple_of(index[i] * rows, rows), rows)],
                    o_sem.at[3 * i],
                ),
                (keep_buf.at[at], outs[2 * i + 1], o_sem.at[3 * i + 2]),
            ]
        )
    finish(stores)


def k_shared(x, do, w_in, w_down, o_out, o_dx):
    width = w_in.shape[1]
    wg, wu, wd = w_in[0], w_in[1], w_down[...]
    hg, dg, du, _ = mlp(x[...], do[:, :width], wg, wu, wd, None)
    o_out[...] = dot(hg, wd).astype(BF16)
    o_dx[...] = (dot(dg, wg, NT) + dot(du, wu, NT)).astype(BF16)


def store_in_cuts(buffer, at, cuts, outs, sems, first):
    return start_all(
        (buffer.at[at, pl.ds(begin, size)], out.at[at], sems.at[first + j])
        for j, (out, (begin, size)) in enumerate(zip(outs, cuts))
    )


def weight_products(x_buf, d_buf, keep_buf, in_buf, down_buf, o_in, o_down, o_sem):
    half = down_buf.shape[0]
    width = in_buf.shape[0]
    step = 256
    stores = []
    for c in range(width // step):
        to = pl.ds(c * step, step)
        in_buf[to, :] = dot(x_buf[:, to], keep_buf[:, half:], TN)
        stores += store_in_cuts(in_buf, to, [(0, half), (half, half)], [o_in.at[0], o_in.at[1]], o_sem, 3 * c)
        down_buf[:, to] = dot(keep_buf[:, :half], d_buf[:, to], TN)
        stores += start_all([(down_buf.at[:, to], o_down.at[:, to], o_sem.at[3 * c + 2])])
    finish(stores)


def k_expert_weights(slots, index, *refs):
    pieces, count = sum(slots), len(slots)
    xs, ds, ks = refs[:pieces], refs[pieces : 2 * pieces], refs[2 * pieces : 2 * pieces + count]
    o_in, o_down, x_buf, d_buf, keep_buf, in_buf, down_buf, x_sem, d_sem, k_sem, o_sem = refs[2 * pieces + count :]
    rows = x_buf.shape[0] // count
    copies = piece_copies(xs, slots, x_buf, x_sem) + piece_copies(ds, slots, d_buf, d_sem)
    copies += [start_all([(ks[i], keep_buf.at[pl.ds(i * rows, rows)], k_sem.at[i])]) for i in range(count)]
    for c in copies:
        finish(c)
    weight_products(x_buf, d_buf, keep_buf, in_buf, down_buf, o_in, o_down, o_sem)


def k_shared_weights(slots, index, *refs):
    s_in, s_down = refs[:2]
    pieces, count = sum(slots), len(slots)
    xs, ds = refs[2 : 2 + pieces], refs[2 + pieces : 2 + 2 * pieces]
    o_in, o_down, x_buf, d_buf, keep_buf, in_buf, down_buf, x_sem, d_sem, o_sem = refs[2 + 2 * pieces :]
    rows = x_buf.shape[0] // count
    x_copies = piece_copies(xs, slots, x_buf, x_sem)
    d_copies = piece_copies(ds, slots, d_buf, d_sem)
    half = s_down.shape[0]
    width = s_in.shape[1]
    for i in range(count):
        at = pl.ds(i * rows, rows)
        finish(x_copies[i] + d_copies[i])
        hg, dg, du, _ = mlp(x_buf[at, :], d_buf[at, :width], s_in[0], s_in[1], s_down[...], None)
        keep_buf[at, :half] = hg
        keep_buf[at, half : 2 * half] = dg
        keep_buf[at, 2 * half :] = du
    weight_products(x_buf, d_buf, keep_buf, in_buf, down_buf, o_in, o_down, o_sem)


def k_outer(groups, cuts, index, *refs):
    counts = [sum(g) for g in groups]
    total = sum(counts)
    outs = refs[total : total + len(cuts)]
    a_buf, b_buf, o_buf, sem, o_sem = refs[total + len(cuts) :]
    copies, at, column = [], 0, 0
    for g, slots in enumerate(groups):
        pieces = refs[at : at + counts[g]]
        width = pieces[0].shape[1]
        buffer = a_buf if g == 0 else b_buf.at[:, pl.ds(column, width)]
        column += 0 if g == 0 else width
        copies += piece_copies(pieces, slots, buffer, sem.at[pl.ds(at, counts[g])])
        at += counts[g]
    for c in copies:
        finish(c)
    step = 256
    stores = []
    for c in range(a_buf.shape[1] // step):
        at = pl.ds(c * step, step)
        o_buf[at, :] = dot(a_buf[:, at], b_buf[...], TN).astype(BF16)
        stores += store_in_cuts(o_buf, at, cuts, outs, o_sem, len(cuts) * c)
    finish(stores)


def outer(a, bs, widths, rows, name):
    columns = a.pieces[0].shape[1]
    total = sum(widths)
    cuts = [(sum(widths[:i]), w) for i, w in enumerate(widths)]
    pieces = [p for g in (a, *bs) for p in g.pieces]
    dma = pltpu.SemaphoreType.DMA
    return call(
        functools.partial(k_outer, [g.slots for g in (a, *bs)], cuts),
        [Far(struct((columns, w), BF16)) for w in widths],
        [Far(p) for p in pieces],
        2 * rows * columns * total,
        name,
        index=a.index,
        scratch=[
            pltpu.VMEM((rows, columns), BF16),
            pltpu.VMEM((rows, total), BF16),
            pltpu.VMEM((columns, total), BF16),
            dma((len(pieces),)),
            dma((len(widths) * (columns // 256),)),
        ],
    )


def k_out_weights(slots, index, *refs):
    n = sum(slots)
    us, ds = refs[:n], refs[n : 2 * n]
    o, u_buf, d_buf, o_buf, u_sem, d_sem, o_sem = refs[2 * n :]
    model = o.shape[1]
    u_copies = piece_copies(us, slots, u_buf, u_sem)
    d_copies = piece_copies(ds, slots, d_buf, d_sem)
    rows = d_buf.shape[0] // len(slots)
    for i in range(len(slots)):
        finish(u_copies[i] + d_copies[i])
        at = pl.ds(i * rows, rows)
        more = d_buf[at, model:].astype(F32)
        d_buf[at, :model] = (d_buf[at, :model].astype(F32) * (more[:, 2:3] + more[:, 3:4])).astype(BF16)
    step = 256
    stores = []
    for c in range(u_buf.shape[1] // step):
        at = pl.ds(c * step, step)
        o_buf[at, :] = dot(u_buf[:, at], d_buf[:, :model], TN).astype(BF16)
        stores += start_all([(o_buf.at[at], o.at[at], o_sem.at[c])])
    finish(stores)


def out_weights(u, d, rows):
    width, model = u.pieces[0].shape[1], d.pieces[0].shape[1] - LANES
    n = len(u.pieces)
    dma = pltpu.SemaphoreType.DMA
    [out] = call(
        functools.partial(k_out_weights, u.slots),
        [Far(struct((width, model), BF16))],
        [Far(p) for p in (*u.pieces, *d.pieces)],
        2 * rows * width * model,
        "out_weights",
        index=u.index,
        scratch=[
            pltpu.VMEM((rows, width), BF16),
            pltpu.VMEM((rows, model + LANES), BF16),
            pltpu.VMEM((width, model), BF16),
            dma((n,)),
            dma((n,)),
            dma((width // 256,)),
        ],
    )
    return out


def k_pair(*refs):
    half = len(refs) // 3
    for a, b, o in zip(refs[:half], refs[half : 2 * half], refs[2 * half :]):
        o[...] = a[...].astype(F32) + b[...].astype(F32)


def both_cores(arrays, name):
    if lax.axis_size("seq") != 8:
        return [a.astype(F32) for a in arrays]
    others = [flip(a, "seq", 1) for a in arrays]
    steps = 4
    return call(
        k_pair,
        [Rows(struct(a.shape, F32), a.shape[0] // steps) for a in arrays],
        [Rows(a, a.shape[0] // steps) for a in (*arrays, *others)],
        0,
        name,
        grid=steps,
    )


def flip(array, axis, bit):
    return lax.ppermute(array, axis, [(i, i ^ bit) for i in range(lax.axis_size(axis))])


def bits_of(axis):
    return [1 << b for b in range(lax.axis_size(axis).bit_length() - 1)]


class Gathered:
    def __init__(self, pieces, slots, index):
        self.pieces, self.slots, self.index = pieces, slots, index

    def tails(self, first, half):
        out, at = [], 0
        for pieces in self.slots:
            last = self.pieces[at + pieces - 1]
            out.append(last[first - half * (pieces - 1) :])
            at += pieces
        return out

    def part(self, first, last):
        at, to = sum(self.slots[:first]), sum(self.slots[:last])
        return Gathered(self.pieces[at:to], self.slots[first:last], self.index[first:last])


XOR_ORDER = (0, 1, 2, 4, 3, 5, 6, 7)


def gather(own, half, cores=True, between=(None, None)):
    size = lax.axis_size("seq")
    place = lax.axis_index("seq")
    if size != 8:
        every = lax.all_gather(own, "seq")
        return Gathered([every[k] for k in range(size)], [1] * size, jnp.arange(size, dtype=jnp.int32))
    core, x, y = bits_of("seq")
    by_x = flip(own, "seq", x)
    by_y = flip(own, "seq", y)
    first_far = []
    if between[0] is not None and not cores:
        by_x, by_y = after((by_x, by_y), between[0])
    elif between[0] is not None:
        first_far = [flip(own, "seq", core)]
        by_x, by_y = after((by_x, by_y), between[0](own, first_far[0]))
    top = flip(by_x[:half], "seq", y)
    bottom = flip(by_y[half:], "seq", x)
    if between[1] is not None:
        first_far += [flip(by_x, "seq", core), flip(by_y, "seq", core)]
        top, bottom = after((top, bottom), between[1](by_x, by_y))
    near = [own, by_x, by_y, top, bottom]
    if not cores:
        index = jnp.stack([place ^ k for k in (0, x, y, x | y)]).astype(jnp.int32)
        return Gathered(near, [1, 1, 1, 2], index)
    far = first_far + [flip(a, "seq", core) for a in near[len(first_far) :]]
    pieces = [own, far[0], by_x, by_y, far[1], far[2], top, bottom, far[3], far[4]]
    return Gathered(pieces, [1, 1, 1, 1, 1, 1, 2, 2], xor_index())


def xor_index():
    return jnp.stack([lax.axis_index("seq") ^ k for k in XOR_ORDER]).astype(jnp.int32)


def low_sum(*terms):
    return sum(t.astype(F32) for t in terms).astype(BF16)


def k_split(x0, x1, y0, y1, d0, d1, o_x, o_y, o_x_late, o_y_late):
    half = o_x_late.shape[0]
    x = low_sum(x0[...], x1[...])
    y = low_sum(y0[...], y1[...])
    d = low_sum(d0[...], d1[...])
    o_x[:half, :] = d[:half]
    o_x[half:, :] = x[:half]
    o_y[:half, :] = d[half:]
    o_y[half:, :] = y[half:]
    o_x_late[...] = x[half:]
    o_y_late[...] = y[:half]


def k_late(x, y, ax, ay, o_x, o_y):
    half = x.shape[0]
    o_x[...] = low_sum(x[...], ay[:half, :])
    o_y[...] = low_sum(y[...], ax[:half, :])


def k_join(a, b, ax, ay, bx, by, o):
    half = bx.shape[0]
    total = a[...].astype(F32) + b[...].astype(F32)
    o[:half, :] = low_sum(total[:half], ax[half:, :], by[...])
    o[half:, :] = low_sum(total[half:], ay[half:, :], bx[...])


def scatter_first(parts, name):
    if lax.axis_size("seq") != 8:
        return [lax.psum_scatter(jnp.concatenate(parts, axis=0), "seq", scatter_dimension=0, tiled=True)]
    parts = dict(zip(XOR_ORDER, parts))
    core, x, y = bits_of("seq")
    rows, width = parts[0].shape
    r3, r5, r7, r1 = (flip(parts[k], "seq", core) for k in (3, 5, 7, 1))
    full, part = struct((rows, width), BF16), struct((rows // 2, width), BF16)
    to_x, to_y, late_x, late_y = call(
        k_split, [full, full, part, part], [parts[2], r3, parts[4], r5, parts[6], r7], 0, name + "_split"
    )
    return [parts[0], r1, flip(to_x, "seq", x), flip(to_y, "seq", y), late_x, late_y]


def scatter_second(state, name):
    if lax.axis_size("seq") != 8:
        return state
    own, r1, ax, ay, late_x, late_y = state
    _, x, y = bits_of("seq")
    part = struct(late_x.shape, BF16)
    late_x, late_y = call(k_late, [part, part], [late_x, late_y, ax, ay], 0, name + "_late")
    return [own, r1, ax, ay, flip(late_x, "seq", x), flip(late_y, "seq", y)]


def scatter_last(state, name):
    if lax.axis_size("seq") != 8:
        return state[0]
    [out] = call(k_join, [struct(state[0].shape, BF16)], state, 0, name + "_join")
    return out


def scan(send, backward, name, between=None, steps=None):
    place = lax.axis_index("seq")
    seqs, size = send.shape[0], send.shape[1] - FRONT
    bits = bits_of("seq")
    state = struct((seqs, size, LANES), F32)
    row = struct((seqs, 8, LANES), F32)
    held = []
    for bit in bits_of("seq"):
        recv = flip(send, "seq", bit)
        is_set = (place & bit) != 0
        ahead = (jnp.logical_not(is_set) if backward else is_set).astype(jnp.int32)[None]
        last = bit == bits[-1]
        if last and between is not None:
            recv = after(recv, between)
        outs = [state] if last else [state, row, struct(send.shape, BF16)]
        made = call(
            functools.partial(k_scan, not held, last),
            [Each(o) for o in outs],
            [Scalars(ahead), Each(recv), Each(send), *(Each(a) for a in held)],
            0,
            name,
            grid=seqs,
        )
        if last:
            return made[0]
        held, send = made[:2], made[2]
        if steps is not None:
            steps.append(send)
    return before


def rows_of_mp(array):
    share = array.shape[0] // lax.axis_size("mp")
    return lax.dynamic_slice_in_dim(array, lax.axis_index("mp") * share, share, 0)


def exchange_mp(array):
    return lax.all_to_all(array, "mp", 0, 0, tiled=True)


def to_shares(array):
    size = lax.axis_size("mp")
    return exchange_mp(array.reshape(size, array.shape[0] // size, array.shape[1]))


def gather_mp(array):
    return lax.all_gather(array, "mp", tiled=True)


def after(values, others):
    return lax.optimization_barrier((values, others))[0]


def all_sum(array, axes):
    for axis in axes:
        for bit in bits_of(axis):
            array = array + flip(array, axis, bit)
    return array


def passed_along(block, axis, distance):
    devices = range(lax.axis_size(axis))
    route = [(i - distance, i) for i in devices if i - distance in devices]
    return lax.ppermute(block, axis, route)


def body(
    tokens, lengths, expert_ids, norm_gains, in_z, in_x, in_bc, in_dt, conv_x, conv_bc,
    head_par, gn_gain, out_w, router, shared_in, shared_down, expert_in, expert_down, d_out,
):
    piece, seqs, model = tokens.shape
    width = in_z.shape[1]
    heads = head_par.shape[1]
    experts = router.shape[1]
    half = expert_in.shape[-1]
    n_seq, n_mp = lax.axis_size("seq"), lax.axis_size("mp")
    seq_at, mp_at = lax.axis_index("seq"), lax.axis_index("mp")
    rows = seqs * piece
    share = rows // n_mp
    bc = 2 * STATE
    beside = beside_rows(experts, model)
    dma = pltpu.SemaphoreType.DMA

    meta = jnp.concatenate([lengths, (seq_at * piece).astype(jnp.int32)[None]])
    tok = jnp.transpose(tokens, (1, 0, 2))
    edge_in = passed_along(tokens[piece - (KCONV - 1) :], "seq", 1)
    front = jnp.pad(jnp.transpose(edge_in, (1, 0, 2)), ((0, 0), (FRONT - (KCONV - 1), 0), (0, 0)))
    tok_front = jnp.concatenate([front, tok], axis=1)
    gn = gn_gain[None]
    picked = jnp.sum(
        (expert_ids[..., None] == jnp.arange(LANES, dtype=jnp.int32)).astype(F32), axis=2
    ).astype(BF16)
    small = [conv_x, conv_bc, head_par, Scalars(meta)]
    d_ext = jnp.transpose(jnp.concatenate([d_out, picked], axis=-1), (1, 0, 2)).reshape(rows, model + LANES)

    def both(*shape, dtype=F32):
        return Each(struct((seqs, *shape), dtype))

    normed, gate_z, xbc, dt_raw, send, totals = call(
        k_in,
        [
            both(piece, model, dtype=BF16),
            both(piece, width),
            both(piece + FRONT, width + bc, dtype=BF16),
            both(piece, LANES),
            both(width + FRONT, LANES, dtype=BF16),
            both(8, LANES),
        ],
        [Each(tok_front), norm_gains, in_z, in_x, in_bc, in_dt, *small],
        2 * rows * model * (2 * width + bc + LANES),
        "mixer_in",
        grid=seqs,
    )
    entering = scan(send, False, "scan")
    intra, c_mat, ecum = call(
        k_intra,
        [both(piece, width), both(piece, STATE, dtype=BF16), both(piece, width)],
        [Each(xbc), Each(dt_raw), *small],
        2 * rows * piece * width * 4,
        "mixer_intra",
        grid=seqs,
    )
    of_rows = struct((share, model), F32)
    mixed, u, part = call(
        k_out,
        [both(piece, width), both(piece, width, dtype=BF16), both(piece, model + LANES, dtype=BF16)],
        [Each(intra), Each(c_mat), Each(ecum), Each(entering), Each(gate_z), gn, out_w],
        2 * rows * width * (STATE + model),
        "mixer_out",
        grid=seqs,
    )
    tok_own = rows_of_mp(tok.reshape(rows, model))
    d_own = rows_of_mp(d_ext)
    arrived = to_shares(part.reshape(rows, model + LANES))
    residual, mixer_own, two_own, scales = call(
        k_rows_one,
        [of_rows, of_rows, struct((share, model), BF16), struct((share, LANES), F32)],
        [tok_own, norm_gains, arrived],
        0,
        "rows_one",
    )
    d_got = gather(d_ext, piece, between=(lambda *_: entering, lambda *_: two_own))
    two = gather_mp(two_own)

    mine = ((seq_at * n_mp + mp_at) // 2).astype(jnp.int32)[None]

    def expert(pieces, first, last, o_all, shared=()):
        part_d = d_got.part(first, last)
        slots, index = part_d.slots, part_d.index
        count = len(slots)
        size = rows * count
        return call(
            functools.partial(k_expert, slots, bool(shared)),
            [Far(struct((n_seq * rows, model), BF16))]
            + [Far(struct((rows, model + LANES), BF16)), Far(struct((rows, 3 * half), BF16))] * count,
            [
                Scalars(mine), router, expert_in, expert_down, *(Far(p) for p in (*pieces, *part_d.pieces)),
                *shared, *(Far(o) for o in o_all),
            ],
            2 * size * model * half * 6.5,
            "experts",
            index=index,
            aliases={5 + 2 * len(pieces): 0} if o_all else None,
            scratch=[
                pltpu.VMEM((size, model), BF16),
                pltpu.VMEM((size, model + LANES), BF16),
                pltpu.VMEM((size, model), BF16),
                pltpu.VMEM((size, model + LANES), BF16),
                pltpu.VMEM((size, 3 * half), BF16),
                dma((len(pieces),)),
                dma((len(pieces),)),
                dma((3 * count,)),
            ],
        )

    def shared_of(x):
        return call(
            k_shared,
            [struct((rows, model), BF16), struct((rows, model), BF16)],
            [x, d_ext, shared_in, shared_down],
            2 * rows * model * half * 6,
            "shared",
        )

    made = []

    def near_experts(own, far):
        made.append(expert([own, far], 0, 2, [], shared_of(own)))
        return made

    def chip_experts(by_x, by_y):
        made.append(expert([by_x, by_y], 2, 4, made[-1][:1]))
        return made[-1]

    if n_seq == 8:
        two, d_got.pieces = lax.optimization_barrier((two, d_got.pieces))
        x_got = gather(two, piece, between=(near_experts, chip_experts))
        made.append(expert(x_got.pieces[4:], 4, 8, made[-1][:1]))
    else:
        x_got = gather(two, piece)
        out_shared, dx_shared = shared_of(two)
        for i in range(0, n_seq, 4):
            made.append(expert(x_got.part(i, i + 4).pieces, i, i + 4, made[-1][:1] if made else []))
    out_all = made[-1][0]
    e_dx = [a for m in made for a in m[1::2]]
    e_keep = [a for m in made for a in m[2::2]]

    g_expert_in = g_expert_down = g_shared_in = g_shared_down = 0.0
    weight_outs = [Far(struct((2, model, half), F32)), Far(struct((half, model), F32))]

    def weight_scratch(keeps, pieces):
        return [
            pltpu.VMEM((8 * rows, model), BF16),
            pltpu.VMEM((8 * rows, model + LANES), BF16),
            pltpu.VMEM((8 * rows, 3 * half), BF16),
            pltpu.VMEM((model, 2 * half), F32),
            pltpu.VMEM((half, model), F32),
            dma((pieces,)),
            dma((pieces,)),
            *([dma((8,))] if keeps else []),
            dma((3 * (model // 256),)),
        ]

    def shared_weights(first, others):
        x = x_got.part(first, first + 8)
        return call(
            functools.partial(k_shared_weights, x.slots),
            weight_outs,
            [shared_in, shared_down, *(Far(a) for a in (*after(x.pieces, others), *d_got.part(first, first + 8).pieces))],
            6 * 2 * 8 * rows * model * half,
            "shared_weights",
            index=x.index,
            scratch=weight_scratch(False, len(x.pieces)),
        )

    def expert_weights(first, others):
        x = x_got.part(first, first + 8)
        return call(
            functools.partial(k_expert_weights, x.slots),
            weight_outs,
            [Far(a) for a in (*after(x.pieces, others), *d_got.part(first, first + 8).pieces, *e_keep[first : first + 8])],
            3 * 2 * 8 * rows * model * half,
            "expert_weights",
            index=x.index,
            scratch=weight_scratch(True, len(x.pieces)),
        )

    state = scatter_first(e_dx, "dx")
    if n_seq == 8:
        g_shared_in, g_shared_down = shared_weights(0, e_dx)
        state, g_shared_in, g_shared_down = lax.optimization_barrier((state, g_shared_in, g_shared_down))
        state = scatter_second(state, "dx")
        g_expert_in, g_expert_down = expert_weights(0, g_shared_down)
        state, g_expert_in, g_expert_down = lax.optimization_barrier((state, g_expert_in, g_expert_down))
    else:
        for first in range(0, n_seq, 8):
            a, b = shared_weights(first, e_dx)
            c, d = expert_weights(first, e_dx)
            g_shared_in, g_shared_down = g_shared_in + a, g_shared_down + b
            g_expert_in, g_expert_down = g_expert_in + c, g_expert_down + d
    dx_sum = scatter_last(state, "dx")
    if n_seq != 8:
        dx_sum = jnp.concatenate([low_sum(dx_sum[:, :model], dx_shared), dx_sum[:, model:]], axis=1)
    arrived = to_shares(dx_sum)
    out_sum = lax.psum_scatter(after(out_all, dx_sum), "seq", scatter_dimension=0, tiled=True)
    if n_seq != 8:
        out_sum = low_sum(out_sum, out_shared)
    dm_own, d_residual, g_two = call(
        k_rows_two,
        [struct((share, model + LANES), BF16), of_rows, struct((experts + 8, model), F32)],
        [d_own, two_own, residual, mixer_own, scales, norm_gains, router, arrived],
        0,
        "rows_two",
    )
    dm = gather_mp(dm_own)
    if n_seq == 8:
        n_got = gather(after(normed, part).reshape(rows, model), piece, False, (dx_sum, None))
    else:
        normed, u = after((normed, u), (dm, g_expert_in, g_shared_in))
        n_got = gather(normed.reshape(rows, model), piece, False)
    u_got = gather(after(u, dx_sum).reshape(rows, width), piece, False)
    if n_seq == 8:
        dm, u_got.pieces = lax.optimization_barrier((dm, u_got.pieces))

    dz, dy, send, g_gn = call(
        k_back_gate,
        [
            both(piece, width, dtype=BF16),
            both(piece, width),
            both(width + FRONT, LANES, dtype=BF16),
            both(8, width),
        ],
        [Rows(dm, piece), Each(mixed), Each(gate_z), gn, out_w, Each(c_mat), Each(ecum), Each(totals)],
        2 * rows * width * (model + STATE),
        "back_gate",
        grid=seqs,
    )
    intra_back = call(
        k_back_intra,
        [both(piece, width), both(piece, STATE), both(piece, STATE), both(piece, LANES), both(piece, model)],
        [Each(xbc), Each(dt_raw), *small, Each(dy), Each(dz), in_z],
        2 * rows * width * (model + 4 * piece),
        "back_intra",
        grid=seqs,
    )
    dxw0, db0, dc0, dcum0, dn0 = intra_back
    steps = []
    leaving = scan(send, True, "scan_back", intra_back, steps)
    dz_got = gather(after(dz, leaving).reshape(rows, width), piece, False)
    dm_got = gather(after(dm, leaving), piece, False)
    out_arrived = to_shares(after(out_sum, steps[0]))
    [out_own] = call(k_rows_out, [struct((n_mp, share, model), BF16)], [residual, out_arrived], 0, "rows_out")
    out_rows = exchange_mp(out_own)

    def in_order(rows):
        return jnp.transpose(rows.reshape(seqs, piece, model), (1, 0, 2)).astype(F32)

    d_xbc, d_dt, g_conv, g_hp = call(
        k_back_state,
        [
            both(piece + FRONT, width + bc),
            both(piece, LANES, dtype=BF16),
            both(8, width + bc),
            both(8, LANES),
        ],
        [
            Each(xbc), Each(dt_raw), *small, Each(dy), Each(dxw0), Each(db0), Each(dc0), Each(dcum0),
            Each(entering), Each(leaving),
        ],
        2 * rows * width * STATE * 20,
        "back_state",
        grid=seqs,
    )
    edge = passed_along(d_xbc[:, :FRONT], "seq", -1)
    if n_seq == 8:
        edge, dz_got.pieces[1:3], out_rows = lax.optimization_barrier((edge, dz_got.pieces[1:3], out_rows))
    output = in_order(out_rows)
    dx, d_bc, part = call(
        k_back_in,
        [
            struct((rows + SMALL, width + LANES), BF16),
            struct((rows + beside, bc), BF16),
            both(piece, model, dtype=BF16),
        ],
        [
            Each(dn0), Each(d_xbc), Each(edge), Each(d_dt), Each(tok_front), g_conv, g_hp, g_gn, g_two,
            in_x, in_bc, in_dt,
        ],
        2 * rows * (width + bc + LANES) * model,
        "back_in",
        grid=seqs,
        scratch=[pltpu.VMEM((8, model), F32)],
    )
    arrived = to_shares(part.reshape(rows, model))
    *head_bits, last_bit = bits_of("mp")
    for bit in head_bits:
        d_bc = low_sum(d_bc, flip(d_bc, "mp", bit))
    d_bc = low_sum(d_bc, flip(d_bc, "mp", last_bit))
    bc_got = gather(d_bc, piece, False)
    dx_got = gather(dx, piece, False)

    g_in_z = g_in_x = g_dt = g_in_bc = g_out_w = 0.0
    size = min(8, len(n_got.slots))
    for first in range(0, len(n_got.slots), size):
        last = first + size
        [a] = outer(n_got.part(first, last), [dz_got.part(first, last)], [width], size * rows, "weights_z")
        g_in_z = g_in_z + a
        g_out_w = g_out_w + out_weights(u_got.part(first, last), dm_got.part(first, last), size * rows)
    if n_seq == 8:
        arrived, g_in_z, g_out_w, d_bc, dx_got.pieces[1:3] = lax.optimization_barrier(
            (arrived, g_in_z, g_out_w, d_bc, dx_got.pieces[1:3])
        )
    [rows_own] = call(
        k_rows_three,
        [struct((n_mp, share, model), BF16)],
        [tok_own, d_residual, norm_gains, arrived],
        0,
        "rows_three",
    )
    rows_all = exchange_mp(rows_own)
    [g_in_z] = both_cores([g_in_z], "cores_z")
    [g_out_w] = both_cores([g_out_w], "cores_out")
    for first in range(0, len(n_got.slots), size):
        last = first + size
        a, b, c = outer(
            n_got.part(first, last), [dx_got.part(first, last), bc_got.part(first, last)], [width, LANES, bc],
            size * rows, "weights_x",
        )
        g_in_x, g_dt, g_in_bc = g_in_x + a, g_dt + b, g_in_bc + c
    if n_seq == 8:
        rows_all, g_in_x, g_dt, g_in_bc, g_in_z, g_out_w = lax.optimization_barrier(
            (rows_all, g_in_x, g_dt, g_in_bc, g_in_z, g_out_w)
        )

    d_tokens = in_order(rows_all)
    small = sum(t.astype(F32) for t in dx_got.tails(rows, piece))
    summed = sum(t.astype(F32) for t in bc_got.tails(rows, piece))
    if n_seq == 8:
        small = small + flip(small, "seq", 1)
        summed = summed + flip(summed, "seq", 1)
    g_in_x, g_dt, g_in_bc = both_cores([g_in_x, g_dt, g_in_bc], "cores_x")
    cuts = model // bc
    g_router = summed[: cuts * experts].reshape(cuts, experts, bc)
    first = cuts * experts
    return (
        output,
        d_tokens,
        summed[first : first + 2 * cuts].reshape(2, model),
        g_in_z,
        g_in_x,
        g_in_bc,
        g_dt[:, :heads],
        small[: KCONV + 1, :width],
        summed[first + 2 * cuts : first + 2 * cuts + KCONV + 1],
        small[:3, width : width + heads],
        small[KCONV + 1, :width],
        g_out_w,
        jnp.transpose(g_router, (0, 2, 1)).reshape(model, experts),
        g_shared_in,
        g_shared_down,
        g_expert_in[None],
        g_expert_down[None],
    )


def solution(mesh):
    in_specs = (
        P("seq", None, None),
        P(),
        P("seq", None, None),
        P(),
        P(None, "mp"),
        P(None, "mp"),
        P(),
        P(None, "mp"),
        P(None, "mp"),
        P(),
        P(None, "mp"),
        P("mp"),
        P("mp", None),
        P(),
        P(None, None, "mp"),
        P("mp", None),
        P(("seq", "mp"), None, None, None),
        P(("seq", "mp"), None, None),
        P("seq", None, None),
    )
    out_specs = (
        P("seq", None, None),
        P("seq", None, None),
        P(),
        P(None, "mp"),
        P(None, "mp"),
        P(),
        P(None, "mp"),
        P(None, "mp"),
        P(),
        P(None, "mp"),
        P("mp"),
        P("mp", None),
        P(),
        P(None, None, "mp"),
        P("mp", None),
        P(("seq", "mp"), None, None, None),
        P(("seq", "mp"), None, None),
    )
    return jax.shard_map(body, mesh=mesh, in_specs=in_specs, out_specs=out_specs, check_vma=False)
```

time: 579 us -> 490 us (0.85)
  waiting for transfers between devices: 147 us -> 95.3 us
  blocking collectives: 75 us -> 38.5 us
  starting transfers between devices: 73.4 us -> 91.3 us
  local copies, waits for them, and re-layouts: 53.1 us -> 42.9 us
    all_gather x4 -> x2, blocking collectives: 75 us -> 38.5 us  [gather_mp(): return lax.all_gather(array, 'mp', tiled=True)]
    psum x1 -> x0, waiting for transfers between devices: 18.4 us -> none  [body(): g_out_w = lax.psum(g_out_w.astype(BF16), 'seq').astype(F32)]
    all_to_all x4 -> x6, waiting for transfers between devices: 34.9 us -> 17.3 us  [exchange_mp(): return lax.all_to_all(array, 'mp', 0, 0, tiled=True)]
    ppermute x74 -> x65, waiting for transfers between devices: 93.9 us -> 76.9 us  [flip(): lax.ppermute(array, axis, [(i, i ^ bit) for i in range(lax.axis_size(axis...]
    all_to_all x4 -> x6, starting transfers between devices: 16.8 us -> 26.9 us  [exchange_mp(): return lax.all_to_all(array, 'mp', 0, 0, tiled=True)]
    ppermute x74 -> x65, starting transfers between devices: 52.5 us -> 60.7 us  [flip(): lax.ppermute(array, axis, [(i, i ^ bit) for i in range(lax.axis_size(axis...]
    slice x14 -> x6, local copies, waits for them, and re-layouts: 9.84 us -> 2.41 us  [the longest x1 0.61 us: body(): small[:KCONV + 1, :width]]
    pallas_call x30 -> x32, Pallas kernels: 195 us -> 191 us  [call(): pl.pallas_call(kernel, out_shape=shapes, grid_spec=grid_spec, input_outpu...]
  transfers between devices with their start and end apart: 82 -> 74, of which waited for: 23 -> 25; matrix products, arithmetic and copies ran while one was open for 8% -> 6% of each run, Pallas kernels for 32% -> 32%
where the time goes in v2:
time: 490 us; the launch traced here: 482 us
  Pallas kernels  191 us (39%)
  waiting for transfers between devices  95.3 us (19%)
  starting transfers between devices  91.3 us (19%)
  local copies, waits for them, and re-layouts  42.9 us (9%)
  blocking collectives  38.5 us (8%)
  between operations  15.2 us (3%)
  other arithmetic  7.87 us (2%)
    pallas_call x32, Pallas kernels, call(): pl.pallas_call(kernel, out_shape=shapes, grid_spec=grid_spec, input_outpu...  191 us
    ppermute x65, waiting for transfers between devices, flip(): lax.ppermute(array, axis, [(i, i ^ bit) for i in range(lax.axis_size(axis...  76.9 us
    ppermute x65, starting transfers between devices, flip(): lax.ppermute(array, axis, [(i, i ^ bit) for i in range(lax.axis_size(axis...  60.7 us
    all_gather x2, blocking collectives, gather_mp(): return lax.all_gather(array, 'mp', tiled=True)  38.5 us
    all_to_all x6, starting transfers between devices, exchange_mp(): return lax.all_to_all(array, 'mp', 0, 0, tiled=True)  26.9 us
    unnamed x116, local copies, waits for them, and re-layouts  21.9 us
    all_to_all x6, waiting for transfers between devices, exchange_mp(): return lax.all_to_all(array, 'mp', 0, 0, tiled=True)  17.3 us
  transfers between devices with their start and end apart: 74, of which 25 were waited for; matrix products, arithmetic and copies ran while one was open for 6% of the time, Pallas kernels for 32%

profile of v2, /device:TPU:0, one launch (start us, length us, event | category | flops | bytes accessed | tf_op | source)
XLA Modules:
  0.0 482.3 jit_solution(12034226610673328995)
XLA Ops:
  14.8 7.5 %mixer_in.1 = (bf16[2,128,1536]{2,1,0:T(8,128)(2,1)}, f32[2,128,768]{2,1,0:T(8,128)}, bf16[2,144,1024]{2,1,0:T(8,128)(2,1)}, f32[2,128,128]{2,1,0:T(8,128)}, bf1...) custom-call(bf16[2,144,1536]{2,1,0:T(8,128)(2,1)} %fusion.1.tok, f32[2,1536]{1,0:T(2,128)} %gains.7, ...), custom_call_target="tpu_custom_call" | custom-call | flops 1509949440 | bytes 9162908 | tf_op jit(solution)/shard_map/mixer_in/pallas_call | solution.py:77
  31.1 10.3 %collective-permute-done.2.recv = bf16[2,784,128]{2,1,0:T(8,128)(2,1)S(1)} collective-permute-done((bf16[2,784,128]{2,1,0:T(8,128)(2,1)}, bf16[2,784,128]{2,1,0:T(8,128)(2,1)S(1)}, u32[]{:S(2)}, u32[]{:S(2)}) %collective-permute-start.2) | collective-permute-done | bytes 401440 | tf_op jit(solution)/shard_map/ppermute | solution.py:773
  78.6 9.3 %all-to-all-done.arrived = bf16[4,64,1664]{2,1,0:T(8,128)(2,1)S(1)} async-done(((bf16[4,64,1664]{2,1,0:T(8,128)(2,1)}), bf16[4,64,1664]{2,1,0:T(8,128)(2,1)S(1)}, u32[]{:S(2)}, u32[]{:S(2)}) %all-to-all-start) | async-done | bytes 852000 | tf_op jit(solution)/shard_map/all_to_all | solution.py:931
  91.9 18.7 %all_gather.6.x.refs_4_.refs_2_.refs_0_ = bf16[256,1536]{1,0:T(8,128)(2,1)S(1)} all-gather(bf16[64,1536]{1,0:T(8,128)(2,1)} %get-tuple-element.200.two), channel_id=1, replica_groups=mesh['seq'=8,'mp'=4] {'mp'}, dimensions={0}, use_global_device_ids=true | all-gather | bytes 983040 | tf_op jit(solution)/shard_map/all_gather | solution.py:940
  120.4 9.8 %experts.3 = (bf16[2048,1536]{1,0:T(8,128)(2,1)}, bf16[256,1664]{1,0:T(8,128)(2,1)}, bf16[256,768]{1,0:T(8,128)(2,1)}, bf16[256,1664]{1,0:T(8,128)(2,1)}, bf16[256,768]{1,0:T(8,128)(2,1)}) custom-call(s32[2]{0:T(128)} %pad_add_fusion.1.index, s32[1]{0:T(128)} %bitcast.12.refs_0_, bf16[1536,16]{1,0:T(8,128)(2,1)} %copy.75.refs_1_.router, ...), custom_call_target="tpu_custom_call" | custom-call | flops 2617245696 | bytes 16039940 | tf_op jit(solution)/shard_map/experts/pallas_call | solution.py:77
  136.9 9.3 %experts.4 = (bf16[2048,1536]{1,0:T(8,128)(2,1)}, bf16[256,1664]{1,0:T(8,128)(2,1)}, bf16[256,768]{1,0:T(8,128)(2,1)}, bf16[256,1664]{1,0:T(8,128)(2,1)}, bf16[256,768]{1,0:T(8,128)(2,1)}) custom-call(s32[2]{0:T(128)} %pad_add_fusion.2.index, s32[1]{0:T(128)} %bitcast.12.refs_0_, ...), custom_call_target="tpu_custom_call", output_to_operand_aliasing={{0}: (9, {})} | custom-call | flops 2617245696 | bytes 20758532 | tf_op jit(solution)/shard_map/experts/pallas_call | solution.py:77
  149.8 14.1 %experts.5 = (bf16[2048,1536]{1,0:T(8,128)(2,1)}, bf16[256,1664]{1,0:T(8,128)(2,1)}, bf16[256,768]{1,0:T(8,128)(2,1)}, bf16[256,1664]{1,0:T(8,128)(2,1)}, bf16[2...) custom-call(s32[4]{0:T(128)} %pad_add_fusion.3.index, ...), custom_call_target="tpu_custom_call", output_to_operand_aliasing={{0}: (17, {})} | custom-call | flops 5234491392 | bytes 26525700 | tf_op jit(solution)/shard_map/experts/pallas_call | solution.py:77
  176.0 18.0 %shared_weights.1 = (f32[2,1536,256]{2,1,0:T(8,128)}, f32[256,1536]{1,0:T(8,128)}) custom-call(s32[8]{0:T(128)} %stack.65.index, bf16[2,1536,256]{2,1,0:T(8,128)(2,1)} %refs_0_.1, bf16[256,1536]{1,0:T(8,128)(2,1)} %refs_1_.4, bf16[256,1536]{1,0:T(8,128)(2,1)} %copy-done.17, bf16[256,1536]{1,0:T(8,128)(2,1)} %collective-permute-done.13.refs_5_.refs_3_.refs_1_, ...), custom_call_target="tpu_custom_call" | custom-call | flops 9663676416 | bytes 20185088 | tf_op jit(solution)/shard_map/shared_weights/pallas_call | solution.py:77
  201.1 12.6 %expert_weights.1 = (f32[2,1536,256]{2,1,0:T(8,128)}, f32[256,1536]{1,0:T(8,128)}) custom-call(s32[8]{0:T(128)} %stack.65.index, bf16[256,1536]{1,0:T(8,128)(2,1)} %copy-done.17, bf16[256,1536]{1,0:T(8,128)(2,1)} %collective-permute-done.13.refs_5_.refs_3_.refs_1_, bf16[256,1536]{1,0:T(8,128)(2,1)} %copy-done.9, bf16[256,1536]{1,0:T(8,128)(2,1)} %copy-done.10, ...), custom_call_target="tpu_custom_call" | custom-call | flops 4831838208 | bytes 20971520 | tf_op jit(solution)/shard_map/expert_weights/pallas_call | solution.py:77
  225.7 6.0 %collective-permute-done.30.refs_1_ = bf16[256,768]{1,0:T(8,128)(2,1)S(1)} collective-permute-done((bf16[256,768]{1,0:T(8,128)(2,1)S(1)}, bf16[256,768]{1,0:T(8,128)(2,1)S(1)}, u32[]{:S(2)}, u32[]{:S(2)}) %collective-permute-start.30) | collective-permute-done | bytes 393248 | tf_op jit(solution)/shard_map/ppermute | solution.py:773
  234.6 7.9 %all-to-all-done.1.arrived = bf16[4,64,1664]{2,1,0:T(8,128)(2,1)S(1)} async-done(((bf16[4,64,1664]{2,1,0:T(8,128)(2,1)}), bf16[4,64,1664]{2,1,0:T(8,128)(2,1)S(1)}, u32[]{:S(2)}, u32[]{:S(2)}) %all-to-all-start.1) | async-done | bytes 852000 | tf_op jit(solution)/shard_map/all_to_all | solution.py:931
  246.9 19.8 %all_gather.7.dm.refs_5_ = bf16[256,1664]{1,0:T(8,128)(2,1)} all-gather(bf16[64,1664]{1,0:T(8,128)(2,1)} %get-tuple-element.286), channel_id=1, replica_groups=mesh['seq'=8,'mp'=4] {'mp'}, dimensions={0}, use_global_device_ids=true | all-gather | bytes 1064960 | tf_op jit(solution)/shard_map/all_gather | solution.py:940
  266.8 5.6 %back_gate.1 = (bf16[2,128,768]{2,1,0:T(8,128)(2,1)}, f32[2,128,768]{2,1,0:T(8,128)}, bf16[2,784,128]{2,1,0:T(8,128)(2,1)}, f32[2,8,768]{2,1,0:T(8,128)}) custom-call(bf16[256,1664]{1,0:T(8,128)(2,1)} %all_gather.7.dm.refs_5_, f32[2,128,768]{2,1,0:T(8,128)} %get-tuple-element.290.y, f32[2,128,768]{2,1,0:T(8,128)} %get-tuple-element.198.z, ...), custom_call_target="tpu_custom_call" | custom-call | flops 654311424 | bytes 7277568 | tf_op jit(solution)/shard_map/back_gate/pallas_call | solution.py:77
  284.6 9.6 %collective-permute-done.35.recv = bf16[2,784,128]{2,1,0:T(8,128)(2,1)S(1)} collective-permute-done((bf16[2,784,128]{2,1,0:T(8,128)(2,1)}, bf16[2,784,128]{2,1,0:T(8,128)(2,1)S(1)}, u32[]{:S(2)}, u32[]{:S(2)}) %collective-permute-start.35) | collective-permute-done | bytes 401440 | tf_op jit(solution)/shard_map/ppermute | solution.py:773
  299.0 6.9 %back_intra.1 = (f32[2,128,768]{2,1,0:T(8,128)}, f32[2,128,128]{2,1,0:T(8,128)}, f32[2,128,128]{2,1,0:T(8,128)}, f32[2,128,128]{2,1,0:T(8,128)}, f32[2,128,1536]{2,1,0:T(8,128)}) custom-call(bf16[2,144,1024]{2,1,0:T(8,128)(2,1)} %get-tuple-element.186.xbc, f32[2,128,128]{2,1,0:T(8,128)} %get-tuple-element.187.dt, f32[5,768]{1,0:T(8,128)} %conv_x.7, ...), custom_call_target="tpu_custom_call" | custom-call | flops 805306368 | bytes 7032988 | tf_op jit(solution)/shard_map/back_intra/pallas_call | solution.py:77
  324.0 8.8 %collective-permute-done.46.refs_6_ = bf16[256,1664]{1,0:T(8,128)(2,1)} collective-permute-done((bf16[256,1664]{1,0:T(8,128)(2,1)S(1)}, bf16[256,1664]{1,0:T(8,128)(2,1)}, u32[]{:S(2)}, u32[]{:S(2)}) %collective-permute-start.46) | collective-permute-done | bytes 852000 | tf_op jit(solution)/shard_map/ppermute | solution.py:773
  334.3 13.1 %back_state.1 = (f32[2,144,1024]{2,1,0:T(8,128)}, bf16[2,128,128]{2,1,0:T(8,128)(2,1)}, f32[2,8,1024]{2,1,0:T(8,128)}, f32[2,8,128]{2,1,0:T(8,128)}) custom-call(bf16[2,144,1024]{2,1,0:T(8,128)(2,1)} %get-tuple-element.186.xbc, f32[2,128,128]{2,1,0:T(8,128)} %get-tuple-element.187.dt, f32[5,768]{1,0:T(8,128)} %conv_x.7, f32[5,256]{1,0:T(8,128)} %conv_bc.7, ...), custom_call_target="tpu_custom_call" | custom-call | flops 1006632960 | bytes 5599388 | tf_op jit(solution)/shard_map/back_state/pallas_call | solution.py:77
  357.1 9.9 %collective-permute-done.39.refs_7_ = bf16[256,768]{1,0:T(8,128)(2,1)S(1)} collective-permute-done((bf16[256,768]{1,0:T(8,128)(2,1)S(1)}, bf16[256,768]{1,0:T(8,128)(2,1)S(1)}, u32[]{:S(2)}, u32[]{:S(2)}) %collective-permute-start.39) | collective-permute-done | bytes 393248 | tf_op jit(solution)/shard_map/ppermute | solution.py:773
  367.0 6.6 %back_in.1 = (bf16[272,896]{1,0:T(8,128)(2,1)}, bf16[384,256]{1,0:T(8,128)(2,1)}, bf16[2,128,1536]{2,1,0:T(8,128)(2,1)}) custom-call(f32[2,128,1536]{2,1,0:T(8,128)} %get-tuple-element.303.dn0, f32[2,144,1024]{2,1,0:T(8,128)} %get-tuple-element.307.dxbc, f32[2,16,1024]{2,1,0:T(8,128)} %copy-done.32, bf16[2,128,128]{2,1,0:T(8,128)(2,1)} %get-tuple-element.315.ddt, ...), custom_call_target="tpu_custom_call" | custom-call | flops 905969664 | bytes 8757248 | tf_op jit(solution)/shard_map/back_in/pallas_call | solution.py:77
  373.6 5.5 %all-to-all-start.4 = ((bf16[4,64,1536]{2,1,0:T(8,128)(2,1)}), bf16[4,64,1536]{2,1,0:T(8,128)(2,1)S(1)}, u32[]{:S(2)}, u32[]{:S(2)}) async-start(bf16[4,64,1536]{2,1,0:T(8,128)(2,1)} %bitcast.65), calls=%async_computation.5 | async-start | bytes 1572864 | tf_op jit(solution)/shard_map/all_to_all | solution.py:931
  389.3 6.8 %out_weights.1.refs_0_ = bf16[768,1536]{1,0:T(8,128)(2,1)} custom-call(s32[4]{0:T(128)} %pad_add_fusion.4.index, bf16[256,768]{1,0:T(8,128)(2,1)} %bitcast.73, bf16[256,768]{1,0:T(8,128)(2,1)} %copy-done.33, bf16[256,768]{1,0:T(8,128)(2,1)} %copy-done.34, bf16[128,768]{1,0:T(8,128)(2,1)} %copy-done.52, bf16[128,768]{1,0:T(8,128)(2,1)} %copy-done.53, ...), custom_call_target="tpu_custom_call" | custom-call | flops 2415919104 | bytes 7340032 | tf_op jit(solution)/shard_map/out_weights/pallas_call | solution.py:77
  400.6 6.5 %weights_z.1.refs_0_ = bf16[1536,768]{1,0:T(8,128)(2,1)} custom-call(s32[4]{0:T(128)} %pad_add_fusion.4.index, bf16[256,1536]{1,0:T(8,128)(2,1)} %bitcast.29.refs_0_, bf16[256,1536]{1,0:T(8,128)(2,1)} %collective-permute-done.40.refs_1_, bf16[256,1536]{1,0:T(8,128)(2,1)} %collective-permute-done.41.refs_2_, ...), custom_call_target="tpu_custom_call" | custom-call | flops 2415919104 | bytes 7077888 | tf_op jit(solution)/shard_map/weights_z/pallas_call | solution.py:77
  435.4 8.5 %weights_x.1 = (bf16[1536,768]{1,0:T(8,128)(2,1)}, bf16[1536,128]{1,0:T(8,128)(2,1)}, bf16[1536,256]{1,0:T(8,128)(2,1)}) custom-call(s32[4]{0:T(128)} %pad_add_fusion.4.index, bf16[256,1536]{1,0:T(8,128)(2,1)} %bitcast.29.refs_0_, bf16[256,1536]{1,0:T(8,128)(2,1)} %collective-permute-done.40.refs_1_, bf16[256,1536]{1,0:T(8,128)(2,1)} %collective-permute-done.41.refs_2_, ...), custom_call_target="tpu_custom_call" | custom-call | flops 3623878656 | bytes 9420800 | tf_op jit(solution)/shard_map/weights_x/pallas_call | solution.py:77
  466.9 6.2 %cores_x.1 = (f32[1536,768]{1,0:T(8,128)}, f32[1536,128]{1,0:T(8,128)}, f32[1536,256]{1,0:T(8,128)}) custom-call(bf16[1536,768]{1,0:T(8,128)(2,1)} %get-tuple-element.345.refs_0_, bf16[1536,128]{1,0:T(8,128)(2,1)} %get-tuple-element.346.refs_1_, bf16[1536,256]{1,0:T(8,128)(2,1)} %get-tuple-element.347.refs_2_, ...), custom_call_target="tpu_custom_call" | custom-call | bytes 14155776 | tf_op jit(solution)/shard_map/cores_x/pallas_call | solution.py:77
  (324 shorter events, 229.7 us)
Async XLA Ops:
  48.8 25.3 %collective-permute-start.6 = (bf16[256,1664]{1,0:T(8,128)(2,1)}, bf16[256,1664]{1,0:T(8,128)(2,1)S(1)}, u32[]{:S(2)}, u32[]{:S(2)}) collective-permute-start(bf16[256,1664]{1,0:T(8,128)(2,1)} %bitcast.4.do.refs_6_.refs_12_.refs_10_), channel_id=1, source_target_pairs={{0,16},{4,20},{8,24},{12,28},{16,0},{20,4},{24,8},{28,12},{1,17},{... | collective-permute-start | bytes 2555912 | tf_op jit(solution)/shard_map/ppermute | solution.py:773
  64.2 23.7 %all-to-all-start = ((bf16[4,64,1664]{2,1,0:T(8,128)(2,1)}), bf16[4,64,1664]{2,1,0:T(8,128)(2,1)S(1)}, u32[]{:S(2)}, u32[]{:S(2)}) async-start(bf16[4,64,1664]{2,1,0:T(8,128)(2,1)} %bitcast.63), calls=%async_computation | async-start | bytes 1703936 | tf_op jit(solution)/shard_map/all_to_all | solution.py:931
  69.1 209.5 %reduce-scatter.2.cloned.1.call-start = ((), (), s32[]{:S(2)}) async-start(), calls=%async_computation.7 | async-start | bytes 7077888 | tf_op jit(solution)/shard_map/reduce_scatter | solution.py:1158
  77.5 33.2 %collective-permute-start.4 = (bf16[256,1664]{1,0:T(8,128)(2,1)}, bf16[256,1664]{1,0:T(8,128)(2,1)}, u32[]{:S(2)}, u32[]{:S(2)}) collective-permute-start(bf16[256,1664]{1,0:T(8,128)(2,1)} %bitcast.4.do.refs_6_.refs_12_.refs_10_), channel_id=1, source_target_pairs={{0,4},{4,0},{8,12},{12,8},{16,20},{20,16},{24,28},{28,24},{1,5},{5... | collective-permute-start | bytes 2555912 | tf_op jit(solution)/shard_map/ppermute | solution.py:773
  77.5 33.2 %collective-permute-start.7 = (bf16[256,1664]{1,0:T(8,128)(2,1)S(1)}, bf16[256,1664]{1,0:T(8,128)(2,1)}, u32[]{:S(2)}, u32[]{:S(2)}) collective-permute-start(bf16[256,1664]{1,0:T(8,128)(2,1)S(1)} %collective-permute-done.5.refs_6_.refs_14_.refs_12_), channel_id=1, source_target_pairs={{0,4},{4,0},{8,12},{12,8},{16,20},{20,16},{24,28},{28,24},{1,5},{5... | collective-permute-start | bytes 2555912 | tf_op jit(solution)/shard_map/ppermute | solution.py:773
  78.0 32.7 %collective-permute-start.8 = (bf16[256,1664]{1,0:T(8,128)(2,1)S(1)}, bf16[256,1664]{1,0:T(8,128)(2,1)}, u32[]{:S(2)}, u32[]{:S(2)}) collective-permute-start(bf16[256,1664]{1,0:T(8,128)(2,1)S(1)} %collective-permute-done.6.refs_7_.refs_15_.refs_13_), channel_id=1, source_target_pairs={{0,4},{4,0},{8,12},{12,8},{16,20},{20,16},{24,28},{28,24},{1,5},{5... | collective-permute-start | bytes 2555912 | tf_op jit(solution)/shard_map/ppermute | solution.py:773
  165.1 28.9 %collective-permute-start.14 = (bf16[256,1664]{1,0:T(8,128)(2,1)}, bf16[256,1664]{1,0:T(8,128)(2,1)S(1)}, u32[]{:S(2)}, u32[]{:S(2)}) collective-permute-start(bf16[256,1664]{1,0:T(8,128)(2,1)} %get-tuple-element.214), channel_id=1, source_target_pairs={{0,4},{4,0},{8,12},{12,8},{16,20},{20,16},{24,28},{28,24},{1,5},{5... | collective-permute-start | bytes 2555912 | tf_op jit(solution)/shard_map/ppermute | solution.py:773
  218.2 24.3 %all-to-all-start.1 = ((bf16[4,64,1664]{2,1,0:T(8,128)(2,1)}), bf16[4,64,1664]{2,1,0:T(8,128)(2,1)S(1)}, u32[]{:S(2)}, u32[]{:S(2)}) async-start(bf16[4,64,1664]{2,1,0:T(8,128)(2,1)} %bitcast.19), calls=%async_computation.1 | async-start | bytes 1703936 | tf_op jit(solution)/shard_map/all_to_all | solution.py:931
  231.7 35.0 %collective-permute-start.32 = (bf16[128,768]{1,0:T(8,128)(2,1)S(1)}, bf16[128,768]{1,0:T(8,128)(2,1)S(1)}, u32[]{:S(2)}, u32[]{:S(2)}) collective-permute-start(bf16[128,768]{1,0:T(8,128)(2,1)S(1)} %slice.139), channel_id=1, source_target_pairs={{0,16},{4,20},{8,24},{12,28},{16,0},{20,4},{24,8},{28,12},{1,17},{... | collective-permute-start | bytes 589832 | tf_op jit(solution)/shard_map/ppermute | solution.py:773
  233.7 33.0 %collective-permute-start.33 = (bf16[128,768]{1,0:T(8,128)(2,1)S(1)}, bf16[128,768]{1,0:T(8,128)(2,1)S(1)}, u32[]{:S(2)}, u32[]{:S(2)}) collective-permute-start(bf16[128,768]{1,0:T(8,128)(2,1)S(1)} %slice.140), channel_id=1, source_target_pairs={{0,8},{4,12},{8,0},{12,4},{16,24},{20,28},{24,16},{28,20},{1,9},{5... | collective-permute-start | bytes 589832 | tf_op jit(solution)/shard_map/ppermute | solution.py:773
  278.6 33.7 %all-to-all-start.2 = ((bf16[4,64,1536]{2,1,0:T(8,128)(2,1)}), bf16[4,64,1536]{2,1,0:T(8,128)(2,1)S(1)}, u32[]{:S(2)}, u32[]{:S(2)}) async-start(bf16[4,64,1536]{2,1,0:T(8,128)(2,1)} %bitcast.64), calls=%async_computation.3 | async-start | bytes 1572864 | tf_op jit(solution)/shard_map/all_to_all | solution.py:931
  310.8 22.1 %collective-permute-start.46 = (bf16[256,1664]{1,0:T(8,128)(2,1)S(1)}, bf16[256,1664]{1,0:T(8,128)(2,1)}, u32[]{:S(2)}, u32[]{:S(2)}) collective-permute-start(bf16[256,1664]{1,0:T(8,128)(2,1)S(1)} %copy-done.2), channel_id=1, source_target_pairs={{0,8},{4,12},{8,0},{12,4},{16,24},{20,28},{24,16},{28,20},{1,9},{5... | collective-permute-start | bytes 2555912 | tf_op jit(solution)/shard_map/ppermute | solution.py:773
  315.5 51.6 %all-to-all-start.3 = ((bf16[4,64,1536]{2,1,0:T(8,128)(2,1)}), bf16[4,64,1536]{2,1,0:T(8,128)(2,1)S(1)}, u32[]{:S(2)}, u32[]{:S(2)}) async-start(bf16[4,64,1536]{2,1,0:T(8,128)(2,1)} %rows_out.1), calls=%async_computation.4 | async-start | bytes 1572864 | tf_op jit(solution)/shard_map/all_to_all | solution.py:931
  320.0 28.3 %collective-permute-start.47 = (bf16[256,1664]{1,0:T(8,128)(2,1)S(1)}, bf16[256,1664]{1,0:T(8,128)(2,1)}, u32[]{:S(2)}, u32[]{:S(2)}) collective-permute-start(bf16[256,1664]{1,0:T(8,128)(2,1)S(1)} %copy-done.2), channel_id=1, source_target_pairs={{0,16},{4,20},{8,24},{12,28},{16,0},{20,4},{24,8},{28,12},{1,17},{... | collective-permute-start | bytes 2555912 | tf_op jit(solution)/shard_map/ppermute | solution.py:773
  320.6 58.6 %collective-permute-start.40 = (bf16[256,1536]{1,0:T(8,128)(2,1)}, bf16[256,1536]{1,0:T(8,128)(2,1)}, u32[]{:S(2)}, u32[]{:S(2)}) collective-permute-start(bf16[256,1536]{1,0:T(8,128)(2,1)} %bitcast.29.refs_0_), channel_id=1, source_target_pairs={{0,8},{4,12},{8,0},{12,4},{16,24},{20,28},{24,16},{28,20},{1,9},{5... | collective-permute-start | bytes 2359304 | tf_op jit(solution)/shard_map/ppermute | solution.py:773
  322.0 57.2 %collective-permute-start.41 = (bf16[256,1536]{1,0:T(8,128)(2,1)}, bf16[256,1536]{1,0:T(8,128)(2,1)}, u32[]{:S(2)}, u32[]{:S(2)}) collective-permute-start(bf16[256,1536]{1,0:T(8,128)(2,1)} %bitcast.29.refs_0_), channel_id=1, source_target_pairs={{0,16},{4,20},{8,24},{12,28},{16,0},{20,4},{24,8},{28,12},{1,17},{... | collective-permute-start | bytes 2359304 | tf_op jit(solution)/shard_map/ppermute | solution.py:773
  322.6 33.2 %collective-permute-start.38 = (bf16[256,768]{1,0:T(8,128)(2,1)S(1)}, bf16[256,768]{1,0:T(8,128)(2,1)S(1)}, u32[]{:S(2)}, u32[]{:S(2)}) collective-permute-start(bf16[256,768]{1,0:T(8,128)(2,1)S(1)} %bitcast.68), channel_id=1, source_target_pairs={{0,8},{4,12},{8,0},{12,4},{16,24},{20,28},{24,16},{28,20},{1,9},{5... | collective-permute-start | bytes 1179656 | tf_op jit(solution)/shard_map/ppermute | solution.py:773
  332.9 34.1 %collective-permute-start.39 = (bf16[256,768]{1,0:T(8,128)(2,1)S(1)}, bf16[256,768]{1,0:T(8,128)(2,1)S(1)}, u32[]{:S(2)}, u32[]{:S(2)}) collective-permute-start(bf16[256,768]{1,0:T(8,128)(2,1)S(1)} %bitcast.69), channel_id=1, source_target_pairs={{0,16},{4,20},{8,24},{12,28},{16,0},{20,4},{24,8},{28,12},{1,17},{... | collective-permute-start | bytes 1179656 | tf_op jit(solution)/shard_map/ppermute | solution.py:773
  351.7 35.4 %collective-permute-start.48 = (bf16[128,1664]{1,0:T(8,128)(2,1)S(1)}, bf16[128,1664]{1,0:T(8,128)(2,1)}, u32[]{:S(2)}, u32[]{:S(2)}) collective-permute-start(bf16[128,1664]{1,0:T(8,128)(2,1)S(1)} %slice.143), channel_id=1, source_target_pairs={{0,16},{4,20},{8,24},{12,28},{16,0},{20,4},{24,8},{28,12},{1,17},{... | collective-permute-start | bytes 1277960 | tf_op jit(solution)/shard_map/ppermute | solution.py:773
  355.8 31.4 %collective-permute-start.49 = (bf16[128,1664]{1,0:T(8,128)(2,1)S(1)}, bf16[128,1664]{1,0:T(8,128)(2,1)}, u32[]{:S(2)}, u32[]{:S(2)}) collective-permute-start(bf16[128,1664]{1,0:T(8,128)(2,1)S(1)} %slice.144), channel_id=1, source_target_pairs={{0,8},{4,12},{8,0},{12,4},{16,24},{20,28},{24,16},{28,20},{1,9},{5... | collective-permute-start | bytes 1277960 | tf_op jit(solution)/shard_map/ppermute | solution.py:773
  373.6 33.5 %all-to-all-start.4 = ((bf16[4,64,1536]{2,1,0:T(8,128)(2,1)}), bf16[4,64,1536]{2,1,0:T(8,128)(2,1)S(1)}, u32[]{:S(2)}, u32[]{:S(2)}) async-start(bf16[4,64,1536]{2,1,0:T(8,128)(2,1)} %bitcast.65), calls=%async_computation.5 | async-start | bytes 1572864 | tf_op jit(solution)/shard_map/all_to_all | solution.py:931
  407.2 36.7 %collective-permute-start.61 = (bf16[768,1536]{1,0:T(8,128)(2,1)}, bf16[768,1536]{1,0:T(8,128)(2,1)}, u32[]{:S(2)}, u32[]{:S(2)}) collective-permute-start(bf16[768,1536]{1,0:T(8,128)(2,1)} %out_weights.1.refs_0_), channel_id=1, source_target_pairs={{0,4},{4,0},{8,12},{12,8},{16,20},{20,16},{24,28},{28,24},{1,5},{5... | collective-permute-start | bytes 7077896 | tf_op jit(solution)/shard_map/ppermute | solution.py:773
  407.3 41.7 %collective-permute-start.60 = (bf16[1536,768]{1,0:T(8,128)(2,1)}, bf16[1536,768]{1,0:T(8,128)(2,1)}, u32[]{:S(2)}, u32[]{:S(2)}) collective-permute-start(bf16[1536,768]{1,0:T(8,128)(2,1)} %weights_z.1.refs_0_), channel_id=1, source_target_pairs={{0,4},{4,0},{8,12},{12,8},{16,20},{20,16},{24,28},{28,24},{1,5},{5... | collective-permute-start | bytes 7077896 | tf_op jit(solution)/shard_map/ppermute | solution.py:773
  410.7 43.4 %all-to-all-start.5 = ((bf16[4,64,1536]{2,1,0:T(8,128)(2,1)}), bf16[4,64,1536]{2,1,0:T(8,128)(2,1)S(1)}, u32[]{:S(2)}, u32[]{:S(2)}) async-start(bf16[4,64,1536]{2,1,0:T(8,128)(2,1)} %rows_three.1), calls=%async_computation.6 | async-start | bytes 1572864 | tf_op jit(solution)/shard_map/all_to_all | solution.py:931
  (105 other events, 926.2 us)
Sparse Core Ops, SparseCore 0:
  218.3 60.2 reduce-scatter.1

commit v3 on v2

--- a/solution.py
+++ b/solution.py
@@ -93,6 +93,11 @@
     return lax.dot_general(a, b, dims, precision=HIGHEST, preferred_element_type=F32)
 
 
+def fine(a, b, dims=NN):
+    high, low = two_terms(a)
+    return dot(high, b, dims) + dot(low, b, dims)
+
+
 def sigmoid(v):
     return 1.0 / (1.0 + jnp.exp(-v))
 
@@ -110,8 +115,12 @@
     return jnp.concatenate([v, jnp.zeros((v.shape[0], LANES - v.shape[1]), v.dtype)], axis=1)
 
 
+def to_rows(v):
+    return jnp.concatenate([v, jnp.zeros((LANES - v.shape[0], v.shape[1]), v.dtype)], axis=0)
+
+
 def spread_matrix(width):
-    return (iota((LANES, width), 1) // HEAD_DIM == iota((LANES, width), 0)).astype(F32)
+    return (iota((LANES, width), 1) // HEAD_DIM == iota((LANES, width), 0)).astype(BF16)
 
 
 def prepared(xbc, dt, conv_x, conv_bc, head_par, meta):
@@ -169,12 +178,12 @@
     o_norm[...] = own
     o_xbc[:, :width] = dot(normed, wx[...]).astype(BF16)
     o_xbc[:, width:] = dot(normed, wbc[...]).astype(BF16)
-    o_dt[...] = to_lanes(dot(own, wdt[...]))
+    o_dt[...] = to_lanes(dot(own, wdt[...], NT))
     o_z[...] = dot(own, wz[...])
     p = prepared(o_xbc, o_dt, conv_x, conv_bc, head_par, meta)
     rows = own.shape[0]
     last = p["cum"][rows - 1 : rows]
-    weight = exact(p["step"] * jnp.exp(last - p["cum"]), spread_matrix(width))
+    weight = fine(p["step"] * jnp.exp(last - p["cum"]), spread_matrix(width))
     decay = jnp.exp(last)
     pack_state(o_send, dot(p["xs"] * weight, p["b"], TN), decay)
     o_tot[...] = jnp.broadcast_to(decay, o_tot.shape)
@@ -205,7 +214,7 @@
     ahead = iota((rows, rows), 0) >= iota((rows, rows), 1)
     cum_t = cum.T
     scores = dot(p["c"], p["b"], NT)
-    spread_out = exact(
+    spread_out = fine(
         jnp.concatenate([p["step"], jnp.exp(cum), jnp.broadcast_to(p["skip"], (8, LANES))], axis=0), spread
     )
     xw = xs * spread_out[:rows]
@@ -286,7 +295,7 @@
     ahead = iota((rows, rows), 0) >= iota((rows, rows), 1)
     cum_t = cum.T
     scores = dot(p["c"], p["b"], NT)
-    xw = p["xs"] * exact(p["step"], spread_matrix(width))
+    xw = p["xs"] * fine(p["step"], spread_matrix(width))
     low, high = pair_masks(rows)
     lane = iota((rows, LANES), 1)
     sub = iota((LANES, rows), 0)
@@ -324,7 +333,7 @@
     rows = cum.shape[0]
     spread = spread_matrix(width)
     last = cum[rows - 1 : rows]
-    spread_out = exact(
+    spread_out = fine(
         jnp.concatenate(
             [step, jnp.exp(cum), jnp.exp(last - cum), jnp.broadcast_to(p["skip"], (8, LANES))], axis=0
         ),
@@ -342,8 +351,9 @@
     to_state = rem_x * dot(b, h1, NT)
     dxw = dxw0[...] + to_state
     db = db0[...] + dot(xw * rem_x, h1)
-    dtotal = jnp.sum(exact(spread, h1 * h0), axis=1, keepdims=True)
-    sums = exact(jnp.concatenate([from_state, xw * to_state, dxw * xs, dyv * xs], axis=0), spread, NT)
+    high, low = two_terms(h1 * h0)
+    dtotal = jnp.sum(dot(spread, high) + dot(spread, low), axis=1, keepdims=True)
+    sums = fine(jnp.concatenate([from_state, xw * to_state, dxw * xs, dyv * xs], axis=0), spread, NT)
     flow = sums[rows : 2 * rows]
     dlast = jnp.broadcast_to(dtotal, (LANES, LANES)).T[0:1] * jnp.exp(last) + jnp.sum(
         flow, axis=0, keepdims=True
@@ -392,7 +402,7 @@
     o_dx[to, :width] = dx
     o_dx[to, width:] = ddt[...]
     o_bc[to, :] = dbc
-    dn = dn0[...] + dot(dx, wx[...], NT) + dot(dbc, wbc[...], NT) + dot(ddt[...], to_lanes(wdt[...]), NT)
+    dn = dn0[...] + dot(dx, wx[...], NT) + dot(dbc, wbc[...], NT) + dot(ddt[...], to_rows(wdt[...]))
     o_part[...] = dn.astype(BF16)
     x = tok[FRONT:, :].astype(F32)
     scale = lax.rsqrt(jnp.mean(x * x, axis=-1, keepdims=True) + EPSILON)
@@ -451,13 +461,13 @@
 
 def k_rows_two(dout, two, residual, mixer, scales, gains, router, arrived, o_dm, o_dr, o_small):
     model = two.shape[1]
-    experts = router.shape[1]
+    experts = router.shape[0]
     both = total_of(arrived)
     dn2, dgate = both[:, :model], both[:, model:]
-    w = to_lanes(router[...])
-    probs = masked_softmax(dot(two[...], w), dout[:, model:].astype(F32))
+    w = to_rows(router[...])
+    probs = masked_softmax(dot(two[...], w, NT), dout[:, model:].astype(F32))
     dlog = (probs * (dgate - jnp.sum(probs * dgate, axis=-1, keepdims=True))).astype(BF16)
-    dn2 = dn2 + dot(dlog, w, NT)
+    dn2 = dn2 + dot(dlog, w)
     scale, scale_two = scales[:, 0:1], scales[:, 1:2]
     scaled = residual[...] * scale_two
     o_small[:experts, :] = dot(dlog, two[...], TN)[:experts]
@@ -474,9 +484,14 @@
 
 
 def k_rows_out(residual, arrived, o):
-    out = (residual[...] + total_of(arrived)).astype(BF16)
-    for k in range(o.shape[0]):
-        o[k] = out
+    o[...] = (residual[...] + total_of(arrived)).astype(BF16)
+
+
+def k_assemble(at, *refs):
+    o = refs[-1]
+    share = refs[0].shape[0]
+    for k, r in enumerate(refs[:-1]):
+        o[pl.ds(pl.multiple_of(at[k] * share, share), share), :] = r[...]
 
 
 def k_rows_three(tok, dr, gains, arrived, o):
@@ -545,18 +560,20 @@
 
 def k_expert(slots, with_shared, index, *refs):
     mine, router, w_in, w_down = refs[:4]
-    pieces, count = sum(slots), len(slots)
-    xs, ds = refs[4 : 4 + pieces], refs[4 + pieces : 4 + 2 * pieces]
-    shared = refs[4 + 2 * pieces : 6 + 2 * pieces] if with_shared else ()
+    slots, d_slots = slots
+    pieces, d_pieces, count = sum(slots), sum(d_slots), len(slots)
+    xs, ds = refs[4 : 4 + pieces], refs[4 + pieces : 4 + pieces + d_pieces]
+    at = 4 + pieces + d_pieces
+    shared = refs[at : at + 2] if with_shared else ()
     refs = refs[len(refs) - 9 - 2 * count :]
     o_all, outs = refs[0], refs[1 : 1 + 2 * count]
     x_buf, d_buf, out_buf, dx_buf, keep_buf, x_sem, d_sem, o_sem = refs[1 + 2 * count :]
     rows = x_buf.shape[0] // count
     x_copies = piece_copies(xs, slots, x_buf, x_sem)
-    d_copies = piece_copies(ds, slots, d_buf, d_sem)
+    d_copies = piece_copies(ds, d_slots, d_buf, d_sem)
     width = w_in.shape[2]
     wg, wu, wd = w_in[0, 0], w_in[0, 1], w_down[0]
-    w = to_lanes(router[...])
+    w = to_rows(router[...])
     half = wg.shape[1]
     stores = []
     for i in range(count):
@@ -566,7 +583,7 @@
         do = d_buf[at, :width]
         mask = d_buf[at, width:].astype(F32)
         lane = iota(mask.shape, 1)
-        probs = masked_softmax(dot(x, w), mask)
+        probs = masked_softmax(dot(x, w, NT), mask)
         gate = jnp.sum(jnp.where(lane == mine[0], probs, 0.0), axis=-1, keepdims=True)
         hg, dg, du, dgate = mlp(x, do, wg, wu, wd, gate)
         dx = dot(dg, wg, NT) + dot(du, wu, NT)
@@ -656,12 +673,13 @@
     weight_products(x_buf, d_buf, keep_buf, in_buf, down_buf, o_in, o_down, o_sem)
 
 
-def k_outer(groups, cuts, index, *refs):
+def k_outer(groups, small, index, *refs):
     counts = [sum(g) for g in groups]
     total = sum(counts)
-    outs = refs[total : total + len(cuts)]
-    a_buf, b_buf, o_buf, sem, o_sem = refs[total + len(cuts) :]
+    o = refs[total]
+    a_buf, b_buf, o_buf, sem, o_sem = refs[total + 1 + small : total + 6 + small]
     copies, at, column = [], 0, 0
+    tails = []
     for g, slots in enumerate(groups):
         pieces = refs[at : at + counts[g]]
         width = pieces[0].shape[1]
@@ -669,6 +687,28 @@
         column += 0 if g == 0 else width
         copies += piece_copies(pieces, slots, buffer, sem.at[pl.ds(at, counts[g])])
         at += counts[g]
+        if small and g > 0:
+            rows = a_buf.shape[0] // len(slots)
+            first = 0
+            for n in slots:
+                piece = pieces[first + n - 1]
+                tails.append((piece, rows // n, column - width, width))
+                first += n
+    if small:
+        o_small, t_buf, t_sem = refs[total + 1], refs[-2], refs[-1]
+        moves = []
+        for k, (piece, begin, to, width) in enumerate(tails):
+            size = piece.shape[0] - begin
+            into = t_buf.at[k % len(groups[0]), pl.ds(0, size), pl.ds(to, width)]
+            moves.append((piece.at[pl.ds(begin, size)], into, t_sem.at[k]))
+        finish(start_all(moves))
+        for k in (0, len(groups[0])):
+            piece, begin, to, width = tails[k]
+            size = piece.shape[0] - begin
+            o_small[:, to : to + width] = jnp.zeros((o_small.shape[0], width), F32)
+            o_small[:size, to : to + width] = sum(
+                t_buf[j, :size, to : to + width].astype(F32) for j in range(len(groups[0]))
+            )
     for c in copies:
         finish(c)
     step = 256
@@ -676,19 +716,20 @@
     for c in range(a_buf.shape[1] // step):
         at = pl.ds(c * step, step)
         o_buf[at, :] = dot(a_buf[:, at], b_buf[...], TN).astype(BF16)
-        stores += store_in_cuts(o_buf, at, cuts, outs, o_sem, len(cuts) * c)
+        stores += start_all([(o_buf.at[at], o.at[at], o_sem.at[c])])
     finish(stores)
 
 
-def outer(a, bs, widths, rows, name):
+def outer(a, bs, rows, name, small=0):
     columns = a.pieces[0].shape[1]
-    total = sum(widths)
-    cuts = [(sum(widths[:i]), w) for i, w in enumerate(widths)]
+    total = sum(b.pieces[0].shape[1] for b in bs)
     pieces = [p for g in (a, *bs) for p in g.pieces]
+    blocks = len(a.slots)
     dma = pltpu.SemaphoreType.DMA
+    more = [pltpu.VMEM((blocks, small, total), BF16), dma((blocks * len(bs),))] if small else []
     return call(
-        functools.partial(k_outer, [g.slots for g in (a, *bs)], cuts),
-        [Far(struct((columns, w), BF16)) for w in widths],
+        functools.partial(k_outer, [g.slots for g in (a, *bs)], int(small > 0)),
+        [Far(struct((columns, total), BF16)), *([struct((small, total), F32)] if small else [])],
         [Far(p) for p in pieces],
         2 * rows * columns * total,
         name,
@@ -698,18 +739,19 @@
             pltpu.VMEM((rows, total), BF16),
             pltpu.VMEM((columns, total), BF16),
             dma((len(pieces),)),
-            dma((len(widths) * (columns // 256),)),
+            dma((columns // 256,)),
+            *more,
         ],
     )
 
 
-def k_out_weights(slots, index, *refs):
-    n = sum(slots)
-    us, ds = refs[:n], refs[n : 2 * n]
-    o, u_buf, d_buf, o_buf, u_sem, d_sem, o_sem = refs[2 * n :]
+def k_out_weights(slots, d_slots, index, *refs):
+    n, total = sum(slots), sum(slots) + sum(d_slots)
+    us, ds = refs[:n], refs[n:total]
+    o, u_buf, d_buf, o_buf, u_sem, d_sem, o_sem = refs[total:]
     model = o.shape[1]
     u_copies = piece_copies(us, slots, u_buf, u_sem)
-    d_copies = piece_copies(ds, slots, d_buf, d_sem)
+    d_copies = piece_copies(ds, d_slots, d_buf, d_sem)
     rows = d_buf.shape[0] // len(slots)
     for i in range(len(slots)):
         finish(u_copies[i] + d_copies[i])
@@ -727,10 +769,9 @@
 
 def out_weights(u, d, rows):
     width, model = u.pieces[0].shape[1], d.pieces[0].shape[1] - LANES
-    n = len(u.pieces)
     dma = pltpu.SemaphoreType.DMA
     [out] = call(
-        functools.partial(k_out_weights, u.slots),
+        functools.partial(k_out_weights, u.slots, d.slots),
         [Far(struct((width, model), BF16))],
         [Far(p) for p in (*u.pieces, *d.pieces)],
         2 * rows * width * model,
@@ -740,32 +781,62 @@
             pltpu.VMEM((rows, width), BF16),
             pltpu.VMEM((rows, model + LANES), BF16),
             pltpu.VMEM((width, model), BF16),
-            dma((n,)),
-            dma((n,)),
+            dma((len(u.pieces),)),
+            dma((len(d.pieces),)),
             dma((width // 256,)),
         ],
     )
     return out
 
 
-def k_pair(*refs):
-    half = len(refs) // 3
-    for a, b, o in zip(refs[:half], refs[half : 2 * half], refs[2 * half :]):
-        o[...] = a[...].astype(F32) + b[...].astype(F32)
-
-
-def both_cores(arrays, name):
+def k_pair(widths, a, b, *refs):
+    outs = refs[: len(widths)]
+    a_buf, b_buf = refs[len(widths) : len(widths) + 2]
+    bufs, sem, o_sem = refs[len(widths) + 2 : -2], refs[-2], refs[-1]
+    steps = sem.shape[0] // 2
+    rows = a_buf.shape[0] // steps
+    loads = [
+        start_all(
+            (src.at[pl.ds(i * rows, rows)], buf.at[pl.ds(i * rows, rows)], sem.at[2 * i + j])
+            for j, (src, buf) in enumerate(((a, a_buf), (b, b_buf)))
+        )
+        for i in range(steps)
+    ]
+    stores = []
+    for i in range(steps):
+        finish(loads[i])
+        at = pl.ds(i * rows, rows)
+        first = 0
+        for k, (o, buf, w) in enumerate(zip(outs, bufs, widths)):
+            total = a_buf[at, first : first + w].astype(F32) + b_buf[at, first : first + w].astype(F32)
+            first += w
+            where = (slice(None), at) if w == LANES else (at,)
+            buf[where if w == LANES else (at, slice(None))] = total.T if w == LANES else total
+            stores += start_all([(buf.at[where], o.at[where], o_sem.at[len(widths) * i + k])])
+    finish(stores)
+
+
+def both_cores(array, widths, name):
     if lax.axis_size("seq") != 8:
-        return [a.astype(F32) for a in arrays]
-    others = [flip(a, "seq", 1) for a in arrays]
-    steps = 4
+        outs = jnp.split(array.astype(F32), [sum(widths[:i]) for i in range(1, len(widths))], axis=1)
+        return [o.T if w == LANES else o for o, w in zip(outs, widths)]
+    rows = array.shape[0]
+    steps = rows // 256
+    shapes = [(w, rows) if w == LANES else (rows, w) for w in widths]
+    dma = pltpu.SemaphoreType.DMA
     return call(
-        k_pair,
-        [Rows(struct(a.shape, F32), a.shape[0] // steps) for a in arrays],
-        [Rows(a, a.shape[0] // steps) for a in (*arrays, *others)],
+        functools.partial(k_pair, widths),
+        [Far(struct(shape, F32)) for shape in shapes],
+        [Far(array), Far(flip(array, "seq", 1))],
         0,
         name,
-        grid=steps,
+        scratch=[
+            pltpu.VMEM(array.shape, BF16),
+            pltpu.VMEM(array.shape, BF16),
+            *(pltpu.VMEM(shape, F32) for shape in shapes),
+            dma((2 * steps,)),
+            dma((len(widths) * steps,)),
+        ],
     )
 
 
@@ -781,14 +852,6 @@
     def __init__(self, pieces, slots, index):
         self.pieces, self.slots, self.index = pieces, slots, index
 
-    def tails(self, first, half):
-        out, at = [], 0
-        for pieces in self.slots:
-            last = self.pieces[at + pieces - 1]
-            out.append(last[first - half * (pieces - 1) :])
-            at += pieces
-        return out
-
     def part(self, first, last):
         at, to = sum(self.slots[:first]), sum(self.slots[:last])
         return Gathered(self.pieces[at:to], self.slots[first:last], self.index[first:last])
@@ -797,33 +860,55 @@
 XOR_ORDER = (0, 1, 2, 4, 3, 5, 6, 7)
 
 
-def gather(own, half, cores=True, between=(None, None)):
-    size = lax.axis_size("seq")
-    place = lax.axis_index("seq")
-    if size != 8:
-        every = lax.all_gather(own, "seq")
-        return Gathered([every[k] for k in range(size)], [1] * size, jnp.arange(size, dtype=jnp.int32))
+def gather_all(own):
+    every = lax.all_gather(own, "seq")
+    size = every.shape[0]
+    return Gathered([every[k] for k in range(size)], [1] * size, jnp.arange(size, dtype=jnp.int32))
+
+
+def gather(own, half, between):
+    if lax.axis_size("seq") != 8:
+        return gather_all(own)
     core, x, y = bits_of("seq")
     by_x = flip(own, "seq", x)
     by_y = flip(own, "seq", y)
-    first_far = []
-    if between[0] is not None and not cores:
-        by_x, by_y = after((by_x, by_y), between[0])
-    elif between[0] is not None:
-        first_far = [flip(own, "seq", core)]
-        by_x, by_y = after((by_x, by_y), between[0](own, first_far[0]))
+    far = [flip(own, "seq", core)]
+    by_x, by_y = after((by_x, by_y), between[0](own, far[0]))
     top = flip(by_x[:half], "seq", y)
     bottom = flip(by_y[half:], "seq", x)
-    if between[1] is not None:
-        first_far += [flip(by_x, "seq", core), flip(by_y, "seq", core)]
-        top, bottom = after((top, bottom), between[1](by_x, by_y))
-    near = [own, by_x, by_y, top, bottom]
-    if not cores:
-        index = jnp.stack([place ^ k for k in (0, x, y, x | y)]).astype(jnp.int32)
-        return Gathered(near, [1, 1, 1, 2], index)
-    far = first_far + [flip(a, "seq", core) for a in near[len(first_far) :]]
+    far += [flip(by_x, "seq", core), flip(by_y, "seq", core)]
+    top, bottom = after((top, bottom), between[1](by_x, by_y))
+    far += [flip(top, "seq", core), flip(bottom, "seq", core)]
     pieces = [own, far[0], by_x, by_y, far[1], far[2], top, bottom, far[3], far[4]]
     return Gathered(pieces, [1, 1, 1, 1, 1, 1, 2, 2], xor_index())
+
+
+def near_index():
+    core, x, y = bits_of("seq")
+    return jnp.stack([lax.axis_index("seq") ^ k for k in (0, x, y, x | y)]).astype(jnp.int32)
+
+
+def gather_near(own, half, wait, first=None):
+    if lax.axis_size("seq") != 8:
+        return gather_all(own)
+    core, x, y = bits_of("seq")
+    by_x, by_y = after(first or first_hop(own), wait)
+    near = [own, by_x, by_y, flip(by_x[:half], "seq", y), flip(by_y[half:], "seq", x)]
+    return Gathered(near, [1, 1, 1, 2], near_index())
+
+
+def first_hop(own):
+    core, x, y = bits_of("seq")
+    return flip(own, "seq", x), flip(own, "seq", y)
+
+
+def gather_lean(own, wait, along_x, first=None):
+    if lax.axis_size("seq") != 8:
+        return gather_all(own)
+    core, x, y = bits_of("seq")
+    by_x, by_y = first or first_hop(own)
+    diagonal = flip(after(by_y, wait), "seq", x) if along_x else flip(after(by_x, wait), "seq", y)
+    return Gathered([own, by_x, by_y, diagonal], [1, 1, 1, 1], near_index())
 
 
 def xor_index():
@@ -891,7 +976,7 @@
     return out
 
 
-def scan(send, backward, name, between=None, steps=None):
+def scan(send, backward, name, beside=(None, None, None), steps=None):
     place = lax.axis_index("seq")
     seqs, size = send.shape[0], send.shape[1] - FRONT
     bits = bits_of("seq")
@@ -903,8 +988,9 @@
         is_set = (place & bit) != 0
         ahead = (jnp.logical_not(is_set) if backward else is_set).astype(jnp.int32)[None]
         last = bit == bits[-1]
-        if last and between is not None:
-            recv = after(recv, between)
+        wait = beside[min(bit.bit_length() - 1, 2)]
+        if wait is not None:
+            recv = after(recv, wait)
         outs = [state] if last else [state, row, struct(send.shape, BF16)]
         made = call(
             functools.partial(k_scan, not held, last),
@@ -999,7 +1085,7 @@
             both(width + FRONT, LANES, dtype=BF16),
             both(8, LANES),
         ],
-        [Each(tok_front), norm_gains, in_z, in_x, in_bc, in_dt, *small],
+        [Each(tok_front), norm_gains, in_z, in_x, in_bc, in_dt.T, *small],
         2 * rows * model * (2 * width + bc + LANES),
         "mixer_in",
         grid=seqs,
@@ -1032,28 +1118,30 @@
         0,
         "rows_one",
     )
-    d_got = gather(d_ext, piece, between=(lambda *_: entering, lambda *_: two_own))
+    d_got = gather(d_ext, piece, (lambda *_: entering, lambda *_: two_own))
     two = gather_mp(two_own)
 
     mine = ((seq_at * n_mp + mp_at) // 2).astype(jnp.int32)[None]
+
+    x_slots = [1] * (n_seq - 2) + ([2, 2] if n_seq == 8 else [1, 1])
 
     def expert(pieces, first, last, o_all, shared=()):
         part_d = d_got.part(first, last)
-        slots, index = part_d.slots, part_d.index
-        count = len(slots)
+        index, count = part_d.index, last - first
+        slots = x_slots[first:last]
         size = rows * count
         return call(
-            functools.partial(k_expert, slots, bool(shared)),
+            functools.partial(k_expert, (slots, part_d.slots), bool(shared)),
             [Far(struct((n_seq * rows, model), BF16))]
             + [Far(struct((rows, model + LANES), BF16)), Far(struct((rows, 3 * half), BF16))] * count,
             [
-                Scalars(mine), router, expert_in, expert_down, *(Far(p) for p in (*pieces, *part_d.pieces)),
+                Scalars(mine), router.T, expert_in, expert_down, *(Far(p) for p in (*pieces, *part_d.pieces)),
                 *shared, *(Far(o) for o in o_all),
             ],
             2 * size * model * half * 6.5,
             "experts",
             index=index,
-            aliases={5 + 2 * len(pieces): 0} if o_all else None,
+            aliases={5 + len(pieces) + len(part_d.pieces): 0} if o_all else None,
             scratch=[
                 pltpu.VMEM((size, model), BF16),
                 pltpu.VMEM((size, model + LANES), BF16),
@@ -1061,7 +1149,7 @@
                 pltpu.VMEM((size, model + LANES), BF16),
                 pltpu.VMEM((size, 3 * half), BF16),
                 dma((len(pieces),)),
-                dma((len(pieces),)),
+                dma((len(part_d.pieces),)),
                 dma((3 * count,)),
             ],
         )
@@ -1079,18 +1167,20 @@
 
     def near_experts(own, far):
         made.append(expert([own, far], 0, 2, [], shared_of(own)))
-        return made
+        return made[-1][1:]
 
     def chip_experts(by_x, by_y):
         made.append(expert([by_x, by_y], 2, 4, made[-1][:1]))
-        return made[-1]
+        return made[-1][1:]
 
     if n_seq == 8:
+        normed, u = normed.reshape(rows, model), u.reshape(rows, width)
+        n_first = first_hop(after(normed, part))
         two, d_got.pieces = lax.optimization_barrier((two, d_got.pieces))
-        x_got = gather(two, piece, between=(near_experts, chip_experts))
+        x_got = gather(two, piece, (near_experts, chip_experts))
         made.append(expert(x_got.pieces[4:], 4, 8, made[-1][:1]))
     else:
-        x_got = gather(two, piece)
+        x_got = gather_all(two)
         out_shared, dx_shared = shared_of(two)
         for i in range(0, n_seq, 4):
             made.append(expert(x_got.part(i, i + 4).pieces, i, i + 4, made[-1][:1] if made else []))
@@ -1161,19 +1251,19 @@
     dm_own, d_residual, g_two = call(
         k_rows_two,
         [struct((share, model + LANES), BF16), of_rows, struct((experts + 8, model), F32)],
-        [d_own, two_own, residual, mixer_own, scales, norm_gains, router, arrived],
+        [d_own, two_own, residual, mixer_own, scales, norm_gains, router.T, arrived],
         0,
         "rows_two",
     )
     dm = gather_mp(dm_own)
     if n_seq == 8:
-        n_got = gather(after(normed, part).reshape(rows, model), piece, False, (dx_sum, None))
+        n_got = gather_near(normed, piece, dx_sum, n_first)
+        u = after(u, dx_sum)
+        dm, u_first = lax.optimization_barrier((dm, first_hop(u)))
     else:
         normed, u = after((normed, u), (dm, g_expert_in, g_shared_in))
-        n_got = gather(normed.reshape(rows, model), piece, False)
-    u_got = gather(after(u, dx_sum).reshape(rows, width), piece, False)
-    if n_seq == 8:
-        dm, u_got.pieces = lax.optimization_barrier((dm, u_got.pieces))
+        n_got = gather_all(normed.reshape(rows, model))
+        u_got = gather_all(u.reshape(rows, width))
 
     dz, dy, send, g_gn = call(
         k_back_gate,
@@ -1198,12 +1288,10 @@
     )
     dxw0, db0, dc0, dcum0, dn0 = intra_back
     steps = []
-    leaving = scan(send, True, "scan_back", intra_back, steps)
-    dz_got = gather(after(dz, leaving).reshape(rows, width), piece, False)
-    dm_got = gather(after(dm, leaving), piece, False)
-    out_arrived = to_shares(after(out_sum, steps[0]))
-    [out_own] = call(k_rows_out, [struct((n_mp, share, model), BF16)], [residual, out_arrived], 0, "rows_out")
-    out_rows = exchange_mp(out_own)
+    dm_first = first_hop(dm) if n_seq == 8 else None
+    leaving = scan(send, True, "scan_back", (None, None, (intra_back, dm_first)), steps)
+    out_arrived = to_shares(after(out_sum, steps[1]))
+    dz_first = first_hop(after(dz, leaving).reshape(rows, width)) if n_seq == 8 else None
 
     def in_order(rows):
         return jnp.transpose(rows.reshape(seqs, piece, model), (1, 0, 2)).astype(F32)
@@ -1226,8 +1314,7 @@
     )
     edge = passed_along(d_xbc[:, :FRONT], "seq", -1)
     if n_seq == 8:
-        edge, dz_got.pieces[1:3], out_rows = lax.optimization_barrier((edge, dz_got.pieces[1:3], out_rows))
-    output = in_order(out_rows)
+        edge, out_arrived, dz_first = lax.optimization_barrier((edge, out_arrived, dz_first))
     dx, d_bc, part = call(
         k_back_in,
         [
@@ -1237,7 +1324,7 @@
         ],
         [
             Each(dn0), Each(d_xbc), Each(edge), Each(d_dt), Each(tok_front), g_conv, g_hp, g_gn, g_two,
-            in_x, in_bc, in_dt,
+            in_x, in_bc, in_dt.T,
         ],
         2 * rows * (width + bc + LANES) * model,
         "back_in",
@@ -1245,24 +1332,31 @@
         scratch=[pltpu.VMEM((8, model), F32)],
     )
     arrived = to_shares(part.reshape(rows, model))
+    [out_own] = call(
+        k_rows_out, [struct((share, model), BF16)], [residual, after(out_arrived, part)], 0, "rows_out"
+    )
+    out_shares = [out_own if k == 0 else flip(out_own, "mp", k) for k in range(n_mp)]
+    dm_got = gather_near(dm, piece, leaving, dm_first)
+    if n_seq == 8:
+        u_got = gather_near(u, piece, leaving, u_first)
+    dz_got = gather_near(dz.reshape(rows, width), piece, part, dz_first)
     *head_bits, last_bit = bits_of("mp")
     for bit in head_bits:
         d_bc = low_sum(d_bc, flip(d_bc, "mp", bit))
     d_bc = low_sum(d_bc, flip(d_bc, "mp", last_bit))
-    bc_got = gather(d_bc, piece, False)
-    dx_got = gather(dx, piece, False)
-
-    g_in_z = g_in_x = g_dt = g_in_bc = g_out_w = 0.0
+    bc_got = gather_lean(d_bc, d_bc, False)
+    dx_first = first_hop(dx) if n_seq == 8 else None
+    if n_seq != 8:
+        dx_got = gather_all(dx)
+
+    g_in_z = g_in_x = g_out_w = small = 0.0
     size = min(8, len(n_got.slots))
     for first in range(0, len(n_got.slots), size):
         last = first + size
-        [a] = outer(n_got.part(first, last), [dz_got.part(first, last)], [width], size * rows, "weights_z")
-        g_in_z = g_in_z + a
         g_out_w = g_out_w + out_weights(u_got.part(first, last), dm_got.part(first, last), size * rows)
     if n_seq == 8:
-        arrived, g_in_z, g_out_w, d_bc, dx_got.pieces[1:3] = lax.optimization_barrier(
-            (arrived, g_in_z, g_out_w, d_bc, dx_got.pieces[1:3])
-        )
+        arrived, g_out_w, d_bc, dx_first = lax.optimization_barrier((arrived, g_out_w, d_bc, dx_first))
+        dx_got = gather_near(dx, piece, (), dx_first)
     [rows_own] = call(
         k_rows_three,
         [struct((n_mp, share, model), BF16)],
@@ -1271,27 +1365,32 @@
         "rows_three",
     )
     rows_all = exchange_mp(rows_own)
-    [g_in_z] = both_cores([g_in_z], "cores_z")
-    [g_out_w] = both_cores([g_out_w], "cores_out")
     for first in range(0, len(n_got.slots), size):
         last = first + size
-        a, b, c = outer(
-            n_got.part(first, last), [dx_got.part(first, last), bc_got.part(first, last)], [width, LANES, bc],
-            size * rows, "weights_x",
+        [a] = outer(n_got.part(first, last), [dz_got.part(first, last)], size * rows, "weights_z")
+        g_in_z = g_in_z + a
+    [g_in_z] = both_cores(g_in_z, [width], "cores_z")
+    [g_out_w] = both_cores(g_out_w, [model], "cores_out")
+    for first in range(0, len(n_got.slots), size):
+        last = first + size
+        a, b = outer(
+            n_got.part(first, last), [dx_got.part(first, last), bc_got.part(first, last)], size * rows, "weights_x",
+            beside,
         )
-        g_in_x, g_dt, g_in_bc = g_in_x + a, g_dt + b, g_in_bc + c
+        g_in_x, small = g_in_x + a, small + b
+    order = after(jnp.stack([mp_at ^ k for k in range(n_mp)]).astype(jnp.int32), g_in_x)
+    [out_rows] = call(k_assemble, [struct((rows, model), BF16)], [Scalars(order), *out_shares], 0, "output")
+    output = in_order(out_rows)
     if n_seq == 8:
-        rows_all, g_in_x, g_dt, g_in_bc, g_in_z, g_out_w = lax.optimization_barrier(
-            (rows_all, g_in_x, g_dt, g_in_bc, g_in_z, g_out_w)
+        rows_all, g_in_x, g_in_z, g_out_w, output = lax.optimization_barrier(
+            (rows_all, g_in_x, g_in_z, g_out_w, output)
         )
 
     d_tokens = in_order(rows_all)
-    small = sum(t.astype(F32) for t in dx_got.tails(rows, piece))
-    summed = sum(t.astype(F32) for t in bc_got.tails(rows, piece))
+    g_in_x, g_dt, g_in_bc = both_cores(g_in_x, [width, LANES, bc], "cores_x")
     if n_seq == 8:
-        small = small + flip(small, "seq", 1)
-        summed = summed + flip(summed, "seq", 1)
-    g_in_x, g_dt, g_in_bc = both_cores([g_in_x, g_dt, g_in_bc], "cores_x")
+        small = small + after(flip(small, "seq", 1), g_in_x)
+    summed = small[:, width + LANES :]
     cuts = model // bc
     g_router = summed[: cuts * experts].reshape(cuts, experts, bc)
     first = cuts * experts
@@ -1302,7 +1401,7 @@
         g_in_z,
         g_in_x,
         g_in_bc,
-        g_dt[:, :heads],
+        g_dt[:heads].T,
         small[: KCONV + 1, :width],
         summed[first + 2 * cuts : first + 2 * cuts + KCONV + 1],
         small[:3, width : width + heads],

time: 490 us -> 482 us (0.984)
  Pallas kernels: 191 us -> 184 us
    all_to_all x6 -> x5, waiting for transfers between devices: 17.3 us -> 26 us  [exchange_mp(): return lax.all_to_all(array, 'mp', 0, 0, tiled=True)]
    pallas_call x32 -> x33, Pallas kernels: 191 us -> 184 us  [call(): pl.pallas_call(kernel, out_shape=shapes, grid_spec=grid_spec, input_outpu...]
    ppermute x65 -> x64, waiting for transfers between devices: 76.9 us -> 70.3 us  [flip(): lax.ppermute(array, axis, [(i, i ^ bit) for i in range(lax.axis_size(axis...]
    all_to_all x6 -> x5, starting transfers between devices: 26.9 us -> 20.6 us  [exchange_mp(): return lax.all_to_all(array, 'mp', 0, 0, tiled=True)]
    slice x0 -> x10, local copies, waits for them, and re-layouts: none -> 6.03 us  [the longest x5 3.99 us: gather_near(): by_y[half:]]
    ppermute x65 -> x64, starting transfers between devices: 60.7 us -> 64.1 us  [flip(): lax.ppermute(array, axis, [(i, i ^ bit) for i in range(lax.axis_size(axis...]
    unnamed x116 -> x119, local copies, waits for them, and re-layouts: 21.9 us -> 20.1 us
  transfers between devices with their start and end apart: 74 -> 72, of which waited for: 25 -> 25; matrix products, arithmetic and copies ran while one was open for 6% -> 5% of each run, Pallas kernels for 32% -> 32%
where the time goes in v3:
time: 482 us; the launch traced here: 474 us
  Pallas kernels  184 us (38%)
  waiting for transfers between devices  97.2 us (20%)
  starting transfers between devices  88.3 us (18%)
  local copies, waits for them, and re-layouts  43.3 us (9%)
  blocking collectives  37.8 us (8%)
  between operations  15.4 us (3%)
  other arithmetic  8.82 us (2%)
    pallas_call x33, Pallas kernels, call(): pl.pallas_call(kernel, out_shape=shapes, grid_spec=grid_spec, input_outpu...  184 us
    ppermute x64, waiting for transfers between devices, flip(): lax.ppermute(array, axis, [(i, i ^ bit) for i in range(lax.axis_size(axis...  70.3 us
    ppermute x64, starting transfers between devices, flip(): lax.ppermute(array, axis, [(i, i ^ bit) for i in range(lax.axis_size(axis...  64.1 us
    all_gather x2, blocking collectives, gather_mp(): return lax.all_gather(array, 'mp', tiled=True)  37.8 us
    all_to_all x5, waiting for transfers between devices, exchange_mp(): return lax.all_to_all(array, 'mp', 0, 0, tiled=True)  26 us
    all_to_all x5, starting transfers between devices, exchange_mp(): return lax.all_to_all(array, 'mp', 0, 0, tiled=True)  20.6 us
    unnamed x119, local copies, waits for them, and re-layouts  20.1 us
  transfers between devices with their start and end apart: 72, of which 25 were waited for; matrix products, arithmetic and copies ran while one was open for 5% of the time, Pallas kernels for 32%

profile of v3, /device:TPU:0, one launch (start us, length us, event | category | flops | bytes accessed | tf_op | source)
XLA Modules:
  0.0 474.4 jit_solution(4159431400411502024)
XLA Ops:
  13.1 7.2 %mixer_in.1 = (bf16[2,128,1536]{2,1,0:T(8,128)(2,1)}, f32[2,128,768]{2,1,0:T(8,128)}, bf16[2,144,1024]{2,1,0:T(8,128)(2,1)}, f32[2,128,128]{2,1,0:T(8,128)}, bf1...) custom-call(bf16[2,144,1536]{2,1,0:T(8,128)(2,1)} %fusion.1.tok, f32[2,1536]{1,0:T(2,128)} %gains.7, ...), custom_call_target="tpu_custom_call" | custom-call | flops 1509949440 | bytes 9162908 | tf_op jit(solution)/shard_map/mixer_in/pallas_call | solution.py:77
  29.8 9.8 %collective-permute-done.2.recv = bf16[2,784,128]{2,1,0:T(8,128)(2,1)S(1)} collective-permute-done((bf16[2,784,128]{2,1,0:T(8,128)(2,1)}, bf16[2,784,128]{2,1,0:T(8,128)(2,1)S(1)}, u32[]{:S(2)}, u32[]{:S(2)}) %collective-permute-start.2) | collective-permute-done | bytes 401440 | tf_op jit(solution)/shard_map/ppermute | solution.py:844
  63.7 4.9 %all-to-all-start = ((bf16[4,64,1664]{2,1,0:T(8,128)(2,1)}), bf16[4,64,1664]{2,1,0:T(8,128)(2,1)S(1)}, u32[]{:S(2)}, u32[]{:S(2)}) async-start(bf16[4,64,1664]{2,1,0:T(8,128)(2,1)} %bitcast.68), calls=%async_computation | async-start | bytes 1703936 | tf_op jit(solution)/shard_map/all_to_all | solution.py:1017
  78.1 9.4 %all-to-all-done.arrived = bf16[4,64,1664]{2,1,0:T(8,128)(2,1)S(1)} async-done(((bf16[4,64,1664]{2,1,0:T(8,128)(2,1)}), bf16[4,64,1664]{2,1,0:T(8,128)(2,1)S(1)}, u32[]{:S(2)}, u32[]{:S(2)}) %all-to-all-start) | async-done | bytes 852000 | tf_op jit(solution)/shard_map/all_to_all | solution.py:1017
  91.5 18.4 %all_gather.6.x.refs_4_.refs_2_.refs_0_ = bf16[256,1536]{1,0:T(8,128)(2,1)S(1)} all-gather(bf16[64,1536]{1,0:T(8,128)(2,1)} %get-tuple-element.205.two), channel_id=1, replica_groups=mesh['seq'=8,'mp'=4] {'mp'}, dimensions={0}, use_global_device_ids=true | all-gather | bytes 983040 | tf_op jit(solution)/shard_map/all_gather | solution.py:1026
  118.8 8.7 %experts.3 = (bf16[2048,1536]{1,0:T(8,128)(2,1)}, bf16[256,1664]{1,0:T(8,128)(2,1)}, bf16[256,768]{1,0:T(8,128)(2,1)}, bf16[256,1664]{1,0:T(8,128)(2,1)}, bf16[256,768]{1,0:T(8,128)(2,1)}) custom-call(s32[2]{0:T(128)} %pad_add_fusion.1.index, s32[1]{0:T(128)} %bitcast.14.refs_0_, bf16[16,1536]{1,0:T(8,128)(2,1)} %bitcast.77, ...), custom_call_target="tpu_custom_call" | custom-call | flops 2617245696 | bytes 16039940 | tf_op jit(solution)/shard_map/experts/pallas_call | solution.py:77
  134.5 8.3 %experts.4 = (bf16[2048,1536]{1,0:T(8,128)(2,1)}, bf16[256,1664]{1,0:T(8,128)(2,1)}, bf16[256,768]{1,0:T(8,128)(2,1)}, bf16[256,1664]{1,0:T(8,128)(2,1)}, bf16[256,768]{1,0:T(8,128)(2,1)}) custom-call(s32[2]{0:T(128)} %pad_add_fusion.2.index, s32[1]{0:T(128)} %bitcast.14.refs_0_, bf16[16,1536]{1,0:T(8,128)(2,1)} %bitcast.78, ...), custom_call_target="tpu_custom_call", output_to_operand_aliasing={{0}: (9, {})} | custom-call | flops 2617245696 | bytes 20758532 | tf_op jit(solution)/shard_map/experts/pallas_call | solution.py:77
  146.1 12.7 %experts.5 = (bf16[2048,1536]{1,0:T(8,128)(2,1)}, bf16[256,1664]{1,0:T(8,128)(2,1)}, bf16[256,768]{1,0:T(8,128)(2,1)}, bf16[256,1664]{1,0:T(8,128)(2,1)}, bf16[2...) custom-call(s32[4]{0:T(128)} %pad_add_fusion.3.index, ...), custom_call_target="tpu_custom_call", output_to_operand_aliasing={{0}: (17, {})} | custom-call | flops 5234491392 | bytes 26525700 | tf_op jit(solution)/shard_map/experts/pallas_call | solution.py:77
  170.8 17.9 %shared_weights.1 = (f32[2,1536,256]{2,1,0:T(8,128)}, f32[256,1536]{1,0:T(8,128)}) custom-call(s32[8]{0:T(128)} %stack.80.index, bf16[2,1536,256]{2,1,0:T(8,128)(2,1)} %refs_0_.1, bf16[256,1536]{1,0:T(8,128)(2,1)} %refs_1_.1, bf16[256,1536]{1,0:T(8,128)(2,1)} %copy-done.17, bf16[256,1536]{1,0:T(8,128)(2,1)} %copy-done.44, bf16[256,1536]{1,0:T(8,128)(2,1)} %copy-done.11, ...), custom_call_target="tpu_custom_call" | custom-call | flops 9663676416 | bytes 20185088 | tf_op jit(solution)/shard_map/shared_weights/pallas_call | solution.py:77
  197.4 12.6 %expert_weights.1 = (f32[2,1536,256]{2,1,0:T(8,128)}, f32[256,1536]{1,0:T(8,128)}) custom-call(s32[8]{0:T(128)} %stack.80.index, bf16[256,1536]{1,0:T(8,128)(2,1)} %copy-done.17, bf16[256,1536]{1,0:T(8,128)(2,1)} %copy-done.44, bf16[256,1536]{1,0:T(8,128)(2,1)} %copy-done.11, bf16[256,1536]{1,0:T(8,128)(2,1)} %copy-done.12, bf16[256,1536]{1,0:T(8,128)(2,1)} %copy-done.45, ...), custom_call_target="tpu_custom_call" | custom-call | flops 4831838208 | bytes 20971520 | tf_op jit(solution)/shard_map/expert_weights/pallas_call | solution.py:77
  222.0 16.5 %all-to-all-done.1.arrived = bf16[4,64,1664]{2,1,0:T(8,128)(2,1)S(1)} async-done(((bf16[4,64,1664]{2,1,0:T(8,128)(2,1)}), bf16[4,64,1664]{2,1,0:T(8,128)(2,1)S(1)}, u32[]{:S(2)}, u32[]{:S(2)}) %all-to-all-start.1) | async-done | bytes 852000 | tf_op jit(solution)/shard_map/all_to_all | solution.py:1017
  242.8 19.4 %all_gather.7.dm.refs_5_ = bf16[256,1664]{1,0:T(8,128)(2,1)} all-gather(bf16[64,1664]{1,0:T(8,128)(2,1)} %get-tuple-element.292), channel_id=1, replica_groups=mesh['seq'=8,'mp'=4] {'mp'}, dimensions={0}, use_global_device_ids=true | all-gather | bytes 1064960 | tf_op jit(solution)/shard_map/all_gather | solution.py:1026
  263.1 5.6 %back_gate.1 = (bf16[2,128,768]{2,1,0:T(8,128)(2,1)}, f32[2,128,768]{2,1,0:T(8,128)}, bf16[2,784,128]{2,1,0:T(8,128)(2,1)}, f32[2,8,768]{2,1,0:T(8,128)}) custom-call(bf16[256,1664]{1,0:T(8,128)(2,1)} %all_gather.7.dm.refs_5_, f32[2,128,768]{2,1,0:T(8,128)} %get-tuple-element.296.y, f32[2,128,768]{2,1,0:T(8,128)} %get-tuple-element.203.z, ...), custom_call_target="tpu_custom_call" | custom-call | flops 654311424 | bytes 7277568 | tf_op jit(solution)/shard_map/back_gate/pallas_call | solution.py:77
  277.4 8.8 %collective-permute-done.33.recv = bf16[2,784,128]{2,1,0:T(8,128)(2,1)S(1)} collective-permute-done((bf16[2,784,128]{2,1,0:T(8,128)(2,1)}, bf16[2,784,128]{2,1,0:T(8,128)(2,1)S(1)}, u32[]{:S(2)}, u32[]{:S(2)}) %collective-permute-start.33) | collective-permute-done | bytes 401440 | tf_op jit(solution)/shard_map/ppermute | solution.py:844
  296.7 6.9 %back_intra.1 = (f32[2,128,768]{2,1,0:T(8,128)}, f32[2,128,128]{2,1,0:T(8,128)}, f32[2,128,128]{2,1,0:T(8,128)}, f32[2,128,128]{2,1,0:T(8,128)}, f32[2,128,1536]{2,1,0:T(8,128)}) custom-call(bf16[2,144,1024]{2,1,0:T(8,128)(2,1)} %get-tuple-element.191.xbc, f32[2,128,128]{2,1,0:T(8,128)} %get-tuple-element.192.dt, f32[5,768]{1,0:T(8,128)} %conv_x.7, ...), custom_call_target="tpu_custom_call" | custom-call | flops 805306368 | bytes 7032988 | tf_op jit(solution)/shard_map/back_intra/pallas_call | solution.py:77
  312.3 8.9 %back_state.1 = (f32[2,144,1024]{2,1,0:T(8,128)}, bf16[2,128,128]{2,1,0:T(8,128)(2,1)}, f32[2,8,1024]{2,1,0:T(8,128)}, f32[2,8,128]{2,1,0:T(8,128)}) custom-call(bf16[2,144,1024]{2,1,0:T(8,128)(2,1)} %get-tuple-element.191.xbc, f32[2,128,128]{2,1,0:T(8,128)} %get-tuple-element.192.dt, f32[5,768]{1,0:T(8,128)} %conv_x.7, f32[5,256]{1,0:T(8,128)} %conv_bc.7, ...), custom_call_target="tpu_custom_call" | custom-call | flops 1006632960 | bytes 5599388 | tf_op jit(solution)/shard_map/back_state/pallas_call | solution.py:77
  325.3 5.4 %collective-permute-start.42 = (bf16[128,1664]{1,0:T(8,128)(2,1)S(1)}, bf16[128,1664]{1,0:T(8,128)(2,1)}, u32[]{:S(2)}, u32[]{:S(2)}) collective-permute-start(bf16[128,1664]{1,0:T(8,128)(2,1)S(1)} %slice.87), channel_id=1, source_target_pairs={{0,16},{4,20},{8,24},{12,28},{16,0},{20,4},{24,8},{28,12},{1,17},{... | collective-permute-start | bytes 1277960 | tf_op jit(solution)/shard_map/ppermute | solution.py:844
  331.5 6.8 %back_in.1 = (bf16[272,896]{1,0:T(8,128)(2,1)}, bf16[384,256]{1,0:T(8,128)(2,1)}, bf16[2,128,1536]{2,1,0:T(8,128)(2,1)}) custom-call(f32[2,128,1536]{2,1,0:T(8,128)} %get-tuple-element.300.dn0, f32[2,144,1024]{2,1,0:T(8,128)} %get-tuple-element.313.dxbc, f32[2,16,1024]{2,1,0:T(8,128)} %copy-done.34, bf16[2,128,128]{2,1,0:T(8,128)(2,1)} %get-tuple-element.319.ddt, ...), custom_call_target="tpu_custom_call" | custom-call | flops 905969664 | bytes 8757248 | tf_op jit(solution)/shard_map/back_in/pallas_call | solution.py:77
  354.2 6.8 %out_weights.1.a = bf16[768,1536]{1,0:T(8,128)(2,1)} custom-call(s32[4]{0:T(128)} %pad_add_fusion.4.index, bf16[256,768]{1,0:T(8,128)(2,1)} %bitcast.87, bf16[256,768]{1,0:T(8,128)(2,1)} %copy-done.35, bf16[256,768]{1,0:T(8,128)(2,1)} %copy-done.37, bf16[128,768]{1,0:T(8,128)(2,1)} %copy-done.54, bf16[128,768]{1,0:T(8,128)(2,1)} %copy-done.55, ...), custom_call_target="tpu_custom_call" | custom-call | flops 2415919104 | bytes 7340032 | tf_op jit(solution)/shard_map/out_weights/pallas_call | solution.py:77
  368.7 9.8 %collective-permute-done.57.refs_8_ = bf16[128,768]{1,0:T(8,128)(2,1)S(1)} collective-permute-done((bf16[128,768]{1,0:T(8,128)(2,1)S(1)}, bf16[128,768]{1,0:T(8,128)(2,1)S(1)}, u32[]{:S(2)}, u32[]{:S(2)}) %collective-permute-start.57) | collective-permute-done | bytes 196640 | tf_op jit(solution)/shard_map/ppermute | solution.py:844
  379.2 6.5 %weights_z.1.a = bf16[1536,768]{1,0:T(8,128)(2,1)} custom-call(s32[4]{0:T(128)} %pad_add_fusion.4.index, bf16[256,1536]{1,0:T(8,128)(2,1)} %bitcast.85, bf16[256,1536]{1,0:T(8,128)(2,1)} %collective-permute-done.48.refs_1_, bf16[256,1536]{1,0:T(8,128)(2,1)} %collective-permute-done.49.refs_2_, bf16[128,1536]{1,0:T(8,128)(2,1)} %collective-permute-done.50.refs_3_, ...), custom_call_target="tpu_custom_call" | custom-call | flops 2415919104 | bytes 7077888 | tf_op jit(solution)/shard_map/weights_z/pallas_call | solution.py:77
  406.2 6.6 %collective-permute-done.56.refs_13_ = bf16[384,256]{1,0:T(8,128)(2,1)} collective-permute-done((bf16[384,256]{1,0:T(8,128)(2,1)S(1)}, bf16[384,256]{1,0:T(8,128)(2,1)}, u32[]{:S(2)}, u32[]{:S(2)}) %collective-permute-start.56) | collective-permute-done | bytes 196640 | tf_op jit(solution)/shard_map/ppermute | solution.py:844
  417.2 9.6 %weights_x.1 = (bf16[1536,1152]{1,0:T(8,128)(2,1)}, f32[128,1152]{1,0:T(8,128)}) custom-call(s32[4]{0:T(128)} %pad_add_fusion.4.index, bf16[256,1536]{1,0:T(8,128)(2,1)} %bitcast.86, bf16[256,1536]{1,0:T(8,128)(2,1)} %collective-permute-done.48.refs_1_, bf16[256,1536]{1,0:T(8,128)(2,1)} %collective-permute-done.49.refs_2_, ...), custom_call_target="tpu_custom_call" | custom-call | flops 3623878656 | bytes 10010624 | tf_op jit(solution)/shard_map/weights_x/pallas_call | solution.py:77
  454.5 6.2 %cores_x.1 = (f32[1536,768]{1,0:T(8,128)}, f32[128,1536]{1,0:T(8,128)}, f32[1536,256]{1,0:T(8,128)}) custom-call(bf16[1536,1152]{1,0:T(8,128)(2,1)} %get-tuple-element.355.a, bf16[1536,1152]{1,0:T(8,128)(2,1)} %collective-permute-done.65.b), custom_call_target="tpu_custom_call" | custom-call | bytes 14155776 | tf_op jit(solution)/shard_map/cores_x/pallas_call | solution.py:77
  (320 shorter events, 225.6 us)
Async XLA Ops:
  48.5 24.5 %collective-permute-start.6 = (bf16[256,1664]{1,0:T(8,128)(2,1)}, bf16[256,1664]{1,0:T(8,128)(2,1)S(1)}, u32[]{:S(2)}, u32[]{:S(2)}) collective-permute-start(bf16[256,1664]{1,0:T(8,128)(2,1)} %bitcast.3.do.refs_6_.refs_12_.refs_10_), channel_id=1, source_target_pairs={{0,16},{4,20},{8,24},{12,28},{16,0},{20,4},{24,8},{28,12},{1,17},{... | collective-permute-start | bytes 2555912 | tf_op jit(solution)/shard_map/ppermute | solution.py:844
  63.7 23.8 %all-to-all-start = ((bf16[4,64,1664]{2,1,0:T(8,128)(2,1)}), bf16[4,64,1664]{2,1,0:T(8,128)(2,1)S(1)}, u32[]{:S(2)}, u32[]{:S(2)}) async-start(bf16[4,64,1664]{2,1,0:T(8,128)(2,1)} %bitcast.68), calls=%async_computation | async-start | bytes 1703936 | tf_op jit(solution)/shard_map/all_to_all | solution.py:1017
  68.6 221.0 %reduce-scatter.2.cloned.1.call-start = ((), (), s32[]{:S(2)}) async-start(), calls=%async_computation.6 | async-start | bytes 7077888 | tf_op jit(solution)/shard_map/reduce_scatter | solution.py:1248
  76.9 33.0 %collective-permute-start.4 = (bf16[256,1664]{1,0:T(8,128)(2,1)}, bf16[256,1664]{1,0:T(8,128)(2,1)}, u32[]{:S(2)}, u32[]{:S(2)}) collective-permute-start(bf16[256,1664]{1,0:T(8,128)(2,1)} %bitcast.3.do.refs_6_.refs_12_.refs_10_), channel_id=1, source_target_pairs={{0,4},{4,0},{8,12},{12,8},{16,20},{20,16},{24,28},{28,24},{1,5},{5... | collective-permute-start | bytes 2555912 | tf_op jit(solution)/shard_map/ppermute | solution.py:844
  76.9 33.0 %collective-permute-start.7 = (bf16[256,1664]{1,0:T(8,128)(2,1)S(1)}, bf16[256,1664]{1,0:T(8,128)(2,1)}, u32[]{:S(2)}, u32[]{:S(2)}) collective-permute-start(bf16[256,1664]{1,0:T(8,128)(2,1)S(1)} %collective-permute-done.5.refs_6_.refs_14_.refs_12_), channel_id=1, source_target_pairs={{0,4},{4,0},{8,12},{12,8},{16,20},{20,16},{24,28},{28,24},{1,5},{5... | collective-permute-start | bytes 2555912 | tf_op jit(solution)/shard_map/ppermute | solution.py:844
  77.4 32.5 %collective-permute-start.8 = (bf16[256,1664]{1,0:T(8,128)(2,1)S(1)}, bf16[256,1664]{1,0:T(8,128)(2,1)}, u32[]{:S(2)}, u32[]{:S(2)}) collective-permute-start(bf16[256,1664]{1,0:T(8,128)(2,1)S(1)} %collective-permute-done.6.refs_7_.refs_15_.refs_13_), channel_id=1, source_target_pairs={{0,4},{4,0},{8,12},{12,8},{16,20},{20,16},{24,28},{28,24},{1,5},{5... | collective-permute-start | bytes 2555912 | tf_op jit(solution)/shard_map/ppermute | solution.py:844
  160.1 28.6 %collective-permute-start.14 = (bf16[256,1664]{1,0:T(8,128)(2,1)S(1)}, bf16[256,1664]{1,0:T(8,128)(2,1)S(1)}, u32[]{:S(2)}, u32[]{:S(2)}) collective-permute-start(bf16[256,1664]{1,0:T(8,128)(2,1)S(1)} %copy-done.43), channel_id=1, source_target_pairs={{0,4},{4,0},{8,12},{12,8},{16,20},{20,16},{24,28},{28,24},{1,5},{5... | collective-permute-start | bytes 2555912 | tf_op jit(solution)/shard_map/ppermute | solution.py:844
  214.5 24.0 %all-to-all-start.1 = ((bf16[4,64,1664]{2,1,0:T(8,128)(2,1)}), bf16[4,64,1664]{2,1,0:T(8,128)(2,1)S(1)}, u32[]{:S(2)}, u32[]{:S(2)}) async-start(bf16[4,64,1664]{2,1,0:T(8,128)(2,1)} %bitcast.21), calls=%async_computation.1 | async-start | bytes 1703936 | tf_op jit(solution)/shard_map/all_to_all | solution.py:1017
  218.2 44.0 %collective-permute-start.30 = (bf16[256,768]{1,0:T(8,128)(2,1)S(1)}, bf16[256,768]{1,0:T(8,128)(2,1)S(1)}, u32[]{:S(2)}, u32[]{:S(2)}) collective-permute-start(bf16[256,768]{1,0:T(8,128)(2,1)S(1)} %bitcast.88), channel_id=1, source_target_pairs={{0,8},{4,12},{8,0},{12,4},{16,24},{20,28},{24,16},{28,20},{1,9},{5... | collective-permute-start | bytes 1179656 | tf_op jit(solution)/shard_map/ppermute | solution.py:844
  218.8 43.4 %collective-permute-start.31 = (bf16[256,768]{1,0:T(8,128)(2,1)S(1)}, bf16[256,768]{1,0:T(8,128)(2,1)S(1)}, u32[]{:S(2)}, u32[]{:S(2)}) collective-permute-start(bf16[256,768]{1,0:T(8,128)(2,1)S(1)} %bitcast.89), channel_id=1, source_target_pairs={{0,16},{4,20},{8,24},{12,28},{16,0},{20,4},{24,8},{28,12},{1,17},{... | collective-permute-start | bytes 1179656 | tf_op jit(solution)/shard_map/ppermute | solution.py:844
  275.1 29.3 %collective-permute-start.35 = (bf16[256,1664]{1,0:T(8,128)(2,1)S(1)}, bf16[256,1664]{1,0:T(8,128)(2,1)S(1)}, u32[]{:S(2)}, u32[]{:S(2)}) collective-permute-start(bf16[256,1664]{1,0:T(8,128)(2,1)S(1)} %copy-done.3), channel_id=1, source_target_pairs={{0,8},{4,12},{8,0},{12,4},{16,24},{20,28},{24,16},{28,20},{1,9},{5... | collective-permute-start | bytes 2555912 | tf_op jit(solution)/shard_map/ppermute | solution.py:844
  275.8 28.6 %collective-permute-start.36 = (bf16[256,1664]{1,0:T(8,128)(2,1)S(1)}, bf16[256,1664]{1,0:T(8,128)(2,1)}, u32[]{:S(2)}, u32[]{:S(2)}) collective-permute-start(bf16[256,1664]{1,0:T(8,128)(2,1)S(1)} %copy-done.3), channel_id=1, source_target_pairs={{0,16},{4,20},{8,24},{12,28},{16,0},{20,4},{24,8},{28,12},{1,17},{... | collective-permute-start | bytes 2555912 | tf_op jit(solution)/shard_map/ppermute | solution.py:844
  289.6 41.8 %all-to-all-start.2 = ((bf16[4,64,1536]{2,1,0:T(8,128)(2,1)}), bf16[4,64,1536]{2,1,0:T(8,128)(2,1)S(1)}, u32[]{:S(2)}, u32[]{:S(2)}) async-start(bf16[4,64,1536]{2,1,0:T(8,128)(2,1)} %bitcast.69), calls=%async_computation.3 | async-start | bytes 1572864 | tf_op jit(solution)/shard_map/all_to_all | solution.py:1017
  294.9 47.8 %collective-permute-start.48 = (bf16[256,1536]{1,0:T(8,128)(2,1)}, bf16[256,1536]{1,0:T(8,128)(2,1)}, u32[]{:S(2)}, u32[]{:S(2)}) collective-permute-start(bf16[256,1536]{1,0:T(8,128)(2,1)} %bitcast.83), channel_id=1, source_target_pairs={{0,8},{4,12},{8,0},{12,4},{16,24},{20,28},{24,16},{28,20},{1,9},{5... | collective-permute-start | bytes 2359304 | tf_op jit(solution)/shard_map/ppermute | solution.py:844
  296.2 47.8 %collective-permute-start.49 = (bf16[256,1536]{1,0:T(8,128)(2,1)}, bf16[256,1536]{1,0:T(8,128)(2,1)}, u32[]{:S(2)}, u32[]{:S(2)}) collective-permute-start(bf16[256,1536]{1,0:T(8,128)(2,1)} %bitcast.84), channel_id=1, source_target_pairs={{0,16},{4,20},{8,24},{12,28},{16,0},{20,4},{24,8},{28,12},{1,17},{... | collective-permute-start | bytes 2359304 | tf_op jit(solution)/shard_map/ppermute | solution.py:844
  309.4 21.3 %collective-permute-start.38 = (bf16[256,768]{1,0:T(8,128)(2,1)S(1)}, bf16[256,768]{1,0:T(8,128)(2,1)S(1)}, u32[]{:S(2)}, u32[]{:S(2)}) collective-permute-start(bf16[256,768]{1,0:T(8,128)(2,1)S(1)} %bitcast.72), channel_id=1, source_target_pairs={{0,8},{4,12},{8,0},{12,4},{16,24},{20,28},{24,16},{28,20},{1,9},{5... | collective-permute-start | bytes 1179656 | tf_op jit(solution)/shard_map/ppermute | solution.py:844
  325.3 28.9 %collective-permute-start.42 = (bf16[128,1664]{1,0:T(8,128)(2,1)S(1)}, bf16[128,1664]{1,0:T(8,128)(2,1)}, u32[]{:S(2)}, u32[]{:S(2)}) collective-permute-start(bf16[128,1664]{1,0:T(8,128)(2,1)S(1)} %slice.87), channel_id=1, source_target_pairs={{0,16},{4,20},{8,24},{12,28},{16,0},{20,4},{24,8},{28,12},{1,17},{... | collective-permute-start | bytes 1277960 | tf_op jit(solution)/shard_map/ppermute | solution.py:844
  330.7 23.5 %collective-permute-start.43 = (bf16[128,1664]{1,0:T(8,128)(2,1)S(1)}, bf16[128,1664]{1,0:T(8,128)(2,1)}, u32[]{:S(2)}, u32[]{:S(2)}) collective-permute-start(bf16[128,1664]{1,0:T(8,128)(2,1)S(1)} %slice.88), channel_id=1, source_target_pairs={{0,8},{4,12},{8,0},{12,4},{16,24},{20,28},{24,16},{28,20},{1,9},{5... | collective-permute-start | bytes 1277960 | tf_op jit(solution)/shard_map/ppermute | solution.py:844
  338.3 47.6 %all-to-all-start.3 = ((bf16[4,64,1536]{2,1,0:T(8,128)(2,1)}), bf16[4,64,1536]{2,1,0:T(8,128)(2,1)S(1)}, u32[]{:S(2)}, u32[]{:S(2)}) async-start(bf16[4,64,1536]{2,1,0:T(8,128)(2,1)} %bitcast.70), calls=%async_computation.4 | async-start | bytes 1572864 | tf_op jit(solution)/shard_map/all_to_all | solution.py:1017
  361.0 24.8 %collective-permute-start.46 = (bf16[272,896]{1,0:T(8,128)(2,1)}, bf16[272,896]{1,0:T(8,128)(2,1)}, u32[]{:S(2)}, u32[]{:S(2)}) collective-permute-start(bf16[272,896]{1,0:T(8,128)(2,1)} %get-tuple-element.332.refs_5_), channel_id=1, source_target_pairs={{0,8},{4,12},{8,0},{12,4},{16,24},{20,28},{24,16},{28,20},{1,9},{5... | collective-permute-start | bytes 1462280 | tf_op jit(solution)/shard_map/ppermute | solution.py:844
  361.6 24.2 %collective-permute-start.47 = (bf16[272,896]{1,0:T(8,128)(2,1)}, bf16[272,896]{1,0:T(8,128)(2,1)}, u32[]{:S(2)}, u32[]{:S(2)}) collective-permute-start(bf16[272,896]{1,0:T(8,128)(2,1)} %get-tuple-element.332.refs_5_), channel_id=1, source_target_pairs={{0,16},{4,20},{8,24},{12,28},{16,0},{20,4},{24,8},{28,12},{1,17},{... | collective-permute-start | bytes 1462280 | tf_op jit(solution)/shard_map/ppermute | solution.py:844
  385.7 51.2 %collective-permute-start.59 = (bf16[1536,768]{1,0:T(8,128)(2,1)}, bf16[1536,768]{1,0:T(8,128)(2,1)S(1)}, u32[]{:S(2)}, u32[]{:S(2)}) collective-permute-start(bf16[1536,768]{1,0:T(8,128)(2,1)} %weights_z.1.a), channel_id=1, source_target_pairs={{0,4},{4,0},{8,12},{12,8},{16,20},{20,16},{24,28},{28,24},{1,5},{5... | collective-permute-start | bytes 7077896 | tf_op jit(solution)/shard_map/ppermute | solution.py:844
  385.9 56.3 %collective-permute-start.60 = (bf16[768,1536]{1,0:T(8,128)(2,1)}, bf16[768,1536]{1,0:T(8,128)(2,1)}, u32[]{:S(2)}, u32[]{:S(2)}) collective-permute-start(bf16[768,1536]{1,0:T(8,128)(2,1)} %out_weights.1.a), channel_id=1, source_target_pairs={{0,4},{4,0},{8,12},{12,8},{16,20},{20,16},{24,28},{28,24},{1,5},{5... | collective-permute-start | bytes 7077896 | tf_op jit(solution)/shard_map/ppermute | solution.py:844
  389.3 57.1 %all-to-all-start.4 = ((bf16[4,64,1536]{2,1,0:T(8,128)(2,1)}), bf16[4,64,1536]{2,1,0:T(8,128)(2,1)}, u32[]{:S(2)}, u32[]{:S(2)}) async-start(bf16[4,64,1536]{2,1,0:T(8,128)(2,1)} %rows_three.1), calls=%async_computation.5 | async-start | bytes 1572864 | tf_op jit(solution)/shard_map/all_to_all | solution.py:1017
  (106 other events, 980.3 us)
Sparse Core Ops, SparseCore 0:
  214.6 60.2 reduce-scatter.1

commit v4 on v3

--- a/solution.py
+++ b/solution.py
@@ -911,6 +911,14 @@
     return Gathered([own, by_x, by_y, diagonal], [1, 1, 1, 1], near_index())
 
 
+def gather_direct(own, first=None):
+    if lax.axis_size("seq") != 8:
+        return gather_all(own)
+    core, x, y = bits_of("seq")
+    by_x, by_y = first or first_hop(own)
+    return Gathered([own, by_x, by_y, flip(own, "seq", x | y)], [1, 1, 1, 1], near_index())
+
+
 def xor_index():
     return jnp.stack([lax.axis_index("seq") ^ k for k in XOR_ORDER]).astype(jnp.int32)
 
@@ -1291,7 +1299,8 @@
     dm_first = first_hop(dm) if n_seq == 8 else None
     leaving = scan(send, True, "scan_back", (None, None, (intra_back, dm_first)), steps)
     out_arrived = to_shares(after(out_sum, steps[1]))
-    dz_first = first_hop(after(dz, leaving).reshape(rows, width)) if n_seq == 8 else None
+    dz = after(dz, leaving).reshape(rows, width)
+    dz_first = first_hop(dz) if n_seq == 8 else None
 
     def in_order(rows):
         return jnp.transpose(rows.reshape(seqs, piece, model), (1, 0, 2)).astype(F32)
@@ -1339,12 +1348,12 @@
     dm_got = gather_near(dm, piece, leaving, dm_first)
     if n_seq == 8:
         u_got = gather_near(u, piece, leaving, u_first)
-    dz_got = gather_near(dz.reshape(rows, width), piece, part, dz_first)
+    dz_got = gather_direct(dz, dz_first)
     *head_bits, last_bit = bits_of("mp")
     for bit in head_bits:
         d_bc = low_sum(d_bc, flip(d_bc, "mp", bit))
     d_bc = low_sum(d_bc, flip(d_bc, "mp", last_bit))
-    bc_got = gather_lean(d_bc, d_bc, False)
+    bc_got = gather_direct(d_bc)
     dx_first = first_hop(dx) if n_seq == 8 else None
     if n_seq != 8:
         dx_got = gather_all(dx)

time: 482 us -> 480 us (level)
    ppermute x64 -> x63, waiting for transfers between devices: 70.3 us -> 65.6 us  [flip(): lax.ppermute(array, axis, [(i, i ^ bit) for i in range(lax.axis_size(axis...]
    ppermute x64 -> x63, starting transfers between devices: 64.1 us -> 67.7 us  [flip(): lax.ppermute(array, axis, [(i, i ^ bit) for i in range(lax.axis_size(axis...]
    unnamed x119 -> x111, local copies, waits for them, and re-layouts: 20.1 us -> 18.2 us
  transfers between devices with their start and end apart: 72 -> 71, of which waited for: 25 -> 27; matrix products, arithmetic and copies ran while one was open for 5% -> 5% of each run, Pallas kernels for 32% -> 32%
where the time goes in v4:
time: 480 us; the launch traced here: 473 us
  Pallas kernels  184 us (38%)
  waiting for transfers between devices  93.5 us (19%)
  starting transfers between devices  92.3 us (19%)
  local copies, waits for them, and re-layouts  41.5 us (9%)
  blocking collectives  37.8 us (8%)
  between operations  15.3 us (3%)
  other arithmetic  8.78 us (2%)
    pallas_call x33, Pallas kernels, call(): pl.pallas_call(kernel, out_shape=shapes, grid_spec=grid_spec, input_outpu...  184 us
    ppermute x63, starting transfers between devices, flip(): lax.ppermute(array, axis, [(i, i ^ bit) for i in range(lax.axis_size(axis...  67.7 us
    ppermute x63, waiting for transfers between devices, flip(): lax.ppermute(array, axis, [(i, i ^ bit) for i in range(lax.axis_size(axis...  65.6 us
    all_gather x2, blocking collectives, gather_mp(): return lax.all_gather(array, 'mp', tiled=True)  37.8 us
    all_to_all x5, waiting for transfers between devices, exchange_mp(): return lax.all_to_all(array, 'mp', 0, 0, tiled=True)  26 us
    all_to_all x5, starting transfers between devices, exchange_mp(): return lax.all_to_all(array, 'mp', 0, 0, tiled=True)  20.9 us
    unnamed x111, local copies, waits for them, and re-layouts  18.2 us
  transfers between devices with their start and end apart: 71, of which 27 were waited for; matrix products, arithmetic and copies ran while one was open for 5% of the time, Pallas kernels for 32%

profile of v4, /device:TPU:0, one launch (start us, length us, event | category | flops | bytes accessed | tf_op | source)
XLA Modules:
  0.0 472.9 jit_solution(18435770809326295042)
XLA Ops:
  13.0 7.2 %mixer_in.1 = (bf16[2,128,1536]{2,1,0:T(8,128)(2,1)}, f32[2,128,768]{2,1,0:T(8,128)}, bf16[2,144,1024]{2,1,0:T(8,128)(2,1)}, f32[2,128,128]{2,1,0:T(8,128)}, bf1...) custom-call(bf16[2,144,1536]{2,1,0:T(8,128)(2,1)} %fusion.1.tok, f32[2,1536]{1,0:T(2,128)} %gains.7, ...), custom_call_target="tpu_custom_call" | custom-call | flops 1509949440 | bytes 9162908 | tf_op jit(solution)/shard_map/mixer_in/pallas_call | solution.py:77
  29.8 9.8 %collective-permute-done.2.recv = bf16[2,784,128]{2,1,0:T(8,128)(2,1)S(1)} collective-permute-done((bf16[2,784,128]{2,1,0:T(8,128)(2,1)}, bf16[2,784,128]{2,1,0:T(8,128)(2,1)S(1)}, u32[]{:S(2)}, u32[]{:S(2)}) %collective-permute-start.2) | collective-permute-done | bytes 401440 | tf_op jit(solution)/shard_map/ppermute | solution.py:844
  78.1 9.4 %all-to-all-done.arrived = bf16[4,64,1664]{2,1,0:T(8,128)(2,1)S(1)} async-done(((bf16[4,64,1664]{2,1,0:T(8,128)(2,1)}), bf16[4,64,1664]{2,1,0:T(8,128)(2,1)S(1)}, u32[]{:S(2)}, u32[]{:S(2)}) %all-to-all-start) | async-done | bytes 852000 | tf_op jit(solution)/shard_map/all_to_all | solution.py:1025
  91.6 18.4 %all_gather.6.x.refs_4_.refs_2_.refs_0_ = bf16[256,1536]{1,0:T(8,128)(2,1)S(1)} all-gather(bf16[64,1536]{1,0:T(8,128)(2,1)} %get-tuple-element.202.two), channel_id=1, replica_groups=mesh['seq'=8,'mp'=4] {'mp'}, dimensions={0}, use_global_device_ids=true | all-gather | bytes 983040 | tf_op jit(solution)/shard_map/all_gather | solution.py:1034
  118.8 8.7 %experts.3 = (bf16[2048,1536]{1,0:T(8,128)(2,1)}, bf16[256,1664]{1,0:T(8,128)(2,1)}, bf16[256,768]{1,0:T(8,128)(2,1)}, bf16[256,1664]{1,0:T(8,128)(2,1)}, bf16[256,768]{1,0:T(8,128)(2,1)}) custom-call(s32[2]{0:T(128)} %pad_add_fusion.1.index, s32[1]{0:T(128)} %bitcast.14.refs_0_, bf16[16,1536]{1,0:T(8,128)(2,1)} %bitcast.77, ...), custom_call_target="tpu_custom_call" | custom-call | flops 2617245696 | bytes 16039940 | tf_op jit(solution)/shard_map/experts/pallas_call | solution.py:77
  134.5 8.3 %experts.4 = (bf16[2048,1536]{1,0:T(8,128)(2,1)}, bf16[256,1664]{1,0:T(8,128)(2,1)}, bf16[256,768]{1,0:T(8,128)(2,1)}, bf16[256,1664]{1,0:T(8,128)(2,1)}, bf16[256,768]{1,0:T(8,128)(2,1)}) custom-call(s32[2]{0:T(128)} %pad_add_fusion.2.index, s32[1]{0:T(128)} %bitcast.14.refs_0_, bf16[16,1536]{1,0:T(8,128)(2,1)} %bitcast.78, ...), custom_call_target="tpu_custom_call", output_to_operand_aliasing={{0}: (9, {})} | custom-call | flops 2617245696 | bytes 20758532 | tf_op jit(solution)/shard_map/experts/pallas_call | solution.py:77
  146.2 12.7 %experts.5 = (bf16[2048,1536]{1,0:T(8,128)(2,1)}, bf16[256,1664]{1,0:T(8,128)(2,1)}, bf16[256,768]{1,0:T(8,128)(2,1)}, bf16[256,1664]{1,0:T(8,128)(2,1)}, bf16[2...) custom-call(s32[4]{0:T(128)} %pad_add_fusion.3.index, ...), custom_call_target="tpu_custom_call", output_to_operand_aliasing={{0}: (17, {})} | custom-call | flops 5234491392 | bytes 26525700 | tf_op jit(solution)/shard_map/experts/pallas_call | solution.py:77
  170.1 17.9 %shared_weights.1 = (f32[2,1536,256]{2,1,0:T(8,128)}, f32[256,1536]{1,0:T(8,128)}) custom-call(s32[8]{0:T(128)} %stack.80.index, bf16[2,1536,256]{2,1,0:T(8,128)(2,1)} %refs_0_.1, bf16[256,1536]{1,0:T(8,128)(2,1)} %refs_1_.1, bf16[256,1536]{1,0:T(8,128)(2,1)} %copy-done.17, bf16[256,1536]{1,0:T(8,128)(2,1)} %copy-done.41, bf16[256,1536]{1,0:T(8,128)(2,1)} %copy-done.11, ...), custom_call_target="tpu_custom_call" | custom-call | flops 9663676416 | bytes 20185088 | tf_op jit(solution)/shard_map/shared_weights/pallas_call | solution.py:77
  196.2 12.6 %expert_weights.1 = (f32[2,1536,256]{2,1,0:T(8,128)}, f32[256,1536]{1,0:T(8,128)}) custom-call(s32[8]{0:T(128)} %stack.80.index, bf16[256,1536]{1,0:T(8,128)(2,1)} %copy-done.17, bf16[256,1536]{1,0:T(8,128)(2,1)} %copy-done.41, bf16[256,1536]{1,0:T(8,128)(2,1)} %copy-done.11, bf16[256,1536]{1,0:T(8,128)(2,1)} %copy-done.12, bf16[256,1536]{1,0:T(8,128)(2,1)} %copy-done.42, ...), custom_call_target="tpu_custom_call" | custom-call | flops 4831838208 | bytes 20971520 | tf_op jit(solution)/shard_map/expert_weights/pallas_call | solution.py:77
  220.8 16.5 %all-to-all-done.1.arrived = bf16[4,64,1664]{2,1,0:T(8,128)(2,1)S(1)} async-done(((bf16[4,64,1664]{2,1,0:T(8,128)(2,1)}), bf16[4,64,1664]{2,1,0:T(8,128)(2,1)S(1)}, u32[]{:S(2)}, u32[]{:S(2)}) %all-to-all-start.1) | async-done | bytes 852000 | tf_op jit(solution)/shard_map/all_to_all | solution.py:1025
  241.6 19.4 %all_gather.7.dm.refs_5_ = bf16[256,1664]{1,0:T(8,128)(2,1)} all-gather(bf16[64,1664]{1,0:T(8,128)(2,1)} %get-tuple-element.289), channel_id=1, replica_groups=mesh['seq'=8,'mp'=4] {'mp'}, dimensions={0}, use_global_device_ids=true | all-gather | bytes 1064960 | tf_op jit(solution)/shard_map/all_gather | solution.py:1034
  261.9 5.6 %back_gate.1 = (bf16[2,128,768]{2,1,0:T(8,128)(2,1)}, f32[2,128,768]{2,1,0:T(8,128)}, bf16[2,784,128]{2,1,0:T(8,128)(2,1)}, f32[2,8,768]{2,1,0:T(8,128)}) custom-call(bf16[256,1664]{1,0:T(8,128)(2,1)} %all_gather.7.dm.refs_5_, f32[2,128,768]{2,1,0:T(8,128)} %get-tuple-element.293.y, f32[2,128,768]{2,1,0:T(8,128)} %get-tuple-element.200.z, ...), custom_call_target="tpu_custom_call" | custom-call | flops 654311424 | bytes 7277568 | tf_op jit(solution)/shard_map/back_gate/pallas_call | solution.py:77
  276.2 8.8 %collective-permute-done.33.recv = bf16[2,784,128]{2,1,0:T(8,128)(2,1)S(1)} collective-permute-done((bf16[2,784,128]{2,1,0:T(8,128)(2,1)}, bf16[2,784,128]{2,1,0:T(8,128)(2,1)S(1)}, u32[]{:S(2)}, u32[]{:S(2)}) %collective-permute-start.33) | collective-permute-done | bytes 401440 | tf_op jit(solution)/shard_map/ppermute | solution.py:844
  295.0 6.9 %back_intra.1 = (f32[2,128,768]{2,1,0:T(8,128)}, f32[2,128,128]{2,1,0:T(8,128)}, f32[2,128,128]{2,1,0:T(8,128)}, f32[2,128,128]{2,1,0:T(8,128)}, f32[2,128,1536]{2,1,0:T(8,128)}) custom-call(bf16[2,144,1024]{2,1,0:T(8,128)(2,1)} %get-tuple-element.188.xbc, f32[2,128,128]{2,1,0:T(8,128)} %get-tuple-element.189.dt, f32[5,768]{1,0:T(8,128)} %conv_x.7, ...), custom_call_target="tpu_custom_call" | custom-call | flops 805306368 | bytes 7032988 | tf_op jit(solution)/shard_map/back_intra/pallas_call | solution.py:77
  310.2 8.9 %back_state.1 = (f32[2,144,1024]{2,1,0:T(8,128)}, bf16[2,128,128]{2,1,0:T(8,128)(2,1)}, f32[2,8,1024]{2,1,0:T(8,128)}, f32[2,8,128]{2,1,0:T(8,128)}) custom-call(bf16[2,144,1024]{2,1,0:T(8,128)(2,1)} %get-tuple-element.188.xbc, f32[2,128,128]{2,1,0:T(8,128)} %get-tuple-element.189.dt, f32[5,768]{1,0:T(8,128)} %conv_x.7, f32[5,256]{1,0:T(8,128)} %conv_bc.7, ...), custom_call_target="tpu_custom_call" | custom-call | flops 1006632960 | bytes 5599388 | tf_op jit(solution)/shard_map/back_state/pallas_call | solution.py:77
  323.2 6.2 %collective-permute-start.42 = (bf16[128,1664]{1,0:T(8,128)(2,1)S(1)}, bf16[128,1664]{1,0:T(8,128)(2,1)}, u32[]{:S(2)}, u32[]{:S(2)}) collective-permute-start(bf16[128,1664]{1,0:T(8,128)(2,1)S(1)} %slice.81), channel_id=1, source_target_pairs={{0,16},{4,20},{8,24},{12,28},{16,0},{20,4},{24,8},{28,12},{1,17},{... | collective-permute-start | bytes 1277960 | tf_op jit(solution)/shard_map/ppermute | solution.py:844
  331.3 6.1 %collective-permute-done.39.refs_7_ = bf16[256,768]{1,0:T(8,128)(2,1)} collective-permute-done((bf16[256,768]{1,0:T(8,128)(2,1)S(1)}, bf16[256,768]{1,0:T(8,128)(2,1)}, u32[]{:S(2)}, u32[]{:S(2)}) %collective-permute-start.39) | collective-permute-done | bytes 393248 | tf_op jit(solution)/shard_map/ppermute | solution.py:844
  337.4 6.8 %back_in.1 = (bf16[272,896]{1,0:T(8,128)(2,1)}, bf16[384,256]{1,0:T(8,128)(2,1)}, bf16[2,128,1536]{2,1,0:T(8,128)(2,1)}) custom-call(f32[2,128,1536]{2,1,0:T(8,128)} %get-tuple-element.297.dn0, f32[2,144,1024]{2,1,0:T(8,128)} %get-tuple-element.310.dxbc, f32[2,16,1024]{2,1,0:T(8,128)} %copy-done.34, bf16[2,128,128]{2,1,0:T(8,128)(2,1)} %get-tuple-element.316.ddt, ...), custom_call_target="tpu_custom_call" | custom-call | flops 905969664 | bytes 8757248 | tf_op jit(solution)/shard_map/back_in/pallas_call | solution.py:77
  362.3 6.8 %out_weights.1.a = bf16[768,1536]{1,0:T(8,128)(2,1)} custom-call(s32[4]{0:T(128)} %pad_add_fusion.4.index, bf16[256,768]{1,0:T(8,128)(2,1)} %bitcast.87, bf16[256,768]{1,0:T(8,128)(2,1)} %copy-done.35, bf16[256,768]{1,0:T(8,128)(2,1)} %copy-done.37, bf16[128,768]{1,0:T(8,128)(2,1)} %copy-done.52, bf16[128,768]{1,0:T(8,128)(2,1)} %copy-done.53, ...), custom_call_target="tpu_custom_call" | custom-call | flops 2415919104 | bytes 7340032 | tf_op jit(solution)/shard_map/out_weights/pallas_call | solution.py:77
  376.6 6.5 %weights_z.1.a = bf16[1536,768]{1,0:T(8,128)(2,1)} custom-call(s32[4]{0:T(128)} %pad_add_fusion.4.index, bf16[256,1536]{1,0:T(8,128)(2,1)} %bitcast.85, bf16[256,1536]{1,0:T(8,128)(2,1)} %collective-permute-done.48.refs_1_, bf16[256,1536]{1,0:T(8,128)(2,1)} %collective-permute-done.49.refs_2_, bf16[128,1536]{1,0:T(8,128)(2,1)} %collective-permute-done.50.refs_3_, ...), custom_call_target="tpu_custom_call" | custom-call | flops 2415919104 | bytes 7077888 | tf_op jit(solution)/shard_map/weights_z/pallas_call | solution.py:77
  386.7 5.0 %all-to-all-start.4 = ((bf16[4,64,1536]{2,1,0:T(8,128)(2,1)}), bf16[4,64,1536]{2,1,0:T(8,128)(2,1)}, u32[]{:S(2)}, u32[]{:S(2)}) async-start(bf16[4,64,1536]{2,1,0:T(8,128)(2,1)} %rows_three.1), calls=%async_computation.5 | async-start | bytes 1572864 | tf_op jit(solution)/shard_map/all_to_all | solution.py:1025
  405.0 4.9 %collective-permute-done.56.refs_13_ = bf16[384,256]{1,0:T(8,128)(2,1)} collective-permute-done((bf16[384,256]{1,0:T(8,128)(2,1)S(1)}, bf16[384,256]{1,0:T(8,128)(2,1)}, u32[]{:S(2)}, u32[]{:S(2)}) %collective-permute-start.56) | collective-permute-done | bytes 196640 | tf_op jit(solution)/shard_map/ppermute | solution.py:844
  414.3 9.6 %weights_x.1 = (bf16[1536,1152]{1,0:T(8,128)(2,1)}, f32[128,1152]{1,0:T(8,128)}) custom-call(s32[4]{0:T(128)} %pad_add_fusion.4.index, bf16[256,1536]{1,0:T(8,128)(2,1)} %bitcast.86, bf16[256,1536]{1,0:T(8,128)(2,1)} %collective-permute-done.48.refs_1_, bf16[256,1536]{1,0:T(8,128)(2,1)} %collective-permute-done.49.refs_2_, ...), custom_call_target="tpu_custom_call" | custom-call | flops 3623878656 | bytes 10010624 | tf_op jit(solution)/shard_map/weights_x/pallas_call | solution.py:77
  453.1 6.2 %cores_x.1 = (f32[1536,768]{1,0:T(8,128)}, f32[128,1536]{1,0:T(8,128)}, f32[1536,256]{1,0:T(8,128)}) custom-call(bf16[1536,1152]{1,0:T(8,128)(2,1)} %get-tuple-element.349.a, bf16[1536,1152]{1,0:T(8,128)(2,1)} %collective-permute-done.64.b), custom_call_target="tpu_custom_call" | custom-call | bytes 14155776 | tf_op jit(solution)/shard_map/cores_x/pallas_call | solution.py:77
  (308 shorter events, 228.5 us)
Async XLA Ops:
  48.5 24.5 %collective-permute-start.6 = (bf16[256,1664]{1,0:T(8,128)(2,1)}, bf16[256,1664]{1,0:T(8,128)(2,1)S(1)}, u32[]{:S(2)}, u32[]{:S(2)}) collective-permute-start(bf16[256,1664]{1,0:T(8,128)(2,1)} %bitcast.3.do.refs_6_.refs_12_.refs_10_), channel_id=1, source_target_pairs={{0,16},{4,20},{8,24},{12,28},{16,0},{20,4},{24,8},{28,12},{1,17},{... | collective-permute-start | bytes 2555912 | tf_op jit(solution)/shard_map/ppermute | solution.py:844
  63.7 23.8 %all-to-all-start = ((bf16[4,64,1664]{2,1,0:T(8,128)(2,1)}), bf16[4,64,1664]{2,1,0:T(8,128)(2,1)S(1)}, u32[]{:S(2)}, u32[]{:S(2)}) async-start(bf16[4,64,1664]{2,1,0:T(8,128)(2,1)} %bitcast.67), calls=%async_computation | async-start | bytes 1703936 | tf_op jit(solution)/shard_map/all_to_all | solution.py:1025
  68.6 219.8 %reduce-scatter.2.cloned.1.call-start = ((), (), s32[]{:S(2)}) async-start(), calls=%async_computation.6 | async-start | bytes 7077888 | tf_op jit(solution)/shard_map/reduce_scatter | solution.py:1256
  76.9 33.1 %collective-permute-start.4 = (bf16[256,1664]{1,0:T(8,128)(2,1)}, bf16[256,1664]{1,0:T(8,128)(2,1)}, u32[]{:S(2)}, u32[]{:S(2)}) collective-permute-start(bf16[256,1664]{1,0:T(8,128)(2,1)} %bitcast.3.do.refs_6_.refs_12_.refs_10_), channel_id=1, source_target_pairs={{0,4},{4,0},{8,12},{12,8},{16,20},{20,16},{24,28},{28,24},{1,5},{5... | collective-permute-start | bytes 2555912 | tf_op jit(solution)/shard_map/ppermute | solution.py:844
  76.9 33.1 %collective-permute-start.7 = (bf16[256,1664]{1,0:T(8,128)(2,1)S(1)}, bf16[256,1664]{1,0:T(8,128)(2,1)}, u32[]{:S(2)}, u32[]{:S(2)}) collective-permute-start(bf16[256,1664]{1,0:T(8,128)(2,1)S(1)} %collective-permute-done.5.refs_6_.refs_14_.refs_12_), channel_id=1, source_target_pairs={{0,4},{4,0},{8,12},{12,8},{16,20},{20,16},{24,28},{28,24},{1,5},{5... | collective-permute-start | bytes 2555912 | tf_op jit(solution)/shard_map/ppermute | solution.py:844
  77.4 32.6 %collective-permute-start.8 = (bf16[256,1664]{1,0:T(8,128)(2,1)S(1)}, bf16[256,1664]{1,0:T(8,128)(2,1)}, u32[]{:S(2)}, u32[]{:S(2)}) collective-permute-start(bf16[256,1664]{1,0:T(8,128)(2,1)S(1)} %collective-permute-done.6.refs_7_.refs_15_.refs_13_), channel_id=1, source_target_pairs={{0,4},{4,0},{8,12},{12,8},{16,20},{20,16},{24,28},{28,24},{1,5},{5... | collective-permute-start | bytes 2555912 | tf_op jit(solution)/shard_map/ppermute | solution.py:844
  160.2 27.8 %collective-permute-start.14 = (bf16[256,1664]{1,0:T(8,128)(2,1)S(1)}, bf16[256,1664]{1,0:T(8,128)(2,1)S(1)}, u32[]{:S(2)}, u32[]{:S(2)}) collective-permute-start(bf16[256,1664]{1,0:T(8,128)(2,1)S(1)} %copy-done.40), channel_id=1, source_target_pairs={{0,4},{4,0},{8,12},{12,8},{16,20},{20,16},{24,28},{28,24},{1,5},{5... | collective-permute-start | bytes 2555912 | tf_op jit(solution)/shard_map/ppermute | solution.py:844
  169.1 21.2 %collective-permute-start.26 = (bf16[256,1664]{1,0:T(8,128)(2,1)}, bf16[256,1664]{1,0:T(8,128)(2,1)S(1)}, u32[]{:S(2)}, u32[]{:S(2)}) collective-permute-start(bf16[256,1664]{1,0:T(8,128)(2,1)} %get-tuple-element.241), channel_id=1, source_target_pairs={{0,8},{4,12},{8,0},{12,4},{16,24},{20,28},{24,16},{28,20},{1,9},{5... | collective-permute-start | bytes 2555912 | tf_op jit(solution)/shard_map/ppermute | solution.py:844
  213.3 24.0 %all-to-all-start.1 = ((bf16[4,64,1664]{2,1,0:T(8,128)(2,1)}), bf16[4,64,1664]{2,1,0:T(8,128)(2,1)S(1)}, u32[]{:S(2)}, u32[]{:S(2)}) async-start(bf16[4,64,1664]{2,1,0:T(8,128)(2,1)} %bitcast.21), calls=%async_computation.1 | async-start | bytes 1703936 | tf_op jit(solution)/shard_map/all_to_all | solution.py:1025
  217.0 44.0 %collective-permute-start.30 = (bf16[256,768]{1,0:T(8,128)(2,1)S(1)}, bf16[256,768]{1,0:T(8,128)(2,1)S(1)}, u32[]{:S(2)}, u32[]{:S(2)}) collective-permute-start(bf16[256,768]{1,0:T(8,128)(2,1)S(1)} %bitcast.88), channel_id=1, source_target_pairs={{0,8},{4,12},{8,0},{12,4},{16,24},{20,28},{24,16},{28,20},{1,9},{5... | collective-permute-start | bytes 1179656 | tf_op jit(solution)/shard_map/ppermute | solution.py:844
  217.6 43.4 %collective-permute-start.31 = (bf16[256,768]{1,0:T(8,128)(2,1)S(1)}, bf16[256,768]{1,0:T(8,128)(2,1)S(1)}, u32[]{:S(2)}, u32[]{:S(2)}) collective-permute-start(bf16[256,768]{1,0:T(8,128)(2,1)S(1)} %bitcast.89), channel_id=1, source_target_pairs={{0,16},{4,20},{8,24},{12,28},{16,0},{20,4},{24,8},{28,12},{1,17},{... | collective-permute-start | bytes 1179656 | tf_op jit(solution)/shard_map/ppermute | solution.py:844
  273.9 29.3 %collective-permute-start.35 = (bf16[256,1664]{1,0:T(8,128)(2,1)S(1)}, bf16[256,1664]{1,0:T(8,128)(2,1)S(1)}, u32[]{:S(2)}, u32[]{:S(2)}) collective-permute-start(bf16[256,1664]{1,0:T(8,128)(2,1)S(1)} %copy-done.3), channel_id=1, source_target_pairs={{0,8},{4,12},{8,0},{12,4},{16,24},{20,28},{24,16},{28,20},{1,9},{5... | collective-permute-start | bytes 2555912 | tf_op jit(solution)/shard_map/ppermute | solution.py:844
  274.6 28.6 %collective-permute-start.36 = (bf16[256,1664]{1,0:T(8,128)(2,1)S(1)}, bf16[256,1664]{1,0:T(8,128)(2,1)}, u32[]{:S(2)}, u32[]{:S(2)}) collective-permute-start(bf16[256,1664]{1,0:T(8,128)(2,1)S(1)} %copy-done.3), channel_id=1, source_target_pairs={{0,16},{4,20},{8,24},{12,28},{16,0},{20,4},{24,8},{28,12},{1,17},{... | collective-permute-start | bytes 2555912 | tf_op jit(solution)/shard_map/ppermute | solution.py:844
  288.4 49.0 %all-to-all-start.2 = ((bf16[4,64,1536]{2,1,0:T(8,128)(2,1)}), bf16[4,64,1536]{2,1,0:T(8,128)(2,1)S(1)}, u32[]{:S(2)}, u32[]{:S(2)}) async-start(bf16[4,64,1536]{2,1,0:T(8,128)(2,1)} %bitcast.68), calls=%async_computation.3 | async-start | bytes 1572864 | tf_op jit(solution)/shard_map/all_to_all | solution.py:1025
  293.7 56.6 %collective-permute-start.48 = (bf16[256,1536]{1,0:T(8,128)(2,1)}, bf16[256,1536]{1,0:T(8,128)(2,1)}, u32[]{:S(2)}, u32[]{:S(2)}) collective-permute-start(bf16[256,1536]{1,0:T(8,128)(2,1)} %bitcast.83), channel_id=1, source_target_pairs={{0,8},{4,12},{8,0},{12,4},{16,24},{20,28},{24,16},{28,20},{1,9},{5... | collective-permute-start | bytes 2359304 | tf_op jit(solution)/shard_map/ppermute | solution.py:844
  306.8 23.7 %collective-permute-start.38 = (bf16[256,768]{1,0:T(8,128)(2,1)S(1)}, bf16[256,768]{1,0:T(8,128)(2,1)S(1)}, u32[]{:S(2)}, u32[]{:S(2)}) collective-permute-start(bf16[256,768]{1,0:T(8,128)(2,1)S(1)} %bitcast.71), channel_id=1, source_target_pairs={{0,8},{4,12},{8,0},{12,4},{16,24},{20,28},{24,16},{28,20},{1,9},{5... | collective-permute-start | bytes 1179656 | tf_op jit(solution)/shard_map/ppermute | solution.py:844
  308.1 43.7 %collective-permute-start.49 = (bf16[256,1536]{1,0:T(8,128)(2,1)}, bf16[256,1536]{1,0:T(8,128)(2,1)}, u32[]{:S(2)}, u32[]{:S(2)}) collective-permute-start(bf16[256,1536]{1,0:T(8,128)(2,1)} %bitcast.84), channel_id=1, source_target_pairs={{0,16},{4,20},{8,24},{12,28},{16,0},{20,4},{24,8},{28,12},{1,17},{... | collective-permute-start | bytes 2359304 | tf_op jit(solution)/shard_map/ppermute | solution.py:844
  309.6 27.7 %collective-permute-start.39 = (bf16[256,768]{1,0:T(8,128)(2,1)S(1)}, bf16[256,768]{1,0:T(8,128)(2,1)}, u32[]{:S(2)}, u32[]{:S(2)}) collective-permute-start(bf16[256,768]{1,0:T(8,128)(2,1)S(1)} %bitcast.72), channel_id=1, source_target_pairs={{0,16},{4,20},{8,24},{12,28},{16,0},{20,4},{24,8},{28,12},{1,17},{... | collective-permute-start | bytes 1179656 | tf_op jit(solution)/shard_map/ppermute | solution.py:844
  323.2 37.1 %collective-permute-start.42 = (bf16[128,1664]{1,0:T(8,128)(2,1)S(1)}, bf16[128,1664]{1,0:T(8,128)(2,1)}, u32[]{:S(2)}, u32[]{:S(2)}) collective-permute-start(bf16[128,1664]{1,0:T(8,128)(2,1)S(1)} %slice.81), channel_id=1, source_target_pairs={{0,16},{4,20},{8,24},{12,28},{16,0},{20,4},{24,8},{28,12},{1,17},{... | collective-permute-start | bytes 1277960 | tf_op jit(solution)/shard_map/ppermute | solution.py:844
  330.5 31.8 %collective-permute-start.43 = (bf16[128,1664]{1,0:T(8,128)(2,1)S(1)}, bf16[128,1664]{1,0:T(8,128)(2,1)}, u32[]{:S(2)}, u32[]{:S(2)}) collective-permute-start(bf16[128,1664]{1,0:T(8,128)(2,1)S(1)} %slice.82), channel_id=1, source_target_pairs={{0,8},{4,12},{8,0},{12,4},{16,24},{20,28},{24,16},{28,20},{1,9},{5... | collective-permute-start | bytes 1277960 | tf_op jit(solution)/shard_map/ppermute | solution.py:844
  344.2 39.1 %all-to-all-start.3 = ((bf16[4,64,1536]{2,1,0:T(8,128)(2,1)}), bf16[4,64,1536]{2,1,0:T(8,128)(2,1)S(1)}, u32[]{:S(2)}, u32[]{:S(2)}) async-start(bf16[4,64,1536]{2,1,0:T(8,128)(2,1)} %bitcast.69), calls=%async_computation.4 | async-start | bytes 1572864 | tf_op jit(solution)/shard_map/all_to_all | solution.py:1025
  383.1 52.3 %collective-permute-start.58 = (bf16[1536,768]{1,0:T(8,128)(2,1)}, bf16[1536,768]{1,0:T(8,128)(2,1)S(1)}, u32[]{:S(2)}, u32[]{:S(2)}) collective-permute-start(bf16[1536,768]{1,0:T(8,128)(2,1)} %weights_z.1.a), channel_id=1, source_target_pairs={{0,4},{4,0},{8,12},{12,8},{16,20},{20,16},{24,28},{28,24},{1,5},{5... | collective-permute-start | bytes 7077896 | tf_op jit(solution)/shard_map/ppermute | solution.py:844
  383.3 57.5 %collective-permute-start.59 = (bf16[768,1536]{1,0:T(8,128)(2,1)}, bf16[768,1536]{1,0:T(8,128)(2,1)}, u32[]{:S(2)}, u32[]{:S(2)}) collective-permute-start(bf16[768,1536]{1,0:T(8,128)(2,1)} %out_weights.1.a), channel_id=1, source_target_pairs={{0,4},{4,0},{8,12},{12,8},{16,20},{20,16},{24,28},{28,24},{1,5},{5... | collective-permute-start | bytes 7077896 | tf_op jit(solution)/shard_map/ppermute | solution.py:844
  386.7 58.2 %all-to-all-start.4 = ((bf16[4,64,1536]{2,1,0:T(8,128)(2,1)}), bf16[4,64,1536]{2,1,0:T(8,128)(2,1)}, u32[]{:S(2)}, u32[]{:S(2)}) async-start(bf16[4,64,1536]{2,1,0:T(8,128)(2,1)} %rows_three.1), calls=%async_computation.5 | async-start | bytes 1572864 | tf_op jit(solution)/shard_map/all_to_all | solution.py:1025
  (101 other events, 951.8 us)
Sparse Core Ops, SparseCore 0:
  213.4 60.2 reduce-scatter.1
